TPU v7x, 128 devices: a whole 4x4x4 slice. The times are simulated.
128 devices in a mesh: group: 4 (over y), rank: 32 (over z, x, core).
Axes of the slice: x: 4, y: 4, z: 4, core: 2. Of those that a mesh axis runs over, the one named last changes fastest.
Arguments:
- local_grads: bfloat16 [4, 32, 256, 8192], P('group', 'rank'), may hold values from -1 to 1
- master: float32 [256, 8192], P(('group', 'rank')), may hold values from -3 to 3
- first_moment: float32 [256, 8192], P(('group', 'rank')), may hold values from -3 to 3
- second_moment: float32 [256, 8192], P(('group', 'rank')), may hold values from 0.05 to 2
- new_owner: int32 [64], replicated, may hold values from 0 to 95, as said below
Outputs:
- weights: bfloat16 [256, 8192], replicated
- kept_state: float32 [256, 3, 8192], P(('group', 'rank'))
- adopted_state: float32 [4, 32, 2, 3, 8192], P('group', 'rank')
Inputs may be any that keep to these rules, and one draw needn't show every extreme that they name: new_owner[j] numbers a surviving device as group * 32 + rank. No surviving device adopts more than 2 rows, and in every draw some device adopts exactly 2.
All inputs are finite; a program needn't handle non-finite values.
Results may differ from a plain program's by a relative error of at most 0.003.
Values may be sent and summed in bfloat16 or wider, within the bound.
No kernel may reach another device: no remote copies, remote signals or barrier semaphores. Data moves between devices by JAX's collectives and lax.ppermute only.
A program may use at most 64 MiB of HBM per device.

v0:
```python
import jax
import jax.numpy as jnp
from jax import lax
from jax.sharding import PartitionSpec as P

ADAM_STEP = 20


beta_one = 0.9
beta_two = 0.95
learn_rate = 0.05
epsilon = 1e-08


def broadcast(value, axis, root):
    mine = lax.axis_index(axis) == root
    return lax.psum(jnp.where(mine, value, jnp.zeros_like(value)), axis)


def adam_update(master, first, second, gradient):
    first_new = beta_one * first + (1.0 - beta_one) * gradient
    second_new = beta_two * second + (1.0 - beta_two) * gradient * gradient
    corr_one = 1.0 - beta_one**ADAM_STEP
    corr_two = 1.0 - beta_two**ADAM_STEP
    master_new = master - learn_rate * (first_new / corr_one) / (
        jnp.sqrt(second_new / corr_two) + epsilon
    )
    return (master_new, first_new, second_new)


def adoption_slots(new_owner):
    number = new_owner.shape[0]
    same_owner = new_owner[:, None] == new_owner[None, :]
    earlier = lax.broadcasted_iota(jnp.int32, (number, number), 1) < lax.broadcasted_iota(
        jnp.int32, (number, number), 0
    )
    return jnp.sum((same_owner & earlier).astype(jnp.int32), axis=1)


def hand_over(packet, new_owner, slot_of, self_index):
    group_total = lax.axis_size("group")
    handed = broadcast(packet, "group", group_total - 1)
    capacity = packet.shape[0]
    shard_rows = lax.all_gather(handed, "rank", axis=0, tiled=True)
    row_count = shard_rows.shape[0]
    slot_ids = lax.broadcasted_iota(jnp.int32, (capacity, row_count), 0)
    selector = ((new_owner[None, :] == self_index) & (slot_of[None, :] == slot_ids)).astype(
        jnp.float32
    )
    return jnp.einsum("kt,tfd->kfd", selector, shard_rows, precision=lax.Precision.HIGHEST)


def body(local_grads, master, first_moment, second_moment, new_owner):
    group_total = lax.axis_size("group")
    rank_total = lax.axis_size("rank")
    group_idx = lax.axis_index("group")
    rank_idx = lax.axis_index("rank")
    row_length = master.shape[1]
    own_grads = local_grads.reshape(local_grads.shape[2], row_length)
    gradient = lax.psum_scatter(
        own_grads.astype(jnp.float32), ("group", "rank"), scatter_dimension=0, tiled=True
    )
    self_index = group_idx * rank_total + rank_idx
    leaving = group_idx == group_total - 1
    slot_of = adoption_slots(new_owner)
    before = jnp.stack([master, first_moment, second_moment, gradient], axis=1)
    received = hand_over(before, new_owner, slot_of, self_index)
    master_new, first_new, second_new = adam_update(master, first_moment, second_moment, gradient)
    adopt_master, adopt_first, adopt_second = adam_update(
        received[:, 0], received[:, 1], received[:, 2], received[:, 3]
    )
    adopted = jnp.stack([adopt_master, adopt_first, adopt_second], axis=1)
    weights = lax.all_gather(master_new.astype(jnp.bfloat16), ("group", "rank"), axis=0, tiled=True)
    packet = jnp.stack([master_new, first_new, second_new], axis=1)
    kept_packet = jnp.where(leaving, jnp.zeros_like(packet), packet)
    return (weights, kept_packet, adopted[None, None])


def solution(mesh):
    in_specs = (
        P("group", "rank", None, None),
        P(("group", "rank"), None),
        P(("group", "rank"), None),
        P(("group", "rank"), None),
        P(),
    )
    out_specs = (P(), P(("group", "rank"), None, None), P("group", "rank", None, None, None))
    return jax.shard_map(body, mesh=mesh, in_specs=in_specs, out_specs=out_specs, check_vma=False)
```

profile of v0, /device:TPU:1, one launch (start us, length us, event | category | flops | bytes accessed | tf_op | source)
XLA Modules:
  0.0 363.9 jit_solution(8938542046865273758)
XLA Ops:
  7.2 0.0 copy-start
  7.2 0.0 all-reduce.6.cloned.1.call-start
  7.2 6.4 %bitcast_convert_fusion = f32[256,8192]{1,0:T(8,128)} fusion(bf16[1,1,256,8192]{3,2,1,0:T(8,128)(2,1)} %param.5), kind=kLoop, calls=%fused_computation.2 | loop fusion | flops 2097152 | bytes 12582912 | tf_op jit(solution)/shard_map/convert_element_type | solution.py:61
  13.7 0.0 all-reduce.6.cloned.1.call-update
  13.7 0.0 all-reduce.4.cloned.1.call-start
  13.8 165.0 %all-reduce.6.cloned.1.call-done = f32[256,8192]{1,0:T(8,128)} async-done(((f32[256,8192]{1,0:T(8,128)}), f32[256,8192]{1,0:T(8,128)}) %all-reduce.6.cloned.1.call-update) | async-done | bytes 8388624
  178.8 0.0 copy-done.1
  178.8 1.8 convert_bitcast_fusion
  180.6 0.8 maximum_select_fusion
  181.4 0.0 all-reduce.4.cloned.1.call-update
  181.4 0.0 all-gather.6.cloned.1.call-start
  181.5 0.7 all-gather.6.cloned.1.call-update
  182.2 0.0 all-gather.4.cloned.1.call-start
  182.2 37.5 %all-reduce.4.cloned.1.call-done = f32[2,4,8192]{2,0,1:T(2,128)} async-done(((f32[2,4,8192]{2,0,1:T(2,128)}), f32[2,4,8192]{2,0,1:T(2,128)}) %all-reduce.4.cloned.1.call-update) | async-done | bytes 262160 | tf_op jit(solution)/shard_map/psum | solution.py:17
  219.7 1.8 copy.10
  221.5 0.0 all-gather.4.cloned.1.call-update
  221.6 0.2 convert_reduce_fusion
  221.8 0.8 maximum_select_fusion.1
  222.6 70.8 %all-gather.6.cloned.1.call-done = bf16[128,2,8192]{2,1,0:T(2,128)(2,1)} async-done(((bf16[1,2,8192]{2,1,0:T(2,128)(2,1)}), bf16[128,2,8192]{2,1,0:T(2,128)(2,1)}) %all-gather.6.cloned.1.call-update) | async-done | bytes 4194320 | tf_op jit(solution)/shard_map/all_gather | solution.py:73
  293.4 7.2 %reshape.16 = bf16[256,8192]{1,0:T(8,128)(2,1)} reshape(bf16[128,2,8192]{2,1,0:T(2,128)(2,1)} %all-gather.6.cloned.1.call-done) | data formatting | bytes 8388608
  300.5 45.5 %all-gather.4.cloned.1.call-done = f32[64,4,8192]{2,1,0:T(4,128)} async-done(((f32[2,4,8192]{2,1,0:T(4,128)}), f32[64,4,8192]{2,1,0:T(4,128)}) %all-gather.4.cloned.1.call-update) | async-done | bytes 8388624 | tf_op jit(solution)/shard_map/all_gather | solution.py:44
  346.0 10.4 %fusion = f32[2,4,8192]{2,0,1:T(2,128)S(1)} fusion(f32[64,4,8192]{2,1,0:T(4,128)} %all-gather.4.cloned.1.call-done, pred[64]{0:T(512)(128)(4,1)S(1)} %broadcast_compare_fusion, s32[64]{0:T(128)S(1)} %convert_reduce_fusion), kind=kOutput, calls=%fused_computation | convolution fusion | flops 50331904 | bytes 8651072 | tf_op jit(solution)/shard_map/kt,tfd->kfd/dot_general | solution.py:50
  356.4 0.2 slice_subtract_fusion
  356.6 0.8 maximum_bitcast_fusion
  (7 shorter events, 0.0 us)
Async XLA Ops:
  7.2 171.6 %copy-start = (f32[2,8192]{1,0:T(2,128)S(1)}, f32[2,8192]{1,0:T(2,128)}, u32[]{:S(2)}) copy-start(f32[2,8192]{1,0:T(2,128)} %param.6) | copy-start | bytes 196612
  7.2 171.6 %copy-start.2 = (f32[2,8192]{1,0:T(2,128)S(1)}, f32[2,8192]{1,0:T(2,128)}, u32[]{:S(2)}) copy-start(f32[2,8192]{1,0:T(2,128)} %param.7) | copy-start | bytes 196612
  7.2 171.6 %copy-start.1 = (f32[2,8192]{1,0:T(2,128)S(1)}, f32[2,8192]{1,0:T(2,128)}, u32[]{:S(2)}) copy-start(f32[2,8192]{1,0:T(2,128)} %param.8) | copy-start | bytes 196612
  7.2 171.6 %all-reduce.6.cloned.1.call-start = ((), (), s32[]{:S(2)}) async-start(), calls=%async_computation.3 | async-start | bytes 16777216
  13.7 207.9 %copy-start.3 = (s32[64]{0:T(128)S(1)}, s32[64]{0:T(128)}, u32[]{:S(2)}) copy-start(s32[64]{0:T(128)} %param.9) | copy-start | bytes 772
  13.7 206.0 %all-reduce.4.cloned.1.call-start = ((), (), s32[]{:S(2)}) async-start(), calls=%async_computation | async-start | bytes 524288 | tf_op jit(solution)/shard_map/psum | solution.py:17
  181.4 111.9 %all-gather.6.cloned.1.call-start = ((), (), s32[]{:S(2)}) async-start(), calls=%async_computation.2 | async-start | bytes 4227072 | tf_op jit(solution)/shard_map/all_gather | solution.py:73
  182.2 163.9 %all-gather.4.cloned.1.call-start = ((), (), s32[]{:S(2)}) async-start(), calls=%async_computation.1 | async-start | bytes 8650752 | tf_op jit(solution)/shard_map/all_gather | solution.py:44
Sparse Core Ops, SparseCore 0:
  13.8 164.8 all-reduce.5
  181.8 37.8 all-reduce.3
  223.4 69.8 all-gather.5
  295.5 50.5 all-gather.3
where the time goes:
time: 364 us
  waiting for transfers between devices  320 us (88%)
  between operations  13.8 us (4%)
  other arithmetic  11 us (3%)
  matrix products  10.4 us (3%)
  local copies, waits for them, and re-layouts  9 us (2%)
    unnamed x5, waiting for transfers between devices  166 us
    all_gather x1, waiting for transfers between devices, body(): lax.all_gather(master_new.astype(jnp.bfloat16), ('group', 'rank'), axis=0...  70.8 us
    all_gather x1, waiting for transfers between devices, hand_over(): shard_rows = lax.all_gather(handed, 'rank', axis=0, tiled=True)  45.5 us
    psum x1, waiting for transfers between devices, broadcast(): return lax.psum(jnp.where(mine, value, jnp.zeros_like(value)), axis)  37.5 us
    dot_general x1, matrix products, hand_over(): jnp.einsum('kt,tfd->kfd', selector, shard_rows, precision=lax.Precision.H...  10.4 us
  transfers between devices with their start and end apart: 4, of which 4 were waited for; matrix products, arithmetic and copies ran while one was open for 3% of the time, Pallas kernels for 0%

commit v1 on v0

v1 whole, which is shorter than its diff:
```python
import functools

import jax
import jax.numpy as jnp
from jax import lax
from jax.experimental import pallas as pl
from jax.experimental.pallas import tpu as pltpu
from jax.sharding import Mesh
from jax.sharding import PartitionSpec as P

ADAM_STEP = 20

beta_one = 0.9
beta_two = 0.95
learn_rate = 0.05
epsilon = 1e-08

CHIPS = ("y", "z", "x")
BF = jnp.bfloat16
F32 = jnp.float32


def adam_update(master, first, second, gradient):
    first_new = beta_one * first + (1.0 - beta_one) * gradient
    second_new = beta_two * second + (1.0 - beta_two) * gradient * gradient
    corr_one = 1.0 - beta_one**ADAM_STEP
    corr_two = 1.0 - beta_two**ADAM_STEP
    master_new = master - learn_rate * (first_new / corr_one) / (
        jnp.sqrt(second_new / corr_two) + epsilon
    )
    return (master_new, first_new, second_new)


def iota(shape, dim):
    return lax.broadcasted_iota(jnp.int32, shape, dim)


def one_hot(target, columns):
    return jnp.where(iota(target.shape, 1) == target, 1.0, 0.0).astype(BF)


def pick(matrix, values):
    return jnp.dot(matrix, values, preferred_element_type=F32)


def kept_blocks(rows, core):
    stacked = jnp.concatenate([rows[:, k * 1024 : (k + 1) * 1024] for k in range(8)], axis=0)
    p = iota((128, 256), 0)
    target = ((p >> 1) & 7) * 32 + (p >> 4) * 4 + 2 * core + (p & 1)
    return pick(one_hot(target, 256), stacked)


def leaving_rows(rows):
    n = iota((64, 64), 0)
    return pick(one_hot(2 * (n & 31) + (n >> 5), 64), rows)


def send_kernel(kept_ref, leave_ref, master_ref, first_ref, second_ref, out_ref, state_ref, rows_ref):
    step = pl.program_id(0)
    core = 1 - lax.axis_index("core")

    @pl.when(step == 0)
    def _():
        rows_ref[...] = jnp.zeros_like(rows_ref)
        rows_ref[0:2, :] = master_ref[...]
        rows_ref[2:4, :] = first_ref[...]
        rows_ref[4:6, :] = second_ref[...]
        for t in range(32):
            for h in range(2):
                state_ref[t, 8 * h : 8 * h + 8, :] = rows_ref[:, t * 256 + h * 128 : t * 256 + (h + 1) * 128]

    @pl.when(step < 6)
    def _():
        blocks = kept_blocks(kept_ref[...], core).astype(BF)
        out_ref[...] = blocks.reshape(8, 16, 1024)

    @pl.when(step >= 6)
    def _():
        rows = leaving_rows(leave_ref[...])
        for q in range(8):
            mine = jnp.where(
                core == 0, rows[:, q * 512 : q * 512 + 256], rows[:, q * 512 + 256 : q * 512 + 512]
            ).astype(BF)
            for a in range(4):
                out_ref[q, :, a * 256 : (a + 1) * 256] = mine[16 * a : 16 * a + 16, :]


def add_kernel(kept_ref, leave_ref, got_ref, out_ref):
    step = pl.program_id(0)
    core = lax.axis_index("core")

    @pl.when(step < 6)
    def _():
        got = got_ref[...].reshape(128, 1024).astype(F32)
        out_ref[...] = (kept_blocks(kept_ref[...], core) + got).astype(BF).reshape(8, 16, 1024)

    @pl.when(step >= 6)
    def _():
        rows = leaving_rows(leave_ref[...])
        for q in range(8):
            mine = jnp.where(
                core == 0, rows[:, q * 512 : q * 512 + 256], rows[:, q * 512 + 256 : q * 512 + 512]
            )
            for a in range(4):
                cut = slice(a * 256, (a + 1) * 256)
                got = got_ref[q, :, cut].astype(F32)
                out_ref[q, :, cut] = (mine[16 * a : 16 * a + 16, :] + got).astype(BF)


def adam_kernel(parts_ref, master_ref, first_ref, second_ref, state_ref, key_ref, kept_ref, out_ref, old_ref):
    leaving = lax.axis_index("y") == 3

    def add(d, total):
        return total + parts_ref[d].astype(F32)

    gradient = lax.fori_loop(1, 64, add, parts_ref[0].astype(F32), unroll=7)

    @pl.when(leaving)
    def _():
        for i in range(3):
            for a in range(4):
                for h in range(2):
                    start = 256 * (a % 2) + 8 * h + 2 * i + a // 2
                    at = a * 256 + h * 128
                    old_ref[i, :, at : at + 128] = state_ref[pl.ds(start, 16, stride=16), :]

    @pl.when(jnp.logical_not(leaving))
    def _():
        for i, ref in enumerate((master_ref, first_ref, second_ref)):
            for k in range(8):
                old_ref[i, 2 * k : 2 * k + 2, :] = ref[:, k * 1024 : (k + 1) * 1024]

    new = adam_update(old_ref[0], old_ref[1], old_ref[2], gradient)
    for i in range(3):
        value = jnp.where(leaving, jnp.zeros_like(new[i]), new[i])
        for k in range(8):
            for r in range(2):
                kept_ref[r, i : i + 1, k * 1024 : (k + 1) * 1024] = value[2 * k + r : 2 * k + r + 1, :]

    weights = new[0].astype(BF)

    def spread(d, carry):
        out_ref[d, :, 0:1024] = weights
        return carry

    lax.fori_loop(0, 64, spread, 0, unroll=8)

    moments = jnp.concatenate(
        [
            new[1 + part // 2][:, a * 256 + (part % 2) * 128 : a * 256 + (part % 2) * 128 + 128]
            for part in range(4)
            for a in range(4)
        ],
        axis=0,
    ).astype(BF)
    p = iota((1024, 256), 0)
    wanted = (p >> 4) * 4 + (p & 3) + 512 * ((p >> 2) & 3)
    chosen = jnp.where(key_ref[0:1, :] == wanted, 1.0, 0.0).astype(BF)
    out_ref[:, :, 1024:1152] = pick(chosen, moments).astype(BF).reshape(64, 16, 128)


def place_kernel(
    own_ref, other_ref, own_left_ref, other_left_ref, key_ref, weights_ref, adopted_ref, rows_ref, state_ref
):
    step = pl.program_id(0)
    core = lax.axis_index("core")
    chip = (lax.axis_index("y") * 4 + lax.axis_index("z")) * 4 + lax.axis_index("x")

    @pl.when(step < 6)
    def _():
        stacked = jnp.concatenate(
            [own_ref[:, :, 0:1024].reshape(128, 1024), other_ref[:, :, 0:1024].reshape(128, 1024)], axis=0
        )
        p = iota((256, 256), 0)
        row = p & 31
        half = jnp.where(((row >> 1) & 1) == core, 0, 128)
        target = half + (row >> 2) * 16 + (p >> 5) * 2 + (row & 1)
        rows = pick(one_hot(target, 256), stacked).astype(BF)
        for k in range(8):
            weights_ref[:, k * 1024 : (k + 1) * 1024] = rows[32 * k : 32 * k + 32, :]

    for h in range(2):

        @pl.when(step == 6 + h)
        def _():
            for q in range(16):
                for ref, side in ((own_left_ref, core), (other_left_ref, 1 - core)):
                    at = pl.ds(pl.multiple_of((2 * q + side) * 256, 256), 256)
                    for r in range(2):
                        a = 2 * r + h
                        rows_ref[16 * r : 16 * r + 16, at] = ref[q, :, a * 256 : (a + 1) * 256]
            rows = rows_ref[...]
            n = iota((32, 32), 0)
            weights_ref[...] = pick(one_hot((n & 1) * 16 + (n >> 1), 32), rows).astype(BF)
            k = iota((8, 32), 0)
            wanted = jnp.where(k < 2, chip * 4 + core * 2 + k, -1)
            chosen = jnp.where(key_ref[1 + h : 2 + h, 0:32] == wanted, 1.0, 0.0).astype(BF)
            masters = pick(chosen, rows)
            if h == 0:
                state_ref[...] = masters
                for ref, side in ((own_left_ref, core), (other_left_ref, 1 - core)):
                    moments = jnp.concatenate([ref[q, :, 1024:1152] for q in range(16)], axis=1)
                    for low in range(2):
                        k = iota((8, 16), 0)
                        target = jnp.where(
                            (k >= 2) & (k < 6), (((k >> 1) - 1) * 2 + low) * 4 + core * 2 + (k & 1), -1
                        )
                        found = pick(one_hot(target, 16), moments)
                        for q in range(16):
                            at = pl.ds(pl.multiple_of((2 * q + side) * 256 + low * 128, 128), 128)
                            state_ref[:, at] += found[:, q * 128 : (q + 1) * 128]
            else:
                state_ref[...] += masters
                for i in range(3):
                    for slot in range(2):
                        adopted_ref[slot, i : i + 1, :] = state_ref[2 * i + slot : 2 * i + slot + 1, :]


def adoption_keys(new_owner):
    number = new_owner.shape[0]
    same_owner = new_owner[:, None] == new_owner[None, :]
    earlier = iota((number, number), 1) < iota((number, number), 0)
    slot = jnp.sum((same_owner & earlier).astype(jnp.int32), axis=1)
    key = (new_owner * 2 + slot).reshape(32, 2).T
    halves = key.reshape(2, 2, 16).transpose(1, 0, 2).reshape(2, 32)
    quarters = (key.reshape(1, 64) + 512 * jnp.arange(4, dtype=jnp.int32)[:, None]).reshape(1, 256)
    return jnp.concatenate([quarters, jnp.pad(halves, ((0, 5), (0, 224)), constant_values=-1)], axis=0)


def params():
    return pltpu.CompilerParams(vmem_limit_bytes=48 * 1024 * 1024)


def body(local_grads, master, first, second, new_owner):
    grads = local_grads.reshape(256, 8192)
    keys = adoption_keys(new_owner)
    kept_spec = pl.BlockSpec((32, 8192), lambda i: (jnp.minimum(i, 5), 0))
    leave_spec = pl.BlockSpec((64, 4096), lambda i: (3, jnp.maximum(i - 6, 0)))
    block_spec = pl.BlockSpec((8, 16, 1024), lambda i: (i, 0, 0))
    state_spec = pl.BlockSpec((2, 8192), lambda i: (0, 0))
    blocks = jax.ShapeDtypeStruct((64, 16, 1024), BF)
    to_send, state = pl.pallas_call(
        send_kernel,
        grid=(8,),
        in_specs=[kept_spec, leave_spec, state_spec, state_spec, state_spec],
        out_specs=[block_spec, pl.BlockSpec((32, 16, 128), lambda i: (0, 0, 0))],
        out_shape=[blocks, jax.ShapeDtypeStruct((32, 16, 128), F32)],
        scratch_shapes=[pltpu.VMEM((8, 8192), F32)],
        compiler_params=params(),
        name="send_blocks",
    )(grads, grads, master, first, second)
    swap = [(0, 1), (1, 0)]
    got = lax.ppermute(to_send, "core", swap)
    state = lax.all_to_all(state, ("z", "x", "core"), 0, 0, tiled=True)
    partial = pl.pallas_call(
        add_kernel,
        grid=(8,),
        in_specs=[kept_spec, leave_spec, block_spec],
        out_specs=block_spec,
        out_shape=blocks,
        compiler_params=params(),
        name="add_blocks",
    )(grads, grads, got)
    partial = lax.all_to_all(partial, CHIPS, 0, 0, tiled=True)
    kept, payload = pl.pallas_call(
        adam_kernel,
        out_shape=[
            jax.ShapeDtypeStruct((2, 3, 8192), F32),
            jax.ShapeDtypeStruct((64, 16, 1152), BF),
        ],
        scratch_shapes=[pltpu.VMEM((3, 16, 1024), F32)],
        compiler_params=params(),
        name="adam",
    )(partial, master, first, second, state.reshape(512, 128), keys)
    own = lax.all_to_all(payload, CHIPS, 0, 0, tiled=True)
    other = lax.ppermute(own, "core", swap)
    group_spec = pl.BlockSpec((8, 16, 1152), lambda i: (jnp.minimum(i, 5), 0, 0))
    left_spec = pl.BlockSpec((16, 16, 1152), lambda i: (3, 0, 0))
    weights, adopted = pl.pallas_call(
        place_kernel,
        grid=(8,),
        in_specs=[group_spec, group_spec, left_spec, left_spec, pl.BlockSpec((8, 256), lambda i: (0, 0))],
        out_specs=[
            pl.BlockSpec((32, 8192), lambda i: (i, 0)),
            pl.BlockSpec((2, 3, 8192), lambda i: (0, 0, 0)),
        ],
        out_shape=[
            jax.ShapeDtypeStruct((256, 8192), BF),
            jax.ShapeDtypeStruct((2, 3, 8192), F32),
        ],
        scratch_shapes=[pltpu.VMEM((32, 8192), BF), pltpu.VMEM((8, 8192), F32)],
        compiler_params=params(),
        name="place",
    )(own, other, own, other, keys)
    return (weights, kept, adopted[None, None])


def solution(mesh):
    fine = Mesh(mesh.devices.reshape(4, 4, 4, 2), ("y", "z", "x", "core"))
    every = ("y", "z", "x", "core")
    in_specs = (P("y", ("z", "x", "core"), None, None), P(every, None), P(every, None), P(every, None), P())
    out_specs = (P(), P(every, None, None), P("y", ("z", "x", "core"), None, None, None))
    return jax.shard_map(body, mesh=fine, in_specs=in_specs, out_specs=out_specs, check_vma=False)
```

time: 364 us -> 118 us (0.32)
  waiting for transfers between devices: 320 us -> 33.3 us
  blocking collectives: 0 us -> 37.7 us
  starting transfers between devices: 0.16 us -> 20.2 us
  Pallas kernels: 0 us -> 19.1 us
  between operations: 13.8 us -> 0.73 us
  other arithmetic: 11 us -> 0.27 us
  matrix products: 10.4 us -> 0 us
    unnamed x5 -> x0, waiting for transfers between devices: 166 us -> none
    all_gather x2 -> x0, waiting for transfers between devices: 116 us -> none  [the longest x1 70.8 us: body(): lax.all_gather(master_new.astype(jnp.bfloat16), ('group', 'rank'), axis=0...]
    all_to_all x0 -> x1, blocking collectives: none -> 37.7 us  [body(): own = lax.all_to_all(payload, CHIPS, 0, 0, tiled=True)]
    psum x1 -> x0, waiting for transfers between devices: 37.5 us -> none  [broadcast(): return lax.psum(jnp.where(mine, value, jnp.zeros_like(value)), axis)]
    all_to_all x0 -> x2, waiting for transfers between devices: none -> 30 us  [the longest x1 28.2 us: body(): partial = lax.all_to_all(partial, CHIPS, 0, 0, tiled=True)]
    pallas_call x0 -> x4, Pallas kernels: none -> 19.1 us  [the longest x1 7.2 us: body(): pl.pallas_call(send_kernel, grid=(8,), in_specs=[kept_spec, leave_spec, s...]
    all_to_all x0 -> x2, starting transfers between devices: none -> 16.7 us  [the longest x1 8.59 us: body(): partial = lax.all_to_all(partial, CHIPS, 0, 0, tiled=True)]
    dot_general x1 -> x0, matrix products: 10.4 us -> none  [hand_over(): jnp.einsum('kt,tfd->kfd', selector, shard_rows, precision=lax.Precision.H...]
  transfers between devices with their start and end apart: 4 -> 4, of which waited for: 4 -> 3; matrix products, arithmetic and copies ran while one was open for 3% -> 1% of each run, Pallas kernels for 0% -> 5%
where the time goes in v1:
time: 118 us; the launch traced here: 117 us
  blocking collectives  37.7 us (32%)
  waiting for transfers between devices  33.3 us (28%)
  starting transfers between devices  20.2 us (17%)
  Pallas kernels  19.1 us (16%)
  local copies, waits for them, and re-layouts  6.02 us (5%)
    all_to_all x1, blocking collectives, body(): own = lax.all_to_all(payload, CHIPS, 0, 0, tiled=True)  37.7 us
    all_to_all x1, waiting for transfers between devices, body(): partial = lax.all_to_all(partial, CHIPS, 0, 0, tiled=True)  28.2 us
    all_to_all x1, starting transfers between devices, body(): partial = lax.all_to_all(partial, CHIPS, 0, 0, tiled=True)  8.59 us
    all_to_all x1, starting transfers between devices, body(): state = lax.all_to_all(state, ('z', 'x', 'core'), 0, 0, tiled=True)  8.12 us
    pallas_call x1, Pallas kernels, body(): pl.pallas_call(send_kernel, grid=(8,), in_specs=[kept_spec, leave_spec, s...  7.2 us
    pallas_call x1, Pallas kernels, body(): pl.pallas_call(add_kernel, grid=(8,), in_specs=[kept_spec, leave_spec, bl...  5.75 us
    unnamed x18, local copies, waits for them, and re-layouts  5.5 us
    pallas_call x1, Pallas kernels, body(): pl.pallas_call(place_kernel, grid=(8,), in_specs=[group_spec, group_spec,...  5.18 us
  transfers between devices with their start and end apart: 4, of which 3 were waited for; matrix products, arithmetic and copies ran while one was open for 1% of the time, Pallas kernels for 5%

profile of v1, /device:TPU:1, one launch (start us, length us, event | category | flops | bytes accessed | tf_op | source)
XLA Modules:
  0.0 117.3 jit_solution(11236224974745126465)
XLA Ops:
  0.6 0.8 copy-done.1
  1.5 0.8 copy-done.3
  2.3 0.8 copy-done.5
  3.2 7.2 %send_blocks.1 = (bf16[64,16,1024]{2,1,0:T(8,128)(2,1)}, f32[32,16,128]{2,1,0:T(8,128)}) custom-call(bf16[256,8192]{1,0:T(8,128)(2,1)} %bitcast.7, bf16[256,8192]{1,0:T(8,128)(2,1)} %bitcast.8, f32[2,8192]{1,0:T(2,128)S(1)} %copy-done.1, f32[2,8192]{1,0:T(2,128)S(1)} %copy-done.3, f32[2,8192]{1,0:T(2,128)S(1)} %copy-done.5), custom_call_target="tpu_custom_call" | custom-call | tf_op jit(solution)/shard_map/send_blocks/pallas_call | solution.py:242
  10.4 1.4 %collective-permute-start = (bf16[64,16,1024]{2,1,0:T(8,128)(2,1)}, bf16[64,16,1024]{2,1,0:T(8,128)(2,1)S(1)}, u32[]{:S(2)}, u32[]{:S(2)}) collective-permute-start(bf16[64,16,1024]{2,1,0:T(8,128)(2,1)} %get-tuple-element.9), channel_id=1, source_target_pairs={{0,1},{1,0},{2,3},{3,2},{4,5},{5,4},{6,7},{7,6},{8,9},{9,8},{10,11... | collective-permute-start | bytes 6291464 | tf_op jit(solution)/shard_map/ppermute | solution.py:253
  11.8 8.1 %all-to-all-start.1 = ((f32[32,16,128]{2,1,0:T(8,128)}), f32[32,16,128]{2,1,0:T(8,128)S(1)}, u32[]{:S(2)}, u32[]{:S(2)}) async-start(f32[32,16,128]{2,1,0:T(8,128)} %get-tuple-element.10), calls=%async_computation.1 | async-start | bytes 524288 | tf_op jit(solution)/shard_map/all_to_all | solution.py:254
  19.9 5.7 %add_blocks.1 = bf16[64,16,1024]{2,1,0:T(8,128)(2,1)S(1)} custom-call(bf16[256,8192]{1,0:T(8,128)(2,1)} %bitcast.9, bf16[256,8192]{1,0:T(8,128)(2,1)} %bitcast.10, bf16[64,16,1024]{2,1,0:T(8,128)(2,1)S(1)} %collective-permute-done.got_ref), custom_call_target="tpu_custom_call" | custom-call | tf_op jit(solution)/shard_map/add_blocks/pallas_call | solution.py:255
  25.7 1.3 %copy-done = bf16[64,16,1024]{2,1,0:T(8,128)(2,1)} copy-done((bf16[64,16,1024]{2,1,0:T(8,128)(2,1)}, bf16[64,16,1024]{2,1,0:T(8,128)(2,1)S(1)}, u32[]{:S(2)}) %copy-start) | copy-done | bytes 2097176
  27.0 1.8 %all-to-all-done.1 = f32[32,16,128]{2,1,0:T(8,128)S(1)} async-done(((f32[32,16,128]{2,1,0:T(8,128)}), f32[32,16,128]{2,1,0:T(8,128)S(1)}, u32[]{:S(2)}, u32[]{:S(2)}) %all-to-all-start.1) | async-done | bytes 262176 | tf_op jit(solution)/shard_map/all_to_all | solution.py:254
  28.8 8.6 %all-to-all-start = ((bf16[64,16,1024]{2,1,0:T(8,128)(2,1)}), bf16[64,16,1024]{2,1,0:T(8,128)(2,1)S(1)}, u32[]{:S(2)}, u32[]{:S(2)}) async-start(bf16[64,16,1024]{2,1,0:T(8,128)(2,1)} %copy-done), calls=%async_computation | async-start | bytes 4194304 | tf_op jit(solution)/shard_map/all_to_all | solution.py:264
  37.4 0.2 convert_reduce_fusion
  37.6 0.1 reshape.55
  37.8 0.1 add.31
  37.9 0.1 reshape.56
  38.0 0.1 reshape.57
  38.1 0.1 add.35
  38.2 28.2 %all-to-all-done.parts_ref = bf16[64,16,1024]{2,1,0:T(8,128)(2,1)S(1)} async-done(((bf16[64,16,1024]{2,1,0:T(8,128)(2,1)}), bf16[64,16,1024]{2,1,0:T(8,128)(2,1)S(1)}, u32[]{:S(2)}, u32[]{:S(2)}) %all-to-all-start) | async-done | bytes 2097184 | tf_op jit(solution)/shard_map/all_to_all | solution.py:264
  66.4 1.0 adam.1
  67.4 37.7 %all_to_all.15.own_ref.own_left_ref = bf16[64,16,1152]{2,1,0:T(8,128)(2,1)S(1)} all-to-all(bf16[64,16,1152]{2,1,0:T(8,128)(2,1)S(1)} %get-tuple-element.11), channel_id=1, replica_groups=mesh['y'=4,'z'=4,'x'=4,'core'=2] {'y','z','x'}, dimensions={0} | all-to-all | bytes 4718592 | tf_op jit(solution)/shard_map/all_to_all | solution.py:275
  105.1 2.0 %collective-permute-start.1 = (bf16[64,16,1152]{2,1,0:T(8,128)(2,1)S(1)}, bf16[64,16,1152]{2,1,0:T(8,128)(2,1)S(1)}, u32[]{:S(2)}, u32[]{:S(2)}) collective-permute-start(bf16[64,16,1152]{2,1,0:T(8,128)(2,1)S(1)} %all_to_all.15.own_ref.own_left_ref), channel_id=1, source_target_pairs={{0,1},{1,0},{2,3},{3,2},{4,5},{5,4},{6,7},{7,6},{8,9},{9,8},{10,11... | collective-permute-start | bytes 7077896 | tf_op jit(solution)/shard_map/ppermute | solution.py:276
  107.1 0.8 copy.21
  107.9 3.3 %collective-permute-done.1.other_ref.other_left_ref = bf16[64,16,1152]{2,1,0:T(8,128)(2,1)S(1)} collective-permute-done((bf16[64,16,1152]{2,1,0:T(8,128)(2,1)S(1)}, bf16[64,16,1152]{2,1,0:T(8,128)(2,1)S(1)}, u32[]{:S(2)}, u32[]{:S(2)}) %collective-permute-start.1) | collective-permute-done | bytes 2359328 | tf_op jit(solution)/shard_map/ppermute | solution.py:276
  111.3 5.2 %place.1 = (bf16[256,8192]{1,0:T(8,128)(2,1)}, f32[2,3,8192]{2,1,0:T(4,128)S(1)}) custom-call(bf16[64,16,1152]{2,1,0:T(8,128)(2,1)S(1)} %all_to_all.15.own_ref.own_left_ref, bf16[64,16,1152]{2,1,0:T(8,128)(2,1)S(1)} %collective-permute-done.1.other_ref.other_left_ref, bf16[64,16,1152]{2,1,0:T(8,128)(2,1)S(1)} %all_to_all.15.own_ref.own_left_ref, ...), custom_call_target="tpu_custom_call" | custom-call | tf_op jit(solution)/shard_map/place/pallas_call | solution.py:279
  116.4 0.8 copy.22
  (19 shorter events, 0.2 us)
Async XLA Ops:
  0.6 0.8 copy-start.1
  1.5 0.8 copy-start.3
  2.3 0.8 copy-start.5
  10.4 9.6 %collective-permute-start = (bf16[64,16,1024]{2,1,0:T(8,128)(2,1)}, bf16[64,16,1024]{2,1,0:T(8,128)(2,1)S(1)}, u32[]{:S(2)}, u32[]{:S(2)}) collective-permute-start(bf16[64,16,1024]{2,1,0:T(8,128)(2,1)} %get-tuple-element.9), channel_id=1, source_target_pairs={{0,1},{1,0},{2,3},{3,2},{4,5},{5,4},{6,7},{7,6},{8,9},{9,8},{10,11... | collective-permute-start | bytes 6291464 | tf_op jit(solution)/shard_map/ppermute | solution.py:253
  11.8 17.0 %all-to-all-start.1 = ((f32[32,16,128]{2,1,0:T(8,128)}), f32[32,16,128]{2,1,0:T(8,128)S(1)}, u32[]{:S(2)}, u32[]{:S(2)}) async-start(f32[32,16,128]{2,1,0:T(8,128)} %get-tuple-element.10), calls=%async_computation.1 | async-start | bytes 524288 | tf_op jit(solution)/shard_map/all_to_all | solution.py:254
  25.7 1.3 %copy-start = (bf16[64,16,1024]{2,1,0:T(8,128)(2,1)}, bf16[64,16,1024]{2,1,0:T(8,128)(2,1)S(1)}, u32[]{:S(2)}) copy-start(bf16[64,16,1024]{2,1,0:T(8,128)(2,1)S(1)} %add_blocks.1) | copy-start | bytes 6291460
  27.0 10.4 %copy-start.7 = (s32[64]{0:T(128)S(1)}, s32[64]{0:T(128)}, u32[]{:S(2)}) copy-start(s32[64]{0:T(128)} %param.9) | copy-start | bytes 772
  27.0 39.4 %copy-start.2 = (f32[2,8192]{1,0:T(2,128)S(1)}, f32[2,8192]{1,0:T(2,128)}, u32[]{:S(2)}) copy-start(f32[2,8192]{1,0:T(2,128)} %master_ref.3) | copy-start | bytes 196612
  27.0 39.4 %copy-start.4 = (f32[2,8192]{1,0:T(2,128)S(1)}, f32[2,8192]{1,0:T(2,128)}, u32[]{:S(2)}) copy-start(f32[2,8192]{1,0:T(2,128)} %first_ref.3) | copy-start | bytes 196612
  27.0 39.4 %copy-start.6 = (f32[2,8192]{1,0:T(2,128)S(1)}, f32[2,8192]{1,0:T(2,128)}, u32[]{:S(2)}) copy-start(f32[2,8192]{1,0:T(2,128)} %second_ref.3) | copy-start | bytes 196612
  28.8 37.6 %all-to-all-start = ((bf16[64,16,1024]{2,1,0:T(8,128)(2,1)}), bf16[64,16,1024]{2,1,0:T(8,128)(2,1)S(1)}, u32[]{:S(2)}, u32[]{:S(2)}) async-start(bf16[64,16,1024]{2,1,0:T(8,128)(2,1)} %copy-done), calls=%async_computation | async-start | bytes 4194304 | tf_op jit(solution)/shard_map/all_to_all | solution.py:264
  105.1 6.2 %collective-permute-start.1 = (bf16[64,16,1152]{2,1,0:T(8,128)(2,1)S(1)}, bf16[64,16,1152]{2,1,0:T(8,128)(2,1)S(1)}, u32[]{:S(2)}, u32[]{:S(2)}) collective-permute-start(bf16[64,16,1152]{2,1,0:T(8,128)(2,1)S(1)} %all_to_all.15.own_ref.own_left_ref), channel_id=1, source_target_pairs={{0,1},{1,0},{2,3},{3,2},{4,5},{5,4},{6,7},{7,6},{8,9},{9,8},{10,11... | collective-permute-start | bytes 7077896 | tf_op jit(solution)/shard_map/ppermute | solution.py:276

commit v2 on v0

v2 whole, which is shorter than its diff:
```python
import jax
import jax.numpy as jnp
from jax import lax
from jax.experimental import pallas as pl
from jax.experimental.pallas import tpu as pltpu
from jax.sharding import Mesh
from jax.sharding import PartitionSpec as P

ADAM_STEP = 20

beta_one = 0.9
beta_two = 0.95
learn_rate = 0.05
epsilon = 1e-08

CHIPS = ("y", "z", "x")
BF = jnp.bfloat16
F32 = jnp.float32
HALF = 4096


def adam_update(master, first, second, gradient):
    first_new = beta_one * first + (1.0 - beta_one) * gradient
    second_new = beta_two * second + (1.0 - beta_two) * gradient * gradient
    corr_one = 1.0 - beta_one**ADAM_STEP
    corr_two = 1.0 - beta_two**ADAM_STEP
    master_new = master - learn_rate * (first_new / corr_one) / (
        jnp.sqrt(second_new / corr_two) + epsilon
    )
    return (master_new, first_new, second_new)


def iota(shape, dim):
    return lax.broadcasted_iota(jnp.int32, shape, dim)


def one_hot(target):
    return jnp.where(iota(target.shape, 1) == target, 1.0, 0.0).astype(BF)


def pick(matrix, values):
    return jnp.dot(matrix, values, preferred_element_type=F32)


def columns(core):
    return pl.ds(pl.multiple_of(core * HALF, HALF), HALF)


def turned(rows):
    return pltpu.roll(rows, 4, axis=0)


def spread_rows(low_ref, middle_ref, second_ref):
    y = lax.axis_index("y")
    return jnp.where(y == 0, low_ref[...], jnp.where(y == 1, middle_ref[...], second_ref[...]))


def pair_kernel(master_ref, first_ref, second_ref, low_ref, middle_ref, pair_ref, rows_ref):
    other = columns(1 - lax.axis_index("core"))
    for i, ref in enumerate((master_ref, first_ref, second_ref)):
        pair_ref[2 * i : 2 * i + 2, :] = ref[:, other]
    rows_ref[...] = spread_rows(low_ref, middle_ref, second_ref)
    pair_ref[6:8, :] = rows_ref[:, other]


def add_kernel(
    own_ref, got_ref, master_ref, first_ref, second_ref, low_ref, middle_ref, pair_ref,
    out_ref, old_ref, rows_ref, split_ref,
):
    core = lax.axis_index("core")
    low = iota((8, 1024), 0) < 4

    def kept(i, carry):
        rows = pl.ds(pl.multiple_of(16 * i, 16), 16)
        parts = []
        for k in range(4):
            cut = slice(k * 1024, (k + 1) * 1024)
            parts.append(own_ref[rows, cut].astype(F32) + got_ref[rows, cut].astype(F32))
        for tile in range(2):
            c = [part[8 * tile : 8 * tile + 8] for part in parts]
            even = [jnp.where(low, c[k], turned(c[k + 1])) for k in (0, 2)]
            odd = [jnp.where(low, turned(c[k]), c[k + 1]) for k in (0, 2)]
            for chip, block in ((4 * i + 2 * tile, even), (4 * i + 2 * tile + 1, odd)):
                out_ref[chip, :, 0:1024] = jnp.concatenate(block, axis=0).astype(BF)
        for chip in range(4):
            out_ref[4 * i + chip, :, 1024:1152] = jnp.zeros((16, 128), BF)
        return carry

    lax.fori_loop(0, 12, kept, 0)

    rows_ref[...] = spread_rows(low_ref, middle_ref, second_ref)
    for mine in range(2):

        @pl.when(core == mine)
        def _():
            for i, ref in enumerate((master_ref, first_ref, second_ref, rows_ref)):
                at = 4 * i + 2 * mine
                old_ref[at : at + 2, :] = ref[:, mine * HALF : (mine + 1) * HALF]
                at = 4 * i + 2 * (1 - mine)
                old_ref[at : at + 2, :] = pair_ref[2 * i : 2 * i + 2, :]

    passed = old_ref[12:16, :]
    high = passed.astype(BF).astype(F32)
    split_ref[0:4, :] = high
    split_ref[4:8, :] = passed - high

    def leave(q, carry):
        cut = pl.ds(pl.multiple_of(q * 256, 256), 256)
        for a in range(4):
            rows = slice(192 + 16 * a, 208 + 16 * a)
            total = own_ref[rows, cut].astype(F32) + got_ref[rows, cut].astype(F32)
            out_ref[48 + q, :, a * 256 : (a + 1) * 256] = total.astype(BF)
        parts = split_ref[:, cut]
        out_ref[48 + q, :, 1024:1152] = jnp.concatenate([parts[:, 0:128], parts[:, 128:256]], axis=0).astype(BF)
        return carry

    lax.fori_loop(0, 16, leave, 0)


def adam_kernel(parts_ref, chip_ref, owner_ref, out_ref, own_ref, other_ref, key_ref, old_ref):
    leaving = lax.axis_index("y") == 3
    core = lax.axis_index("core")

    def add(d, total):
        return total + parts_ref[d, :, 0:1024].astype(F32)

    gradient = lax.fori_loop(1, 64, add, parts_ref[0, :, 0:1024].astype(F32), unroll=7)

    @pl.when(leaving)
    def _():
        for i, y in enumerate((0, 1, 3)):
            for q in range(16):
                parts = parts_ref[16 * y + q, :, 1024:1152].astype(F32)
                for h in range(2):
                    value = parts[8 * h : 8 * h + 4] + parts[8 * h + 4 : 8 * h + 8]
                    at = (q // 4) * 256 + h * 128
                    old_ref[i, 4 * (q % 4) : 4 * (q % 4) + 4, at : at + 128] = value

    @pl.when(jnp.logical_not(leaving))
    def _():
        for i in range(3):
            for k in range(4):
                old_ref[i, 4 * k : 4 * k + 4, :] = chip_ref[4 * i : 4 * i + 4, k * 1024 : (k + 1) * 1024]

    new = adam_update(old_ref[0], old_ref[1], old_ref[2], gradient)
    own_ref[6:8, :] = jnp.zeros((2, HALF), F32)
    other_ref[6:8, :] = jnp.zeros((2, HALF), F32)
    values = [jnp.where(leaving, jnp.zeros_like(value), value) for value in new]
    for mine in range(2):

        @pl.when(core == mine)
        def _():
            for i in range(3):
                for k in range(4):
                    cut = slice(k * 1024, (k + 1) * 1024)
                    at = 4 * k + 2 * mine
                    own_ref[2 * i : 2 * i + 2, cut] = values[i][at : at + 2, :]
                    at = 4 * k + 2 * (1 - mine)
                    other_ref[2 * i : 2 * i + 2, cut] = values[i][at : at + 2, :]

    weights = new[0].astype(BF)

    def spread(d, carry):
        out_ref[d, :, 0:1024] = weights
        return carry

    lax.fori_loop(0, 64, spread, 0, unroll=8)

    lane, row = iota((64, 256), 1), iota((64, 256), 0)
    tiled = jnp.where((lane & 63) == row, 1.0, 0.0).astype(BF)
    across = pick(jnp.broadcast_to(owner_ref[...], (64, 64)).astype(F32).astype(BF), tiled)
    down = jnp.sum(jnp.where(lane == row, across, 0.0), axis=1, keepdims=True)
    earlier = (across == down) & (row < (lane & 63))
    slot = jnp.sum(jnp.where(earlier, 1.0, 0.0), axis=0, keepdims=True)
    key = (across[0:1, :] * 2.0 + slot).astype(jnp.int32) + 512 * (iota((1, 256), 1) >> 6)
    key_ref[...] = key
    moments = jnp.concatenate(
        [
            new[1 + part // 2][:, a * 256 + (part % 2) * 128 : a * 256 + (part % 2) * 128 + 128]
            for part in range(4)
            for a in range(4)
        ],
        axis=0,
    ).astype(BF)
    p = iota((1024, 256), 0)
    wanted = (p >> 4) * 4 + (p & 3) + 512 * ((p >> 2) & 3)
    chosen = jnp.where(key == wanted, 1.0, 0.0).astype(BF)
    out_ref[:, :, 1024:1152] = pick(chosen, moments).astype(BF).reshape(64, 16, 128)


def place_half(blocks_ref, key_ref, weights_ref, adopted_ref, adopted_at, rows_ref, sems, core, side):
    chip = (lax.axis_index("y") * 4 + lax.axis_index("z")) * 4 + lax.axis_index("x")
    low = iota((8, 1024), 0) < 4

    def store(i):
        rows = pl.ds(pl.multiple_of(32 * i, 32), 32)
        return pltpu.make_async_copy(rows_ref.at[rows, :], weights_ref.at[rows, columns(side)], sems.at[i])

    def kept(i, carry):
        for g in range(2):
            tiles = []
            for tile in range(2):
                number = 8 * i + 4 * g + 2 * tile
                even = blocks_ref[number, :, 0:1024].astype(F32)
                odd = blocks_ref[number + 1, :, 0:1024].astype(F32)
                cut = []
                for s in (slice(0, 8), slice(8, 16)):
                    cut.append(jnp.where(low, even[s], turned(odd[s])))
                    cut.append(jnp.where(low, turned(even[s]), odd[s]))
                tiles.append(cut)
            rows = pl.ds(pl.multiple_of(32 * i + 16 * g, 16), 16)
            for k in range(4):
                rows_ref[rows, k * 1024 : (k + 1) * 1024] = jnp.concatenate(
                    [tiles[0][k], tiles[1][k]], axis=0
                ).astype(BF)
        store(i).start()
        return carry

    lax.fori_loop(0, 6, kept, 0)
    for q in range(16):
        for a in range(4):
            rows_ref[192 + 16 * a : 208 + 16 * a, q * 256 : (q + 1) * 256] = blocks_ref[
                48 + q, :, a * 256 : (a + 1) * 256
            ]
    for i in range(6, 8):
        store(i).start()
    k = iota((8, 64), 0)
    wanted = jnp.where(k < 2, chip * 4 + core * 2 + k, -1)
    chosen = jnp.where(key_ref[:, 0:64] == wanted, 1.0, 0.0).astype(BF)
    masters = pick(chosen, rows_ref[192:256, :])
    adopted_ref[0, :, adopted_at(0, HALF)] = masters[0:2, :]
    moments = jnp.concatenate([blocks_ref[48 + q, :, 1024:1152] for q in range(16)], axis=1)
    for h in range(2):
        k = iota((8, 16), 0)
        found = pick(one_hot(jnp.where(k < 4, ((k >> 1) * 2 + h) * 4 + core * 2 + (k & 1), -1)), moments)
        for q in range(16):
            for i in range(2):
                adopted_ref[1 + i, :, adopted_at(q * 256 + h * 128, 128)] = found[
                    2 * i : 2 * i + 2, q * 128 : (q + 1) * 128
                ]
    for i in range(8):
        store(i).wait()


def place_own_kernel(blocks_ref, key_ref, weights_ref, adopted_ref, rows_ref, sems):
    core = lax.axis_index("core")
    place_half(
        blocks_ref, key_ref, weights_ref, adopted_ref, lambda start, size: slice(start, start + size),
        rows_ref, sems, core, core,
    )


def place_other_kernel(
    blocks_ref, key_ref, _, half_ref, own_ref, other_ref, weights_ref, adopted_ref, kept_ref, rows_ref, sems
):
    core = lax.axis_index("core")
    side = 1 - core

    def at(start, size):
        return pl.ds(pl.multiple_of(side * HALF + start, 128), size)

    place_half(blocks_ref, key_ref, weights_ref, adopted_ref, at, rows_ref, sems, core, side)
    for i in range(3):
        adopted_ref[i, :, columns(core)] = half_ref[i]
        kept_ref[i, :, columns(core)] = own_ref[2 * i : 2 * i + 2, :]
        kept_ref[i, :, columns(side)] = other_ref[2 * i : 2 * i + 2, :]


def params(mib=40):
    return pltpu.CompilerParams(vmem_limit_bytes=mib * 1024 * 1024)


def shape(dims, dtype):
    return jax.ShapeDtypeStruct(dims, dtype)


def swapped(value):
    return lax.ppermute(value, "core", [(0, 1), (1, 0)])


def from_leaving(value, group):
    return lax.ppermute(value, ("y", "z", "x", "core"), [(96 + rank, 32 * group + rank) for rank in range(32)])


def body(local_grads, master, first, second, new_owner):
    grads = local_grads.reshape(256, 8192)
    vmem = pl.BlockSpec(memory_space=pltpu.VMEM)
    hbm = pl.BlockSpec(memory_space=pltpu.HBM)
    core = lax.axis_index("core")
    got = swapped(lax.dynamic_slice(grads, (0, (1 - core) * HALF), (256, HALF)))
    own = lax.dynamic_slice(grads, (0, core * HALF), (256, HALF))
    low, middle = from_leaving(master, 0), from_leaving(first, 1)
    pair = pl.pallas_call(
        pair_kernel,
        in_specs=[vmem] * 5,
        out_specs=vmem,
        out_shape=shape((8, HALF), F32),
        scratch_shapes=[pltpu.VMEM((2, 8192), F32)],
        compiler_params=params(),
        name="pair",
    )(master, first, second, low, middle)
    pair = swapped(pair)
    partial, old = pl.pallas_call(
        add_kernel,
        in_specs=[vmem] * 8,
        out_specs=[vmem] * 2,
        out_shape=[shape((64, 16, 1152), BF), shape((16, HALF), F32)],
        scratch_shapes=[pltpu.VMEM((2, 8192), F32), pltpu.VMEM((8, HALF), F32)],
        compiler_params=params(),
        name="add_blocks",
    )(own, got, master, first, second, low, middle, pair)
    partial = lax.all_to_all(partial, CHIPS, 0, 0, tiled=True)
    payload, own_new, other_new, key = pl.pallas_call(
        adam_kernel,
        in_specs=[vmem] * 3,
        out_specs=[vmem] * 4,
        out_shape=[
            shape((64, 16, 1152), BF),
            shape((8, HALF), F32),
            shape((8, HALF), F32),
            shape((1, 256), jnp.int32),
        ],
        scratch_shapes=[pltpu.VMEM((3, 16, 1024), F32)],
        compiler_params=params(),
        name="adam",
    )(partial, old, new_owner.reshape(1, 64))
    other_new = swapped(other_new)
    blocks = lax.all_to_all(payload, CHIPS, 0, 0, tiled=True)
    other_blocks = swapped(blocks)
    scratch = [pltpu.VMEM((256, HALF), BF), pltpu.SemaphoreType.DMA((8,))]
    weights, adopted = pl.pallas_call(
        place_own_kernel,
        in_specs=[vmem, vmem],
        out_specs=[hbm, vmem],
        out_shape=[shape((256, 8192), BF), shape((3, 2, HALF), F32)],
        scratch_shapes=scratch,
        compiler_params=params(),
        cost_estimate=pl.CostEstimate(flops=8_000_000, bytes_accessed=8_000_000, transcendentals=0),
        name="place_own",
    )(blocks, key)
    weights, adopted, kept = pl.pallas_call(
        place_other_kernel,
        in_specs=[vmem, vmem, hbm, vmem, vmem, vmem],
        out_specs=[hbm, vmem, vmem],
        out_shape=[shape((256, 8192), BF), shape((3, 2, 8192), F32), shape((3, 2, 8192), F32)],
        scratch_shapes=scratch,
        input_output_aliases={2: 0},
        compiler_params=params(),
        name="place_other",
    )(other_blocks, key, weights, adopted, own_new, other_new)
    return (weights, kept.transpose(1, 0, 2), adopted.transpose(1, 0, 2)[None, None])


def solution(mesh):
    fine = Mesh(mesh.devices.reshape(4, 4, 4, 2), ("y", "z", "x", "core"))
    every = ("y", "z", "x", "core")
    in_specs = (P("y", ("z", "x", "core"), None, None), P(every, None), P(every, None), P(every, None), P())
    out_specs = (P(), P(every, None, None), P("y", ("z", "x", "core"), None, None, None))
    return jax.shard_map(body, mesh=fine, in_specs=in_specs, out_specs=out_specs, check_vma=False)
```

time: 364 us -> 105 us (0.29)
  waiting for transfers between devices: 320 us -> 8.71 us
  blocking collectives: 0 us -> 80.2 us
  between operations: 13.8 us -> 0.73 us
  other arithmetic: 11 us -> 0 us
  matrix products: 10.4 us -> 0 us
  local copies, waits for them, and re-layouts: 9 us -> 2.78 us
  starting transfers between devices: 0.16 us -> 6.37 us
  Pallas kernels: 0 us -> 5.86 us
    unnamed x5 -> x0, waiting for transfers between devices: 166 us -> none
    all_gather x2 -> x0, waiting for transfers between devices: 116 us -> none  [the longest x1 70.8 us: body(): lax.all_gather(master_new.astype(jnp.bfloat16), ('group', 'rank'), axis=0...]
    all_to_all x0 -> x2, blocking collectives: none -> 80.2 us  [the longest x1 42.8 us: body(): partial = lax.all_to_all(partial, CHIPS, 0, 0, tiled=True)]
    psum x1 -> x0, waiting for transfers between devices: 37.5 us -> none  [broadcast(): return lax.psum(jnp.where(mine, value, jnp.zeros_like(value)), axis)]
    dot_general x1 -> x0, matrix products: 10.4 us -> none  [hand_over(): jnp.einsum('kt,tfd->kfd', selector, shard_rows, precision=lax.Precision.H...]
    ppermute x0 -> x6, waiting for transfers between devices: none -> 8.71 us  [the longest x2 4.81 us: from_leaving(): lax.ppermute(value, ('y', 'z', 'x', 'core'), [(96 + rank, 32 * group + ra...]
    unnamed x9 -> x8, local copies, waits for them, and re-layouts: 7.18 us -> 0.02 us
    convert_element_type x1 -> x0, other arithmetic: 6.44 us -> none  [body(): own_grads.astype(jnp.float32)]
  transfers between devices with their start and end apart: 4 -> 6, of which waited for: 4 -> 3; matrix products, arithmetic and copies ran while one was open for 3% -> 0% of each run, Pallas kernels for 0% -> 1%
where the time goes in v2:
time: 105 us
  blocking collectives  80.2 us (76%)
  waiting for transfers between devices  8.71 us (8%)
  starting transfers between devices  6.37 us (6%)
  Pallas kernels  5.86 us (6%)
  local copies, waits for them, and re-layouts  2.78 us (3%)
    all_to_all x1, blocking collectives, body(): partial = lax.all_to_all(partial, CHIPS, 0, 0, tiled=True)  42.8 us
    all_to_all x1, blocking collectives, body(): blocks = lax.all_to_all(payload, CHIPS, 0, 0, tiled=True)  37.3 us
    ppermute x2, waiting for transfers between devices, from_leaving(): lax.ppermute(value, ('y', 'z', 'x', 'core'), [(96 + rank, 32 * group + ra...  4.81 us
    ppermute x4, starting transfers between devices, swapped(): return lax.ppermute(value, 'core', [(0, 1), (1, 0)])  4.42 us
    ppermute x4, waiting for transfers between devices, swapped(): return lax.ppermute(value, 'core', [(0, 1), (1, 0)])  3.89 us
    dynamic_slice x1, local copies, waits for them, and re-layouts, body(): got = swapped(lax.dynamic_slice(grads, (0, (1 - core) * HALF), (256, HALF)))  2.76 us
    pallas_call x1, Pallas kernels, body(): pl.pallas_call(place_other_kernel, in_specs=[vmem, vmem, hbm, vmem, vmem,...  2.22 us
  transfers between devices with their start and end apart: 6, of which 3 were waited for; matrix products, arithmetic and copies ran while one was open for 0% of the time, Pallas kernels for 1%

profile of v2, /device:TPU:1, one launch (start us, length us, event | category | flops | bytes accessed | tf_op | source)
XLA Modules:
  0.0 104.6 jit_solution(3845333195836177854)
XLA Ops:
  0.6 0.0 copy-start
  0.6 0.0 copy-start.1
  0.7 0.0 copy-start.2
  0.7 2.8 %dynamic-slice_bitcast_fusion = (bf16[256,4096]{1,0:T(8,128)(2,1)S(1)}, bf16[256,4096]{1,0:T(8,128)(2,1)S(1)}) fusion(bf16[1,1,256,8192]{3,2,1,0:T(8,128)(2,1)} %param.5, s32[]{:T(128)S(6)} %select_n.7, s32[]{:T(128)S(6)} %select_n.6), kind=kLoop, calls=%fused_computation | loop fusion | bytes 8388616 | tf_op jit(solution)/shard_map/dynamic_slice | solution.py:290
  3.4 1.5 %collective-permute-start = (bf16[256,4096]{1,0:T(8,128)(2,1)S(1)}, bf16[256,4096]{1,0:T(8,128)(2,1)S(1)}, u32[]{:S(2)}, u32[]{:S(2)}) collective-permute-start(bf16[256,4096]{1,0:T(8,128)(2,1)S(1)} %get-tuple-element.25), channel_id=1, source_target_pairs={{0,1},{1,0},{2,3},{3,2},{4,5},{5,4},{6,7},{7,6},{8,9},{9,8},{10,11... | collective-permute-start | bytes 6291464 | tf_op jit(solution)/shard_map/ppermute | solution.py:278
  4.9 1.3 %collective-permute-start.1 = (f32[2,8192]{1,0:T(2,128)S(1)}, f32[2,8192]{1,0:T(2,128)S(1)}, u32[]{:S(2)}, u32[]{:S(2)}) collective-permute-start(f32[2,8192]{1,0:T(2,128)S(1)} %copy-done), channel_id=1, source_target_pairs={{96,0},{97,1},{98,2},{99,3},{100,4},{101,5},{102,6},{103,7},{104,8... | collective-permute-start | bytes 196616 | tf_op jit(solution)/shard_map/ppermute | solution.py:282
  6.2 0.7 collective-permute-start.2
  6.9 4.8 %collective-permute-done.1.low_ref = f32[2,8192]{1,0:T(2,128)S(1)} collective-permute-done((f32[2,8192]{1,0:T(2,128)S(1)}, f32[2,8192]{1,0:T(2,128)S(1)}, u32[]{:S(2)}, u32[]{:S(2)}) %collective-permute-start.1) | collective-permute-done | bytes 65568 | tf_op jit(solution)/shard_map/ppermute | solution.py:282
  11.7 0.0 collective-permute-done.2.middle_ref
  11.7 0.1 pair.1
  11.8 0.9 collective-permute-start.3
  12.7 1.0 collective-permute-done.3.pair_ref
  13.7 0.0 collective-permute-done.got_ref
  13.7 1.0 add_blocks.1
  14.7 0.0 copy-start.3
  14.7 42.8 %all_to_all.10.parts_ref = bf16[64,16,1152]{2,1,0:T(8,128)(2,1)S(1)} all-to-all(bf16[64,16,1152]{2,1,0:T(8,128)(2,1)S(1)} %get-tuple-element.14), channel_id=1, replica_groups=mesh['y'=4,'z'=4,'x'=4,'core'=2] {'y','z','x'}, dimensions={0} | all-to-all | bytes 4718592 | tf_op jit(solution)/shard_map/all_to_all | solution.py:312
  57.5 1.2 %adam.1 = (bf16[64,16,1152]{2,1,0:T(8,128)(2,1)S(1)}, f32[8,4096]{1,0:T(8,128)S(1)}, f32[8,4096]{1,0:T(8,128)S(1)}, s32[1,256]{1,0:T(1,128)S(1)}) custom-call(bf16[64,16,1152]{2,1,0:T(8,128)(2,1)S(1)} %all_to_all.10.parts_ref, f32[16,4096]{1,0:T(8,128)S(1)} %get-tuple-element.15.chip_ref, s32[1,64]{1,0:T(1,128)S(1)} %bitcast.9), custom_call_target="tpu_custom_call" | custom-call | tf_op jit(solution)/shard_map/adam/pallas_call | solution.py:313
  58.7 37.3 %all_to_all.11.blocks_ref = bf16[64,16,1152]{2,1,0:T(8,128)(2,1)S(1)} all-to-all(bf16[64,16,1152]{2,1,0:T(8,128)(2,1)S(1)} %get-tuple-element.16), channel_id=1, replica_groups=mesh['y'=4,'z'=4,'x'=4,'core'=2] {'y','z','x'}, dimensions={0} | all-to-all | bytes 4718592 | tf_op jit(solution)/shard_map/all_to_all | solution.py:328
  96.0 2.0 %collective-permute-start.4 = (bf16[64,16,1152]{2,1,0:T(8,128)(2,1)S(1)}, bf16[64,16,1152]{2,1,0:T(8,128)(2,1)S(1)}, u32[]{:S(2)}, u32[]{:S(2)}) collective-permute-start(bf16[64,16,1152]{2,1,0:T(8,128)(2,1)S(1)} %all_to_all.11.blocks_ref), channel_id=1, source_target_pairs={{0,1},{1,0},{2,3},{3,2},{4,5},{5,4},{6,7},{7,6},{8,9},{9,8},{10,11... | collective-permute-start | bytes 7077896 | tf_op jit(solution)/shard_map/ppermute | solution.py:278
  98.0 0.0 collective-permute-start.5
  98.0 1.4 %place_own.1 = (bf16[256,8192]{1,0:T(8,128)(2,1)}, f32[3,2,4096]{2,1,0:T(2,128)S(1)}) custom-call(bf16[64,16,1152]{2,1,0:T(8,128)(2,1)S(1)} %all_to_all.11.blocks_ref, s32[1,256]{1,0:T(1,128)S(1)} %get-tuple-element.17.key_ref), custom_call_target="tpu_custom_call" | custom-call | flops 8000000 | bytes 8000000 | tf_op jit(solution)/shard_map/place_own/pallas_call | solution.py:331
  99.5 2.9 %collective-permute-done.5.other_ref = f32[8,4096]{1,0:T(8,128)S(1)} collective-permute-done((f32[8,4096]{1,0:T(8,128)S(1)}, f32[8,4096]{1,0:T(8,128)S(1)}, u32[]{:S(2)}, u32[]{:S(2)}) %collective-permute-start.5) | collective-permute-done | bytes 131104 | tf_op jit(solution)/shard_map/ppermute | solution.py:278
  102.4 0.0 collective-permute-done.4.blocks_ref
  102.4 2.2 %place_other.1 = (bf16[256,8192]{1,0:T(8,128)(2,1)}, f32[3,2,8192]{2,1,0:T(2,128)}, f32[3,2,8192]{2,1,0:T(2,128)}) custom-call(bf16[64,16,1152]{2,1,0:T(8,128)(2,1)S(1)} %collective-permute-done.4.blocks_ref, s32[1,256]{1,0:T(1,128)S(1)} %get-tuple-element.17.key_ref, bf16[256,8192]{1,0:T(8,128)(2,1)} %get-tuple-element.18._, ...), custom_call_target="tpu_custom_call", output_to_operand_aliasing={{0}: (2, {})} | custom-call | tf_op jit(solution)/shard_map/place_other/pallas_call | solution.py:341
  (4 shorter events, 0.0 us)
Async XLA Ops:
  0.6 4.3 %copy-start = (f32[2,8192]{1,0:T(2,128)S(1)}, f32[2,8192]{1,0:T(2,128)}, u32[]{:S(2)}) copy-start(f32[2,8192]{1,0:T(2,128)} %master_ref.3) | copy-start | bytes 196612
  0.6 5.6 %copy-start.1 = (f32[2,8192]{1,0:T(2,128)S(1)}, f32[2,8192]{1,0:T(2,128)}, u32[]{:S(2)}) copy-start(f32[2,8192]{1,0:T(2,128)} %first_ref.3) | copy-start | bytes 196612
  0.7 11.1 %copy-start.2 = (f32[2,8192]{1,0:T(2,128)S(1)}, f32[2,8192]{1,0:T(2,128)}, u32[]{:S(2)}) copy-start(f32[2,8192]{1,0:T(2,128)} %second_ref.3) | copy-start | bytes 196612
  3.4 10.2 %collective-permute-start = (bf16[256,4096]{1,0:T(8,128)(2,1)S(1)}, bf16[256,4096]{1,0:T(8,128)(2,1)S(1)}, u32[]{:S(2)}, u32[]{:S(2)}) collective-permute-start(bf16[256,4096]{1,0:T(8,128)(2,1)S(1)} %get-tuple-element.25), channel_id=1, source_target_pairs={{0,1},{1,0},{2,3},{3,2},{4,5},{5,4},{6,7},{7,6},{8,9},{9,8},{10,11... | collective-permute-start | bytes 6291464 | tf_op jit(solution)/shard_map/ppermute | solution.py:278
  4.9 6.8 %collective-permute-start.1 = (f32[2,8192]{1,0:T(2,128)S(1)}, f32[2,8192]{1,0:T(2,128)S(1)}, u32[]{:S(2)}, u32[]{:S(2)}) collective-permute-start(f32[2,8192]{1,0:T(2,128)S(1)} %copy-done), channel_id=1, source_target_pairs={{96,0},{97,1},{98,2},{99,3},{100,4},{101,5},{102,6},{103,7},{104,8... | collective-permute-start | bytes 196616 | tf_op jit(solution)/shard_map/ppermute | solution.py:282
  6.2 5.5 %collective-permute-start.2 = (f32[2,8192]{1,0:T(2,128)S(1)}, f32[2,8192]{1,0:T(2,128)S(1)}, u32[]{:S(2)}, u32[]{:S(2)}) collective-permute-start(f32[2,8192]{1,0:T(2,128)S(1)} %copy-done.1), channel_id=1, source_target_pairs={{96,32},{97,33},{98,34},{99,35},{100,36},{101,37},{102,38},{103,39... | collective-permute-start | bytes 196616 | tf_op jit(solution)/shard_map/ppermute | solution.py:282
  11.8 1.9 %collective-permute-start.3 = (f32[8,4096]{1,0:T(8,128)S(1)}, f32[8,4096]{1,0:T(8,128)S(1)}, u32[]{:S(2)}, u32[]{:S(2)}) collective-permute-start(f32[8,4096]{1,0:T(8,128)S(1)} %pair.1), channel_id=1, source_target_pairs={{0,1},{1,0},{2,3},{3,2},{4,5},{5,4},{6,7},{7,6},{8,9},{9,8},{10,11... | collective-permute-start | bytes 393224 | tf_op jit(solution)/shard_map/ppermute | solution.py:278
  14.7 42.9 %copy-start.3 = (s32[64]{0:T(128)S(1)}, s32[64]{0:T(128)}, u32[]{:S(2)}) copy-start(s32[64]{0:T(128)} %param.9) | copy-start | bytes 772
  96.0 6.4 %collective-permute-start.4 = (bf16[64,16,1152]{2,1,0:T(8,128)(2,1)S(1)}, bf16[64,16,1152]{2,1,0:T(8,128)(2,1)S(1)}, u32[]{:S(2)}, u32[]{:S(2)}) collective-permute-start(bf16[64,16,1152]{2,1,0:T(8,128)(2,1)S(1)} %all_to_all.11.blocks_ref), channel_id=1, source_target_pairs={{0,1},{1,0},{2,3},{3,2},{4,5},{5,4},{6,7},{7,6},{8,9},{9,8},{10,11... | collective-permute-start | bytes 7077896 | tf_op jit(solution)/shard_map/ppermute | solution.py:278
  98.0 4.3 %collective-permute-start.5 = (f32[8,4096]{1,0:T(8,128)S(1)}, f32[8,4096]{1,0:T(8,128)S(1)}, u32[]{:S(2)}, u32[]{:S(2)}) collective-permute-start(f32[8,4096]{1,0:T(8,128)S(1)} %get-tuple-element.21), channel_id=1, source_target_pairs={{0,1},{1,0},{2,3},{3,2},{4,5},{5,4},{6,7},{7,6},{8,9},{9,8},{10,11... | collective-permute-start | bytes 393224 | tf_op jit(solution)/shard_map/ppermute | solution.py:278

commit v3 on v2

--- a/solution.py
+++ b/solution.py
@@ -55,19 +55,27 @@
     return jnp.where(y == 0, low_ref[...], jnp.where(y == 1, middle_ref[...], second_ref[...]))
 
 
-def pair_kernel(master_ref, first_ref, second_ref, low_ref, middle_ref, pair_ref, rows_ref):
+def chip_class(chip):
+    return (chip & 1) ^ (((chip >> 4) & 1) * 2) ^ (((chip >> 2) & 1) * 3)
+
+
+def own_chip():
+    return (lax.axis_index("y") * 4 + lax.axis_index("z")) * 4 + lax.axis_index("x")
+
+
+def quarter(number):
+    return pl.ds(pl.multiple_of(number * 256, 256), 256)
+
+
+def add_kernel(
+    own_ref, got_ref, master_ref, first_ref, second_ref, low_ref, middle_ref,
+    keep_ref, x_up, x_down, y_up, y_down, z_up, z_down, pair_ref, blocks_ref, rows_ref,
+):
     other = columns(1 - lax.axis_index("core"))
     for i, ref in enumerate((master_ref, first_ref, second_ref)):
         pair_ref[2 * i : 2 * i + 2, :] = ref[:, other]
     rows_ref[...] = spread_rows(low_ref, middle_ref, second_ref)
     pair_ref[6:8, :] = rows_ref[:, other]
-
-
-def add_kernel(
-    own_ref, got_ref, master_ref, first_ref, second_ref, low_ref, middle_ref, pair_ref,
-    out_ref, old_ref, rows_ref, split_ref,
-):
-    core = lax.axis_index("core")
     low = iota((8, 1024), 0) < 4
 
     def kept(i, carry):
@@ -81,12 +89,43 @@
             even = [jnp.where(low, c[k], turned(c[k + 1])) for k in (0, 2)]
             odd = [jnp.where(low, turned(c[k]), c[k + 1]) for k in (0, 2)]
             for chip, block in ((4 * i + 2 * tile, even), (4 * i + 2 * tile + 1, odd)):
-                out_ref[chip, :, 0:1024] = jnp.concatenate(block, axis=0).astype(BF)
-        for chip in range(4):
-            out_ref[4 * i + chip, :, 1024:1152] = jnp.zeros((16, 128), BF)
+                blocks_ref[chip] = jnp.concatenate(block, axis=0).astype(BF)
         return carry
 
     lax.fori_loop(0, 12, kept, 0)
+
+    def leave(q, carry):
+        cut = pl.ds(pl.multiple_of(q * 256, 256), 256)
+        for a in range(4):
+            rows = slice(192 + 16 * a, 208 + 16 * a)
+            total = own_ref[rows, cut].astype(F32) + got_ref[rows, cut].astype(F32)
+            blocks_ref[48 + q, :, a * 256 : (a + 1) * 256] = total.astype(BF)
+        return carry
+
+    lax.fori_loop(0, 16, leave, 0)
+    kind = chip_class(own_chip())
+    keep_ref[...] = blocks_ref[:, :, quarter(kind)]
+    for axis, (up, down) in enumerate(((x_up, x_down), (y_up, y_down), (z_up, z_down))):
+        up[...] = blocks_ref[0:32, :, quarter(kind ^ (axis + 1))]
+        down[...] = blocks_ref[32:64, :, quarter(kind ^ (axis + 1))]
+
+
+def merge_kernel(
+    keep_ref, x_up, x_down, y_up, y_down, z_up, z_down,
+    master_ref, first_ref, second_ref, low_ref, middle_ref, pair_ref,
+    out_ref, old_ref, rows_ref, split_ref,
+):
+    core = lax.axis_index("core")
+
+    def add(d, carry):
+        for base, refs in ((0, (x_up, y_up, z_up)), (32, (x_down, y_down, z_down))):
+            total = keep_ref[base + d].astype(F32)
+            for ref in refs:
+                total = total + ref[d].astype(F32)
+            out_ref[base + d, :, 0:256] = total.astype(BF)
+        return carry
+
+    lax.fori_loop(0, 32, add, 0, unroll=8)
 
     rows_ref[...] = spread_rows(low_ref, middle_ref, second_ref)
     for mine in range(2):
@@ -104,33 +143,34 @@
     split_ref[0:4, :] = high
     split_ref[4:8, :] = passed - high
 
+    def empty(d, carry):
+        out_ref[d, :, 256:384] = jnp.zeros((16, 128), BF)
+        return carry
+
+    lax.fori_loop(0, 48, empty, 0, unroll=8)
+
     def leave(q, carry):
-        cut = pl.ds(pl.multiple_of(q * 256, 256), 256)
-        for a in range(4):
-            rows = slice(192 + 16 * a, 208 + 16 * a)
-            total = own_ref[rows, cut].astype(F32) + got_ref[rows, cut].astype(F32)
-            out_ref[48 + q, :, a * 256 : (a + 1) * 256] = total.astype(BF)
-        parts = split_ref[:, cut]
-        out_ref[48 + q, :, 1024:1152] = jnp.concatenate([parts[:, 0:128], parts[:, 128:256]], axis=0).astype(BF)
-        return carry
-
-    lax.fori_loop(0, 16, leave, 0)
+        parts = split_ref[:, quarter(q)]
+        out_ref[48 + q, :, 256:384] = jnp.concatenate([parts[:, 0:128], parts[:, 128:256]], axis=0).astype(BF)
+        return carry
+
+    lax.fori_loop(0, 16, leave, 0, unroll=4)
 
 
 def adam_kernel(parts_ref, chip_ref, owner_ref, out_ref, own_ref, other_ref, key_ref, old_ref):
     leaving = lax.axis_index("y") == 3
     core = lax.axis_index("core")
-
-    def add(d, total):
-        return total + parts_ref[d, :, 0:1024].astype(F32)
-
-    gradient = lax.fori_loop(1, 64, add, parts_ref[0, :, 0:1024].astype(F32), unroll=7)
+    totals = [jnp.zeros((16, 256), F32)] * 4
+    for chip in range(64):
+        kind = chip_class(chip)
+        totals[kind] = totals[kind] + parts_ref[chip, :, 0:256].astype(F32)
+    gradient = jnp.concatenate(totals, axis=1)
 
     @pl.when(leaving)
     def _():
         for i, y in enumerate((0, 1, 3)):
             for q in range(16):
-                parts = parts_ref[16 * y + q, :, 1024:1152].astype(F32)
+                parts = parts_ref[16 * y + q, :, 256:384].astype(F32)
                 for h in range(2):
                     value = parts[8 * h : 8 * h + 4] + parts[8 * h + 4 : 8 * h + 8]
                     at = (q // 4) * 256 + h * 128
@@ -160,11 +200,9 @@
 
     weights = new[0].astype(BF)
 
-    def spread(d, carry):
-        out_ref[d, :, 0:1024] = weights
-        return carry
-
-    lax.fori_loop(0, 64, spread, 0, unroll=8)
+    for chip in range(64):
+        kind = chip_class(chip)
+        out_ref[chip, :, 0:256] = weights[:, kind * 256 : (kind + 1) * 256]
 
     lane, row = iota((64, 256), 1), iota((64, 256), 0)
     tiled = jnp.where((lane & 63) == row, 1.0, 0.0).astype(BF)
@@ -185,43 +223,60 @@
     p = iota((1024, 256), 0)
     wanted = (p >> 4) * 4 + (p & 3) + 512 * ((p >> 2) & 3)
     chosen = jnp.where(key == wanted, 1.0, 0.0).astype(BF)
-    out_ref[:, :, 1024:1152] = pick(chosen, moments).astype(BF).reshape(64, 16, 128)
-
-
-def place_half(blocks_ref, key_ref, weights_ref, adopted_ref, adopted_at, rows_ref, sems, core, side):
-    chip = (lax.axis_index("y") * 4 + lax.axis_index("z")) * 4 + lax.axis_index("x")
-    low = iota((8, 1024), 0) < 4
+    out_ref[:, :, 256:384] = pick(chosen, moments).astype(BF).reshape(64, 16, 128)
+
+
+def halve_kernel(blocks_ref, *out_refs):
+    for i, ref in enumerate(out_refs):
+        ref[...] = blocks_ref[32 * (i % 2) : 32 * (i % 2) + 32, :, 0:256]
+
+
+def join_kernel(blocks_ref, x_up, x_down, y_up, y_down, z_up, z_down, out_ref):
+    out_ref[:, :, 0:384] = blocks_ref[...]
+    for at, up, down in ((384, x_up, x_down), (640, y_up, y_down), (896, z_up, z_down)):
+        out_ref[0:32, :, at : at + 256] = up[...]
+        out_ref[32:64, :, at : at + 256] = down[...]
+
+
+def place_half(views, key_ref, weights_ref, adopted_ref, adopted_at, rows_ref, sems, core, side):
+    blocks_ref = views[0][0][0]
+    chip = own_chip()
+    kind = chip_class(chip)
+    low = iota((8, 256), 0) < 4
 
     def store(i):
         rows = pl.ds(pl.multiple_of(32 * i, 32), 32)
         return pltpu.make_async_copy(rows_ref.at[rows, :], weights_ref.at[rows, columns(side)], sems.at[i])
 
-    def kept(i, carry):
-        for g in range(2):
-            tiles = []
-            for tile in range(2):
-                number = 8 * i + 4 * g + 2 * tile
-                even = blocks_ref[number, :, 0:1024].astype(F32)
-                odd = blocks_ref[number + 1, :, 0:1024].astype(F32)
-                cut = []
-                for s in (slice(0, 8), slice(8, 16)):
-                    cut.append(jnp.where(low, even[s], turned(odd[s])))
-                    cut.append(jnp.where(low, turned(even[s]), odd[s]))
-                tiles.append(cut)
-            rows = pl.ds(pl.multiple_of(32 * i + 16 * g, 16), 16)
-            for k in range(4):
-                rows_ref[rows, k * 1024 : (k + 1) * 1024] = jnp.concatenate(
-                    [tiles[0][k], tiles[1][k]], axis=0
-                ).astype(BF)
+    def kept(last, i, carry):
+        for axis in range(4):
+            ref, base, lane = views[axis][last]
+            for g in range(2):
+                tiles = []
+                for tile in range(2):
+                    number = 8 * i + 4 * g + 2 * tile - base
+                    even = ref[number, :, lane : lane + 256].astype(F32)
+                    odd = ref[number + 1, :, lane : lane + 256].astype(F32)
+                    cut = []
+                    for s in (slice(0, 8), slice(8, 16)):
+                        cut.append(jnp.where(low, even[s], turned(odd[s])))
+                        cut.append(jnp.where(low, turned(even[s]), odd[s]))
+                    tiles.append(cut)
+                rows = pl.ds(pl.multiple_of(32 * i + 16 * g, 16), 16)
+                for k in range(4):
+                    rows_ref[rows, quarter((kind ^ axis) + 4 * k)] = jnp.concatenate(
+                        [tiles[0][k], tiles[1][k]], axis=0
+                    ).astype(BF)
         store(i).start()
         return carry
 
-    lax.fori_loop(0, 6, kept, 0)
-    for q in range(16):
-        for a in range(4):
-            rows_ref[192 + 16 * a : 208 + 16 * a, q * 256 : (q + 1) * 256] = blocks_ref[
-                48 + q, :, a * 256 : (a + 1) * 256
-            ]
+    lax.fori_loop(0, 4, lambda i, carry: kept(0, i, carry), 0)
+    lax.fori_loop(4, 6, lambda i, carry: kept(1, i, carry), 0)
+    for axis in range(4):
+        ref, base, lane = views[axis][1]
+        rows = pl.ds(pl.multiple_of(192 + 16 * (kind ^ axis), 16), 16)
+        for q in range(16):
+            rows_ref[rows, q * 256 : (q + 1) * 256] = ref[48 + q - base, :, lane : lane + 256]
     for i in range(6, 8):
         store(i).start()
     k = iota((8, 64), 0)
@@ -229,7 +284,7 @@
     chosen = jnp.where(key_ref[:, 0:64] == wanted, 1.0, 0.0).astype(BF)
     masters = pick(chosen, rows_ref[192:256, :])
     adopted_ref[0, :, adopted_at(0, HALF)] = masters[0:2, :]
-    moments = jnp.concatenate([blocks_ref[48 + q, :, 1024:1152] for q in range(16)], axis=1)
+    moments = jnp.concatenate([blocks_ref[48 + q, :, 256:384] for q in range(16)], axis=1)
     for h in range(2):
         k = iota((8, 16), 0)
         found = pick(one_hot(jnp.where(k < 4, ((k >> 1) * 2 + h) * 4 + core * 2 + (k & 1), -1)), moments)
@@ -242,24 +297,29 @@
         store(i).wait()
 
 
-def place_own_kernel(blocks_ref, key_ref, weights_ref, adopted_ref, rows_ref, sems):
+def place_own_kernel(*refs):
+    blocks_ref, *pieces = refs[:7]
+    key_ref, weights_ref, adopted_ref, rows_ref, sems = refs[7:]
+    views = [[(blocks_ref, 0, 0)] * 2]
+    views += [[(pieces[2 * axis + last], 32 * last, 0) for last in range(2)] for axis in range(3)]
     core = lax.axis_index("core")
     place_half(
-        blocks_ref, key_ref, weights_ref, adopted_ref, lambda start, size: slice(start, start + size),
+        views, key_ref, weights_ref, adopted_ref, lambda start, size: slice(start, start + size),
         rows_ref, sems, core, core,
     )
 
 
-def place_other_kernel(
-    blocks_ref, key_ref, _, half_ref, own_ref, other_ref, weights_ref, adopted_ref, kept_ref, rows_ref, sems
-):
+def place_other_kernel(*refs):
+    joined_ref, key_ref, _, half_ref, own_ref, other_ref = refs[:6]
+    weights_ref, adopted_ref, kept_ref, rows_ref, sems = refs[6:]
+    views = [[(joined_ref, 0, lane)] * 2 for lane in (0, 384, 640, 896)]
     core = lax.axis_index("core")
     side = 1 - core
 
     def at(start, size):
         return pl.ds(pl.multiple_of(side * HALF + start, 128), size)
 
-    place_half(blocks_ref, key_ref, weights_ref, adopted_ref, at, rows_ref, sems, core, side)
+    place_half(views, key_ref, weights_ref, adopted_ref, at, rows_ref, sems, core, side)
     for i in range(3):
         adopted_ref[i, :, columns(core)] = half_ref[i]
         kept_ref[i, :, columns(core)] = own_ref[2 * i : 2 * i + 2, :]
@@ -276,6 +336,14 @@
 
 def swapped(value):
     return lax.ppermute(value, "core", [(0, 1), (1, 0)])
+
+
+def to_neighbours(up_and_down):
+    got = []
+    for i, axis in enumerate(("x", "y", "z")):
+        for value, shift in zip(up_and_down[2 * i : 2 * i + 2], (1, 3)):
+            got.append(lax.ppermute(value, axis, [(p, (p + shift) % 4) for p in range(4)]))
+    return got
 
 
 def from_leaving(value, group):
@@ -290,32 +358,35 @@
     got = swapped(lax.dynamic_slice(grads, (0, (1 - core) * HALF), (256, HALF)))
     own = lax.dynamic_slice(grads, (0, core * HALF), (256, HALF))
     low, middle = from_leaving(master, 0), from_leaving(first, 1)
-    pair = pl.pallas_call(
-        pair_kernel,
-        in_specs=[vmem] * 5,
-        out_specs=vmem,
-        out_shape=shape((8, HALF), F32),
-        scratch_shapes=[pltpu.VMEM((2, 8192), F32)],
-        compiler_params=params(),
-        name="pair",
-    )(master, first, second, low, middle)
+    piece = shape((32, 16, 256), BF)
+    *to_send, pair = pl.pallas_call(
+        add_kernel,
+        in_specs=[vmem] * 7,
+        out_specs=[vmem] * 8,
+        out_shape=[shape((64, 16, 256), BF)] + [piece] * 6 + [shape((8, HALF), F32)],
+        scratch_shapes=[pltpu.VMEM((64, 16, 1024), BF), pltpu.VMEM((2, 8192), F32)],
+        compiler_params=params(),
+        name="add_blocks",
+    )(own, got, master, first, second, low, middle)
+    keep, *to_send = to_send
+    arrived = to_neighbours(to_send)
     pair = swapped(pair)
     partial, old = pl.pallas_call(
-        add_kernel,
-        in_specs=[vmem] * 8,
+        merge_kernel,
+        in_specs=[vmem] * 13,
         out_specs=[vmem] * 2,
-        out_shape=[shape((64, 16, 1152), BF), shape((16, HALF), F32)],
+        out_shape=[shape((64, 16, 384), BF), shape((16, HALF), F32)],
         scratch_shapes=[pltpu.VMEM((2, 8192), F32), pltpu.VMEM((8, HALF), F32)],
         compiler_params=params(),
-        name="add_blocks",
-    )(own, got, master, first, second, low, middle, pair)
+        name="merge",
+    )(keep, *arrived, master, first, second, low, middle, pair)
     partial = lax.all_to_all(partial, CHIPS, 0, 0, tiled=True)
     payload, own_new, other_new, key = pl.pallas_call(
         adam_kernel,
         in_specs=[vmem] * 3,
         out_specs=[vmem] * 4,
         out_shape=[
-            shape((64, 16, 1152), BF),
+            shape((64, 16, 384), BF),
             shape((8, HALF), F32),
             shape((8, HALF), F32),
             shape((1, 256), jnp.int32),
@@ -326,28 +397,45 @@
     )(partial, old, new_owner.reshape(1, 64))
     other_new = swapped(other_new)
     blocks = lax.all_to_all(payload, CHIPS, 0, 0, tiled=True)
-    other_blocks = swapped(blocks)
+    halves = pl.pallas_call(
+        halve_kernel,
+        in_specs=[vmem],
+        out_specs=[vmem] * 6,
+        out_shape=[piece] * 6,
+        compiler_params=params(),
+        name="halve",
+    )(blocks)
+    pieces = [blocks] + to_neighbours(halves)
+    joined = pl.pallas_call(
+        join_kernel,
+        in_specs=[vmem] * 7,
+        out_specs=vmem,
+        out_shape=shape((64, 16, 1152), BF),
+        compiler_params=params(),
+        name="join",
+    )(*pieces)
+    other_joined = swapped(joined)
     scratch = [pltpu.VMEM((256, HALF), BF), pltpu.SemaphoreType.DMA((8,))]
     weights, adopted = pl.pallas_call(
         place_own_kernel,
-        in_specs=[vmem, vmem],
+        in_specs=[vmem] * 8,
         out_specs=[hbm, vmem],
         out_shape=[shape((256, 8192), BF), shape((3, 2, HALF), F32)],
         scratch_shapes=scratch,
         compiler_params=params(),
         cost_estimate=pl.CostEstimate(flops=8_000_000, bytes_accessed=8_000_000, transcendentals=0),
         name="place_own",
-    )(blocks, key)
+    )(*pieces, key)
     weights, adopted, kept = pl.pallas_call(
         place_other_kernel,
-        in_specs=[vmem, vmem, hbm, vmem, vmem, vmem],
+        in_specs=[vmem] * 2 + [hbm] + [vmem] * 3,
         out_specs=[hbm, vmem, vmem],
         out_shape=[shape((256, 8192), BF), shape((3, 2, 8192), F32), shape((3, 2, 8192), F32)],
         scratch_shapes=scratch,
         input_output_aliases={2: 0},
         compiler_params=params(),
         name="place_other",
-    )(other_blocks, key, weights, adopted, own_new, other_new)
+    )(other_joined, key, weights, adopted, own_new, other_new)
     return (weights, kept.transpose(1, 0, 2), adopted.transpose(1, 0, 2)[None, None])
 
 

time: 105 us -> 95.4 us (0.909)
  blocking collectives: 80.2 us -> 39.1 us
  starting transfers between devices: 6.37 us -> 29.4 us
  waiting for transfers between devices: 8.71 us -> 16.7 us
    all_to_all x1, blocking collectives: 42.8 us -> 22.3 us  [body(): partial = lax.all_to_all(partial, CHIPS, 0, 0, tiled=True)]
    all_to_all x1, blocking collectives: 37.3 us -> 16.8 us  [body(): blocks = lax.all_to_all(payload, CHIPS, 0, 0, tiled=True)]
    ppermute x0 -> x12, starting transfers between devices: none -> 18 us  [to_neighbours(): lax.ppermute(value, axis, [(p, (p + shift) % 4) for p in range(4)])]
    ppermute x0 -> x12, waiting for transfers between devices: none -> 9.11 us  [to_neighbours(): lax.ppermute(value, axis, [(p, (p + shift) % 4) for p in range(4)])]
    ppermute x4, starting transfers between devices: 4.42 us -> 9.43 us  [swapped(): return lax.ppermute(value, 'core', [(0, 1), (1, 0)])]
    ppermute x4, waiting for transfers between devices: 3.89 us -> 2.81 us  [swapped(): return lax.ppermute(value, 'core', [(0, 1), (1, 0)])]
    pallas_call x4 -> x6, Pallas kernels: 4.69 us -> 5.62 us  [the longest x1 2.22 us: body(): pl.pallas_call(place_other_kernel, in_specs=[vmem] * 2 + [hbm] + [vmem] *...]
  transfers between devices with their start and end apart: 6 -> 18, of which waited for: 3 -> 9; matrix products, arithmetic and copies ran while one was open for 0% -> 0% of each run, Pallas kernels for 1% -> 2%
where the time goes in v3:
time: 95.4 us; the launch traced here: 95.1 us
  blocking collectives  39.1 us (41%)
  starting transfers between devices  29.4 us (31%)
  waiting for transfers between devices  16.7 us (18%)
  Pallas kernels  6.41 us (7%)
  local copies, waits for them, and re-layouts  2.78 us (3%)
    all_to_all x1, blocking collectives, body(): partial = lax.all_to_all(partial, CHIPS, 0, 0, tiled=True)  22.3 us
    ppermute x12, starting transfers between devices, to_neighbours(): lax.ppermute(value, axis, [(p, (p + shift) % 4) for p in range(4)])  18 us
    all_to_all x1, blocking collectives, body(): blocks = lax.all_to_all(payload, CHIPS, 0, 0, tiled=True)  16.8 us
    ppermute x4, starting transfers between devices, swapped(): return lax.ppermute(value, 'core', [(0, 1), (1, 0)])  9.43 us
    ppermute x12, waiting for transfers between devices, to_neighbours(): lax.ppermute(value, axis, [(p, (p + shift) % 4) for p in range(4)])  9.11 us
    ppermute x2, waiting for transfers between devices, from_leaving(): lax.ppermute(value, ('y', 'z', 'x', 'core'), [(96 + rank, 32 * group + ra...  4.81 us
    ppermute x4, waiting for transfers between devices, swapped(): return lax.ppermute(value, 'core', [(0, 1), (1, 0)])  2.81 us
    dynamic_slice x1, local copies, waits for them, and re-layouts, body(): got = swapped(lax.dynamic_slice(grads, (0, (1 - core) * HALF), (256, HALF)))  2.76 us
  transfers between devices with their start and end apart: 18, of which 9 were waited for; matrix products, arithmetic and copies ran while one was open for 0% of the time, Pallas kernels for 2%

profile of v3, /device:TPU:1, one launch (start us, length us, event | category | flops | bytes accessed | tf_op | source)
XLA Modules:
  0.0 95.1 jit_solution(16539865644471977715)
XLA Ops:
  0.7 2.8 %dynamic-slice_bitcast_fusion = (bf16[256,4096]{1,0:T(8,128)(2,1)S(1)}, bf16[256,4096]{1,0:T(8,128)(2,1)S(1)}) fusion(bf16[1,1,256,8192]{3,2,1,0:T(8,128)(2,1)} %param.5, s32[]{:T(128)S(6)} %select_n.7, s32[]{:T(128)S(6)} %select_n.6), kind=kLoop, calls=%fused_computation | loop fusion | bytes 8388616 | tf_op jit(solution)/shard_map/dynamic_slice | solution.py:358
  3.4 1.5 %collective-permute-start = (bf16[256,4096]{1,0:T(8,128)(2,1)S(1)}, bf16[256,4096]{1,0:T(8,128)(2,1)S(1)}, u32[]{:S(2)}, u32[]{:S(2)}) collective-permute-start(bf16[256,4096]{1,0:T(8,128)(2,1)S(1)} %get-tuple-element.53), channel_id=1, source_target_pairs={{0,1},{1,0},{2,3},{3,2},{4,5},{5,4},{6,7},{7,6},{8,9},{9,8},{10,11... | collective-permute-start | bytes 6291464 | tf_op jit(solution)/shard_map/ppermute | solution.py:338
  4.9 1.3 %collective-permute-start.1 = (f32[2,8192]{1,0:T(2,128)S(1)}, f32[2,8192]{1,0:T(2,128)S(1)}, u32[]{:S(2)}, u32[]{:S(2)}) collective-permute-start(f32[2,8192]{1,0:T(2,128)S(1)} %copy-done), channel_id=1, source_target_pairs={{96,0},{97,1},{98,2},{99,3},{100,4},{101,5},{102,6},{103,7},{104,8... | collective-permute-start | bytes 196616 | tf_op jit(solution)/shard_map/ppermute | solution.py:350
  6.9 4.8 %collective-permute-done.1.low_ref = f32[2,8192]{1,0:T(2,128)S(1)} collective-permute-done((f32[2,8192]{1,0:T(2,128)S(1)}, f32[2,8192]{1,0:T(2,128)S(1)}, u32[]{:S(2)}, u32[]{:S(2)}) %collective-permute-start.1) | collective-permute-done | bytes 65568 | tf_op jit(solution)/shard_map/ppermute | solution.py:350
  11.7 1.2 %add_blocks.1 = (bf16[64,16,256]{2,1,0:T(8,128)(2,1)S(1)}, bf16[32,16,256]{2,1,0:T(8,128)(2,1)S(1)}, bf16[32,16,256]{2,1,0:T(8,128)(2,1)S(1)}, bf16[32,16,256]{2...) custom-call(bf16[256,4096]{1,0:T(8,128)(2,1)S(1)} %get-tuple-element, ...), custom_call_target="tpu_custom_call" | custom-call | tf_op jit(solution)/shard_map/add_blocks/pallas_call | solution.py:362
  13.0 1.4 %collective-permute-start.3 = (bf16[32,16,256]{2,1,0:T(8,128)(2,1)S(1)}, bf16[32,16,256]{2,1,0:T(8,128)(2,1)S(1)}, u32[]{:S(2)}, u32[]{:S(2)}) collective-permute-start(bf16[32,16,256]{2,1,0:T(8,128)(2,1)S(1)} %get-tuple-element.29), channel_id=1, source_target_pairs={{0,2},{2,4},{4,6},{6,0},{1,3},{3,5},{5,7},{7,1},{8,10},{10,12},{12... | collective-permute-start | bytes 786440 | tf_op jit(solution)/shard_map/ppermute | solution.py:345
  14.3 1.1 %collective-permute-start.9 = (f32[8,4096]{1,0:T(8,128)S(1)}, f32[8,4096]{1,0:T(8,128)S(1)}, u32[]{:S(2)}, u32[]{:S(2)}) collective-permute-start(f32[8,4096]{1,0:T(8,128)S(1)} %get-tuple-element.35), channel_id=1, source_target_pairs={{0,1},{1,0},{2,3},{3,2},{4,5},{5,4},{6,7},{7,6},{8,9},{9,8},{10,11... | collective-permute-start | bytes 393224 | tf_op jit(solution)/shard_map/ppermute | solution.py:338
  15.4 1.4 %collective-permute-start.4 = (bf16[32,16,256]{2,1,0:T(8,128)(2,1)S(1)}, bf16[32,16,256]{2,1,0:T(8,128)(2,1)S(1)}, u32[]{:S(2)}, u32[]{:S(2)}) collective-permute-start(bf16[32,16,256]{2,1,0:T(8,128)(2,1)S(1)} %get-tuple-element.30), channel_id=1, source_target_pairs={{0,6},{2,0},{4,2},{6,4},{1,7},{3,1},{5,3},{7,5},{8,14},{10,8},{12,... | collective-permute-start | bytes 786440 | tf_op jit(solution)/shard_map/ppermute | solution.py:345
  16.8 2.3 %collective-permute-start.5 = (bf16[32,16,256]{2,1,0:T(8,128)(2,1)S(1)}, bf16[32,16,256]{2,1,0:T(8,128)(2,1)S(1)}, u32[]{:S(2)}, u32[]{:S(2)}) collective-permute-start(bf16[32,16,256]{2,1,0:T(8,128)(2,1)S(1)} %get-tuple-element.31), channel_id=1, source_target_pairs={{0,32},{32,64},{64,96},{96,0},{1,33},{33,65},{65,97},{97,1},{2,34}... | collective-permute-start | bytes 786440 | tf_op jit(solution)/shard_map/ppermute | solution.py:345
  19.5 1.7 %collective-permute-start.7 = (bf16[32,16,256]{2,1,0:T(8,128)(2,1)S(1)}, bf16[32,16,256]{2,1,0:T(8,128)(2,1)S(1)}, u32[]{:S(2)}, u32[]{:S(2)}) collective-permute-start(bf16[32,16,256]{2,1,0:T(8,128)(2,1)S(1)} %get-tuple-element.33), channel_id=1, source_target_pairs={{0,8},{8,16},{16,24},{24,0},{1,9},{9,17},{17,25},{25,1},{2,10},{10... | collective-permute-start | bytes 786440 | tf_op jit(solution)/shard_map/ppermute | solution.py:345
  21.2 3.8 %collective-permute-start.8 = (bf16[32,16,256]{2,1,0:T(8,128)(2,1)S(1)}, bf16[32,16,256]{2,1,0:T(8,128)(2,1)S(1)}, u32[]{:S(2)}, u32[]{:S(2)}) collective-permute-start(bf16[32,16,256]{2,1,0:T(8,128)(2,1)S(1)} %get-tuple-element.34), channel_id=1, source_target_pairs={{0,24},{8,0},{16,8},{24,16},{1,25},{9,1},{17,9},{25,17},{2,26},{10... | collective-permute-start | bytes 786440 | tf_op jit(solution)/shard_map/ppermute | solution.py:345
  26.4 2.7 %collective-permute-done.7.z_up = bf16[32,16,256]{2,1,0:T(8,128)(2,1)S(1)} collective-permute-done((bf16[32,16,256]{2,1,0:T(8,128)(2,1)S(1)}, bf16[32,16,256]{2,1,0:T(8,128)(2,1)S(1)}, u32[]{:S(2)}, u32[]{:S(2)}) %collective-permute-start.7) | collective-permute-done | bytes 262176 | tf_op jit(solution)/shard_map/ppermute | solution.py:345
  29.6 22.3 %all_to_all.10.parts_ref = bf16[64,16,384]{2,1,0:T(8,128)(2,1)S(1)} all-to-all(bf16[64,16,384]{2,1,0:T(8,128)(2,1)S(1)} %get-tuple-element.36), channel_id=1, replica_groups=mesh['y'=4,'z'=4,'x'=4,'core'=2] {'y','z','x'}, dimensions={0} | all-to-all | bytes 1572864 | tf_op jit(solution)/shard_map/all_to_all | solution.py:383
  52.7 16.8 %all_to_all.11.blocks_ref.refs_0_ = bf16[64,16,384]{2,1,0:T(8,128)(2,1)S(1)} all-to-all(bf16[64,16,384]{2,1,0:T(8,128)(2,1)S(1)} %get-tuple-element.38), channel_id=1, replica_groups=mesh['y'=4,'z'=4,'x'=4,'core'=2] {'y','z','x'}, dimensions={0} | all-to-all | bytes 1572864 | tf_op jit(solution)/shard_map/all_to_all | solution.py:399
  69.8 2.6 %collective-permute-start.11 = (bf16[32,16,256]{2,1,0:T(8,128)(2,1)S(1)}, bf16[32,16,256]{2,1,0:T(8,128)(2,1)S(1)}, u32[]{:S(2)}, u32[]{:S(2)}) collective-permute-start(bf16[32,16,256]{2,1,0:T(8,128)(2,1)S(1)} %get-tuple-element.40), channel_id=1, source_target_pairs={{0,6},{2,0},{4,2},{6,4},{1,7},{3,1},{5,3},{7,5},{8,14},{10,8},{12,... | collective-permute-start | bytes 786440 | tf_op jit(solution)/shard_map/ppermute | solution.py:345
  72.4 2.6 %collective-permute-start.13 = (bf16[32,16,256]{2,1,0:T(8,128)(2,1)S(1)}, bf16[32,16,256]{2,1,0:T(8,128)(2,1)S(1)}, u32[]{:S(2)}, u32[]{:S(2)}) collective-permute-start(bf16[32,16,256]{2,1,0:T(8,128)(2,1)S(1)} %get-tuple-element.42), channel_id=1, source_target_pairs={{0,96},{32,0},{64,32},{96,64},{1,97},{33,1},{65,33},{97,65},{2,98}... | collective-permute-start | bytes 786440 | tf_op jit(solution)/shard_map/ppermute | solution.py:345
  75.1 1.1 %collective-permute-done.10.x_up.refs_1_ = bf16[32,16,256]{2,1,0:T(8,128)(2,1)S(1)} collective-permute-done((bf16[32,16,256]{2,1,0:T(8,128)(2,1)S(1)}, bf16[32,16,256]{2,1,0:T(8,128)(2,1)S(1)}, u32[]{:S(2)}, u32[]{:S(2)}) %collective-permute-start.10) | collective-permute-done | bytes 262176 | tf_op jit(solution)/shard_map/ppermute | solution.py:345
  76.1 1.6 %collective-permute-start.15 = (bf16[32,16,256]{2,1,0:T(8,128)(2,1)S(1)}, bf16[32,16,256]{2,1,0:T(8,128)(2,1)S(1)}, u32[]{:S(2)}, u32[]{:S(2)}) collective-permute-start(bf16[32,16,256]{2,1,0:T(8,128)(2,1)S(1)} %get-tuple-element.44), channel_id=1, source_target_pairs={{0,24},{8,0},{16,8},{24,16},{1,25},{9,1},{17,9},{25,17},{2,26},{10... | collective-permute-start | bytes 786440 | tf_op jit(solution)/shard_map/ppermute | solution.py:345
  77.8 1.4 %collective-permute-done.12.y_up.refs_3_ = bf16[32,16,256]{2,1,0:T(8,128)(2,1)S(1)} collective-permute-done((bf16[32,16,256]{2,1,0:T(8,128)(2,1)S(1)}, bf16[32,16,256]{2,1,0:T(8,128)(2,1)S(1)}, u32[]{:S(2)}, u32[]{:S(2)}) %collective-permute-start.12) | collective-permute-done | bytes 262176 | tf_op jit(solution)/shard_map/ppermute | solution.py:345
  79.1 2.4 %collective-permute-done.14.z_up.refs_5_ = bf16[32,16,256]{2,1,0:T(8,128)(2,1)S(1)} collective-permute-done((bf16[32,16,256]{2,1,0:T(8,128)(2,1)S(1)}, bf16[32,16,256]{2,1,0:T(8,128)(2,1)S(1)}, u32[]{:S(2)}, u32[]{:S(2)}) %collective-permute-start.14) | collective-permute-done | bytes 262176 | tf_op jit(solution)/shard_map/ppermute | solution.py:345
  81.8 6.7 %collective-permute-start.16 = (bf16[64,16,1152]{2,1,0:T(8,128)(2,1)S(1)}, bf16[64,16,1152]{2,1,0:T(8,128)(2,1)S(1)}, u32[]{:S(2)}, u32[]{:S(2)}) collective-permute-start(bf16[64,16,1152]{2,1,0:T(8,128)(2,1)S(1)} %join.1), channel_id=1, source_target_pairs={{0,1},{1,0},{2,3},{3,2},{4,5},{5,4},{6,7},{7,6},{8,9},{9,8},{10,11... | collective-permute-start | bytes 7077896 | tf_op jit(solution)/shard_map/ppermute | solution.py:338
  88.7 1.4 %place_own.1 = (bf16[256,8192]{1,0:T(8,128)(2,1)}, f32[3,2,4096]{2,1,0:T(2,128)S(1)}) custom-call(bf16[64,16,384]{2,1,0:T(8,128)(2,1)S(1)} %all_to_all.11.blocks_ref.refs_0_, bf16[32,16,256]{2,1,0:T(8,128)(2,1)S(1)} %collective-permute-done.10.x_up.refs_1_, bf16[32,16,256]{2,1,0:T(8,128)(2,1)S(1)} %collective-permute-done.11.x_down.refs_2_, ...), custom_call_target="tpu_custom_call" | custom-call | flops 8000000 | bytes 8000000 | tf_op jit(solution)/shard_map/place_own/pallas_call | solution.py:419
  90.1 2.8 %collective-permute-done.17.refs_5_ = f32[8,4096]{1,0:T(8,128)S(1)} collective-permute-done((f32[8,4096]{1,0:T(8,128)S(1)}, f32[8,4096]{1,0:T(8,128)S(1)}, u32[]{:S(2)}, u32[]{:S(2)}) %collective-permute-start.17) | collective-permute-done | bytes 131104 | tf_op jit(solution)/shard_map/ppermute | solution.py:338
  92.9 2.2 %place_other.1 = (bf16[256,8192]{1,0:T(8,128)(2,1)}, f32[3,2,8192]{2,1,0:T(2,128)}, f32[3,2,8192]{2,1,0:T(2,128)}) custom-call(bf16[64,16,1152]{2,1,0:T(8,128)(2,1)S(1)} %collective-permute-done.16.refs_0_, s32[1,256]{1,0:T(1,128)S(1)} %get-tuple-element.45.refs_7_.refs_1_, ...), custom_call_target="tpu_custom_call", output_to_operand_aliasing={{0}: (2, {})} | custom-call | tf_op jit(solution)/shard_map/place_other/pallas_call | solution.py:429
  (30 shorter events, 4.4 us)
Async XLA Ops:
  0.6 4.3 %copy-start = (f32[2,8192]{1,0:T(2,128)S(1)}, f32[2,8192]{1,0:T(2,128)}, u32[]{:S(2)}) copy-start(f32[2,8192]{1,0:T(2,128)} %master_ref.3) | copy-start | bytes 196612
  0.6 5.6 %copy-start.1 = (f32[2,8192]{1,0:T(2,128)S(1)}, f32[2,8192]{1,0:T(2,128)}, u32[]{:S(2)}) copy-start(f32[2,8192]{1,0:T(2,128)} %first_ref.3) | copy-start | bytes 196612
  0.7 11.1 %copy-start.2 = (f32[2,8192]{1,0:T(2,128)S(1)}, f32[2,8192]{1,0:T(2,128)}, u32[]{:S(2)}) copy-start(f32[2,8192]{1,0:T(2,128)} %second_ref.3) | copy-start | bytes 196612
  3.4 8.3 %collective-permute-start = (bf16[256,4096]{1,0:T(8,128)(2,1)S(1)}, bf16[256,4096]{1,0:T(8,128)(2,1)S(1)}, u32[]{:S(2)}, u32[]{:S(2)}) collective-permute-start(bf16[256,4096]{1,0:T(8,128)(2,1)S(1)} %get-tuple-element.53), channel_id=1, source_target_pairs={{0,1},{1,0},{2,3},{3,2},{4,5},{5,4},{6,7},{7,6},{8,9},{9,8},{10,11... | collective-permute-start | bytes 6291464 | tf_op jit(solution)/shard_map/ppermute | solution.py:338
  4.9 6.8 %collective-permute-start.1 = (f32[2,8192]{1,0:T(2,128)S(1)}, f32[2,8192]{1,0:T(2,128)S(1)}, u32[]{:S(2)}, u32[]{:S(2)}) collective-permute-start(f32[2,8192]{1,0:T(2,128)S(1)} %copy-done), channel_id=1, source_target_pairs={{96,0},{97,1},{98,2},{99,3},{100,4},{101,5},{102,6},{103,7},{104,8... | collective-permute-start | bytes 196616 | tf_op jit(solution)/shard_map/ppermute | solution.py:350
  6.2 5.5 %collective-permute-start.2 = (f32[2,8192]{1,0:T(2,128)S(1)}, f32[2,8192]{1,0:T(2,128)S(1)}, u32[]{:S(2)}, u32[]{:S(2)}) collective-permute-start(f32[2,8192]{1,0:T(2,128)S(1)} %copy-done.1), channel_id=1, source_target_pairs={{96,32},{97,33},{98,34},{99,35},{100,36},{101,37},{102,38},{103,39... | collective-permute-start | bytes 196616 | tf_op jit(solution)/shard_map/ppermute | solution.py:350
  12.9 39.0 %copy-start.3 = (s32[64]{0:T(128)S(1)}, s32[64]{0:T(128)}, u32[]{:S(2)}) copy-start(s32[64]{0:T(128)} %param.9) | copy-start | bytes 772
  13.0 8.3 %collective-permute-start.3 = (bf16[32,16,256]{2,1,0:T(8,128)(2,1)S(1)}, bf16[32,16,256]{2,1,0:T(8,128)(2,1)S(1)}, u32[]{:S(2)}, u32[]{:S(2)}) collective-permute-start(bf16[32,16,256]{2,1,0:T(8,128)(2,1)S(1)} %get-tuple-element.29), channel_id=1, source_target_pairs={{0,2},{2,4},{4,6},{6,0},{1,3},{3,5},{5,7},{7,1},{8,10},{10,12},{12... | collective-permute-start | bytes 786440 | tf_op jit(solution)/shard_map/ppermute | solution.py:345
  14.3 5.2 %collective-permute-start.9 = (f32[8,4096]{1,0:T(8,128)S(1)}, f32[8,4096]{1,0:T(8,128)S(1)}, u32[]{:S(2)}, u32[]{:S(2)}) collective-permute-start(f32[8,4096]{1,0:T(8,128)S(1)} %get-tuple-element.35), channel_id=1, source_target_pairs={{0,1},{1,0},{2,3},{3,2},{4,5},{5,4},{6,7},{7,6},{8,9},{9,8},{10,11... | collective-permute-start | bytes 393224 | tf_op jit(solution)/shard_map/ppermute | solution.py:338
  15.4 9.7 %collective-permute-start.4 = (bf16[32,16,256]{2,1,0:T(8,128)(2,1)S(1)}, bf16[32,16,256]{2,1,0:T(8,128)(2,1)S(1)}, u32[]{:S(2)}, u32[]{:S(2)}) collective-permute-start(bf16[32,16,256]{2,1,0:T(8,128)(2,1)S(1)} %get-tuple-element.30), channel_id=1, source_target_pairs={{0,6},{2,0},{4,2},{6,4},{1,7},{3,1},{5,3},{7,5},{8,14},{10,8},{12,... | collective-permute-start | bytes 786440 | tf_op jit(solution)/shard_map/ppermute | solution.py:345
  16.8 8.8 %collective-permute-start.5 = (bf16[32,16,256]{2,1,0:T(8,128)(2,1)S(1)}, bf16[32,16,256]{2,1,0:T(8,128)(2,1)S(1)}, u32[]{:S(2)}, u32[]{:S(2)}) collective-permute-start(bf16[32,16,256]{2,1,0:T(8,128)(2,1)S(1)} %get-tuple-element.31), channel_id=1, source_target_pairs={{0,32},{32,64},{64,96},{96,0},{1,33},{33,65},{65,97},{97,1},{2,34}... | collective-permute-start | bytes 786440 | tf_op jit(solution)/shard_map/ppermute | solution.py:345
  19.1 7.3 %collective-permute-start.6 = (bf16[32,16,256]{2,1,0:T(8,128)(2,1)S(1)}, bf16[32,16,256]{2,1,0:T(8,128)(2,1)S(1)}, u32[]{:S(2)}, u32[]{:S(2)}) collective-permute-start(bf16[32,16,256]{2,1,0:T(8,128)(2,1)S(1)} %get-tuple-element.32), channel_id=1, source_target_pairs={{0,96},{32,0},{64,32},{96,64},{1,97},{33,1},{65,33},{97,65},{2,98}... | collective-permute-start | bytes 786440 | tf_op jit(solution)/shard_map/ppermute | solution.py:345
  19.5 9.7 %collective-permute-start.7 = (bf16[32,16,256]{2,1,0:T(8,128)(2,1)S(1)}, bf16[32,16,256]{2,1,0:T(8,128)(2,1)S(1)}, u32[]{:S(2)}, u32[]{:S(2)}) collective-permute-start(bf16[32,16,256]{2,1,0:T(8,128)(2,1)S(1)} %get-tuple-element.33), channel_id=1, source_target_pairs={{0,8},{8,16},{16,24},{24,0},{1,9},{9,17},{17,25},{25,1},{2,10},{10... | collective-permute-start | bytes 786440 | tf_op jit(solution)/shard_map/ppermute | solution.py:345
  21.2 7.9 %collective-permute-start.8 = (bf16[32,16,256]{2,1,0:T(8,128)(2,1)S(1)}, bf16[32,16,256]{2,1,0:T(8,128)(2,1)S(1)}, u32[]{:S(2)}, u32[]{:S(2)}) collective-permute-start(bf16[32,16,256]{2,1,0:T(8,128)(2,1)S(1)} %get-tuple-element.34), channel_id=1, source_target_pairs={{0,24},{8,0},{16,8},{24,16},{1,25},{9,1},{17,9},{25,17},{2,26},{10... | collective-permute-start | bytes 786440 | tf_op jit(solution)/shard_map/ppermute | solution.py:345
  69.6 6.5 %collective-permute-start.10 = (bf16[32,16,256]{2,1,0:T(8,128)(2,1)S(1)}, bf16[32,16,256]{2,1,0:T(8,128)(2,1)S(1)}, u32[]{:S(2)}, u32[]{:S(2)}) collective-permute-start(bf16[32,16,256]{2,1,0:T(8,128)(2,1)S(1)} %get-tuple-element.39), channel_id=1, source_target_pairs={{0,2},{2,4},{4,6},{6,0},{1,3},{3,5},{5,7},{7,1},{8,10},{10,12},{12... | collective-permute-start | bytes 786440 | tf_op jit(solution)/shard_map/ppermute | solution.py:345
  69.8 8.0 %collective-permute-start.11 = (bf16[32,16,256]{2,1,0:T(8,128)(2,1)S(1)}, bf16[32,16,256]{2,1,0:T(8,128)(2,1)S(1)}, u32[]{:S(2)}, u32[]{:S(2)}) collective-permute-start(bf16[32,16,256]{2,1,0:T(8,128)(2,1)S(1)} %get-tuple-element.40), channel_id=1, source_target_pairs={{0,6},{2,0},{4,2},{6,4},{1,7},{3,1},{5,3},{7,5},{8,14},{10,8},{12,... | collective-permute-start | bytes 786440 | tf_op jit(solution)/shard_map/ppermute | solution.py:345
  72.4 6.7 %collective-permute-start.12 = (bf16[32,16,256]{2,1,0:T(8,128)(2,1)S(1)}, bf16[32,16,256]{2,1,0:T(8,128)(2,1)S(1)}, u32[]{:S(2)}, u32[]{:S(2)}) collective-permute-start(bf16[32,16,256]{2,1,0:T(8,128)(2,1)S(1)} %get-tuple-element.41), channel_id=1, source_target_pairs={{0,32},{32,64},{64,96},{96,0},{1,33},{33,65},{65,97},{97,1},{2,34}... | collective-permute-start | bytes 786440 | tf_op jit(solution)/shard_map/ppermute | solution.py:345
  72.4 6.7 %collective-permute-start.13 = (bf16[32,16,256]{2,1,0:T(8,128)(2,1)S(1)}, bf16[32,16,256]{2,1,0:T(8,128)(2,1)S(1)}, u32[]{:S(2)}, u32[]{:S(2)}) collective-permute-start(bf16[32,16,256]{2,1,0:T(8,128)(2,1)S(1)} %get-tuple-element.42), channel_id=1, source_target_pairs={{0,96},{32,0},{64,32},{96,64},{1,97},{33,1},{65,33},{97,65},{2,98}... | collective-permute-start | bytes 786440 | tf_op jit(solution)/shard_map/ppermute | solution.py:345
  75.1 6.4 %collective-permute-start.14 = (bf16[32,16,256]{2,1,0:T(8,128)(2,1)S(1)}, bf16[32,16,256]{2,1,0:T(8,128)(2,1)S(1)}, u32[]{:S(2)}, u32[]{:S(2)}) collective-permute-start(bf16[32,16,256]{2,1,0:T(8,128)(2,1)S(1)} %get-tuple-element.43), channel_id=1, source_target_pairs={{0,8},{8,16},{16,24},{24,0},{1,9},{9,17},{17,25},{25,1},{2,10},{10... | collective-permute-start | bytes 786440 | tf_op jit(solution)/shard_map/ppermute | solution.py:345
  76.1 5.5 %collective-permute-start.15 = (bf16[32,16,256]{2,1,0:T(8,128)(2,1)S(1)}, bf16[32,16,256]{2,1,0:T(8,128)(2,1)S(1)}, u32[]{:S(2)}, u32[]{:S(2)}) collective-permute-start(bf16[32,16,256]{2,1,0:T(8,128)(2,1)S(1)} %get-tuple-element.44), channel_id=1, source_target_pairs={{0,24},{8,0},{16,8},{24,16},{1,25},{9,1},{17,9},{25,17},{2,26},{10... | collective-permute-start | bytes 786440 | tf_op jit(solution)/shard_map/ppermute | solution.py:345
  81.8 11.1 %collective-permute-start.16 = (bf16[64,16,1152]{2,1,0:T(8,128)(2,1)S(1)}, bf16[64,16,1152]{2,1,0:T(8,128)(2,1)S(1)}, u32[]{:S(2)}, u32[]{:S(2)}) collective-permute-start(bf16[64,16,1152]{2,1,0:T(8,128)(2,1)S(1)} %join.1), channel_id=1, source_target_pairs={{0,1},{1,0},{2,3},{3,2},{4,5},{5,4},{6,7},{7,6},{8,9},{9,8},{10,11... | collective-permute-start | bytes 7077896 | tf_op jit(solution)/shard_map/ppermute | solution.py:338
  88.6 4.3 %collective-permute-start.17 = (f32[8,4096]{1,0:T(8,128)S(1)}, f32[8,4096]{1,0:T(8,128)S(1)}, u32[]{:S(2)}, u32[]{:S(2)}) collective-permute-start(f32[8,4096]{1,0:T(8,128)S(1)} %get-tuple-element.49), channel_id=1, source_target_pairs={{0,1},{1,0},{2,3},{3,2},{4,5},{5,4},{6,7},{7,6},{8,9},{9,8},{10,11... | collective-permute-start | bytes 393224 | tf_op jit(solution)/shard_map/ppermute | solution.py:338

commit v4 on v3

--- a/solution.py
+++ b/solution.py
@@ -55,35 +55,39 @@
     return jnp.where(y == 0, low_ref[...], jnp.where(y == 1, middle_ref[...], second_ref[...]))
 
 
-def chip_class(chip):
-    return (chip & 1) ^ (((chip >> 4) & 1) * 2) ^ (((chip >> 2) & 1) * 3)
-
-
-def own_chip():
-    return (lax.axis_index("y") * 4 + lax.axis_index("z")) * 4 + lax.axis_index("x")
-
-
-def quarter(number):
-    return pl.ds(pl.multiple_of(number * 256, 256), 256)
-
-
-def add_kernel(
-    own_ref, got_ref, master_ref, first_ref, second_ref, low_ref, middle_ref,
-    keep_ref, x_up, x_down, y_up, y_down, z_up, z_down, pair_ref, blocks_ref, rows_ref,
-):
+def pair_kernel(master_ref, first_ref, second_ref, low_ref, middle_ref, pair_ref, rows_ref):
     other = columns(1 - lax.axis_index("core"))
     for i, ref in enumerate((master_ref, first_ref, second_ref)):
         pair_ref[2 * i : 2 * i + 2, :] = ref[:, other]
     rows_ref[...] = spread_rows(low_ref, middle_ref, second_ref)
     pair_ref[6:8, :] = rows_ref[:, other]
+
+
+def chip_class(chip):
+    return (chip & 1) ^ (((chip >> 4) & 1) * 2) ^ (((chip >> 2) & 1) * 3)
+
+
+def own_chip():
+    return (lax.axis_index("y") * 4 + lax.axis_index("z")) * 4 + lax.axis_index("x")
+
+
+def quarter(number):
+    return pl.ds(pl.multiple_of(number * 256, 256), 256)
+
+
+def add_kernel(
+    grads_ref, got_ref, low_ref, middle_ref, keep_ref, x_ref, y_ref, z_ref, blocks_ref
+):
+    core = lax.axis_index("core")
     low = iota((8, 1024), 0) < 4
 
     def kept(i, carry):
         rows = pl.ds(pl.multiple_of(16 * i, 16), 16)
         parts = []
         for k in range(4):
-            cut = slice(k * 1024, (k + 1) * 1024)
-            parts.append(own_ref[rows, cut].astype(F32) + got_ref[rows, cut].astype(F32))
+            cut = pl.ds(pl.multiple_of(core * HALF + k * 1024, 1024), 1024)
+            got = got_ref[rows, k * 1024 : (k + 1) * 1024]
+            parts.append(grads_ref[rows, cut].astype(F32) + got.astype(F32))
         for tile in range(2):
             c = [part[8 * tile : 8 * tile + 8] for part in parts]
             even = [jnp.where(low, c[k], turned(c[k + 1])) for k in (0, 2)]
@@ -96,36 +100,35 @@
 
     def leave(q, carry):
         cut = pl.ds(pl.multiple_of(q * 256, 256), 256)
+        own_cut = pl.ds(pl.multiple_of(core * HALF + q * 256, 256), 256)
         for a in range(4):
             rows = slice(192 + 16 * a, 208 + 16 * a)
-            total = own_ref[rows, cut].astype(F32) + got_ref[rows, cut].astype(F32)
+            total = grads_ref[rows, own_cut].astype(F32) + got_ref[rows, cut].astype(F32)
             blocks_ref[48 + q, :, a * 256 : (a + 1) * 256] = total.astype(BF)
         return carry
 
     lax.fori_loop(0, 16, leave, 0)
     kind = chip_class(own_chip())
     keep_ref[...] = blocks_ref[:, :, quarter(kind)]
-    for axis, (up, down) in enumerate(((x_up, x_down), (y_up, y_down), (z_up, z_down))):
-        up[...] = blocks_ref[0:32, :, quarter(kind ^ (axis + 1))]
-        down[...] = blocks_ref[32:64, :, quarter(kind ^ (axis + 1))]
+    for axis, ref in enumerate((x_ref, y_ref, z_ref)):
+        ref[...] = blocks_ref[:, :, quarter(kind ^ (axis + 1))]
 
 
 def merge_kernel(
-    keep_ref, x_up, x_down, y_up, y_down, z_up, z_down,
+    keep_ref, x_ref, y_ref, z_ref,
     master_ref, first_ref, second_ref, low_ref, middle_ref, pair_ref,
     out_ref, old_ref, rows_ref, split_ref,
 ):
     core = lax.axis_index("core")
 
     def add(d, carry):
-        for base, refs in ((0, (x_up, y_up, z_up)), (32, (x_down, y_down, z_down))):
-            total = keep_ref[base + d].astype(F32)
-            for ref in refs:
-                total = total + ref[d].astype(F32)
-            out_ref[base + d, :, 0:256] = total.astype(BF)
-        return carry
-
-    lax.fori_loop(0, 32, add, 0, unroll=8)
+        total = keep_ref[d].astype(F32)
+        for ref in (x_ref, y_ref, z_ref):
+            total = total + ref[d].astype(F32)
+        out_ref[d, :, 0:256] = total.astype(BF)
+        return carry
+
+    lax.fori_loop(0, 64, add, 0, unroll=8)
 
     rows_ref[...] = spread_rows(low_ref, middle_ref, second_ref)
     for mine in range(2):
@@ -226,20 +229,18 @@
     out_ref[:, :, 256:384] = pick(chosen, moments).astype(BF).reshape(64, 16, 128)
 
 
-def halve_kernel(blocks_ref, *out_refs):
-    for i, ref in enumerate(out_refs):
-        ref[...] = blocks_ref[32 * (i % 2) : 32 * (i % 2) + 32, :, 0:256]
-
-
-def join_kernel(blocks_ref, x_up, x_down, y_up, y_down, z_up, z_down, out_ref):
+def copy_kernel(blocks_ref, out_ref):
+    out_ref[...] = blocks_ref[:, :, 0:256]
+
+
+def join_kernel(blocks_ref, x_ref, y_ref, z_ref, out_ref):
     out_ref[:, :, 0:384] = blocks_ref[...]
-    for at, up, down in ((384, x_up, x_down), (640, y_up, y_down), (896, z_up, z_down)):
-        out_ref[0:32, :, at : at + 256] = up[...]
-        out_ref[32:64, :, at : at + 256] = down[...]
-
-
-def place_half(views, key_ref, weights_ref, adopted_ref, adopted_at, rows_ref, sems, core, side):
-    blocks_ref = views[0][0][0]
+    for at, ref in ((384, x_ref), (640, y_ref), (896, z_ref)):
+        out_ref[:, :, at : at + 256] = ref[...]
+
+
+def place_half(views, key_ref, weights_ref, adopted_ref, adopted_at, adopted_ready, rows_ref, sems, core, side):
+    blocks_ref = views[0][0]
     chip = own_chip()
     kind = chip_class(chip)
     low = iota((8, 256), 0) < 4
@@ -248,13 +249,13 @@
         rows = pl.ds(pl.multiple_of(32 * i, 32), 32)
         return pltpu.make_async_copy(rows_ref.at[rows, :], weights_ref.at[rows, columns(side)], sems.at[i])
 
-    def kept(last, i, carry):
+    def kept(i, carry):
         for axis in range(4):
-            ref, base, lane = views[axis][last]
+            ref, lane = views[axis]
             for g in range(2):
                 tiles = []
                 for tile in range(2):
-                    number = 8 * i + 4 * g + 2 * tile - base
+                    number = 8 * i + 4 * g + 2 * tile
                     even = ref[number, :, lane : lane + 256].astype(F32)
                     odd = ref[number + 1, :, lane : lane + 256].astype(F32)
                     cut = []
@@ -270,13 +271,11 @@
         store(i).start()
         return carry
 
-    lax.fori_loop(0, 4, lambda i, carry: kept(0, i, carry), 0)
-    lax.fori_loop(4, 6, lambda i, carry: kept(1, i, carry), 0)
     for axis in range(4):
-        ref, base, lane = views[axis][1]
+        ref, lane = views[axis]
         rows = pl.ds(pl.multiple_of(192 + 16 * (kind ^ axis), 16), 16)
         for q in range(16):
-            rows_ref[rows, q * 256 : (q + 1) * 256] = ref[48 + q - base, :, lane : lane + 256]
+            rows_ref[rows, q * 256 : (q + 1) * 256] = ref[48 + q, :, lane : lane + 256]
     for i in range(6, 8):
         store(i).start()
     k = iota((8, 64), 0)
@@ -293,37 +292,43 @@
                 adopted_ref[1 + i, :, adopted_at(q * 256 + h * 128, 128)] = found[
                     2 * i : 2 * i + 2, q * 128 : (q + 1) * 128
                 ]
+    adopted_ready()
+    lax.fori_loop(0, 6, kept, 0)
     for i in range(8):
         store(i).wait()
 
 
-def place_own_kernel(*refs):
-    blocks_ref, *pieces = refs[:7]
-    key_ref, weights_ref, adopted_ref, rows_ref, sems = refs[7:]
-    views = [[(blocks_ref, 0, 0)] * 2]
-    views += [[(pieces[2 * axis + last], 32 * last, 0) for last in range(2)] for axis in range(3)]
+def place_own_kernel(
+    blocks_ref, x_ref, y_ref, z_ref, key_ref, weights_ref, adopted_ref, rows_ref, sems
+):
+    views = [(ref, 0) for ref in (blocks_ref, x_ref, y_ref, z_ref)]
     core = lax.axis_index("core")
     place_half(
-        views, key_ref, weights_ref, adopted_ref, lambda start, size: slice(start, start + size),
+        views, key_ref, weights_ref, adopted_ref, lambda start, size: slice(start, start + size), lambda: None,
         rows_ref, sems, core, core,
     )
 
 
 def place_other_kernel(*refs):
     joined_ref, key_ref, _, half_ref, own_ref, other_ref = refs[:6]
-    weights_ref, adopted_ref, kept_ref, rows_ref, sems = refs[6:]
-    views = [[(joined_ref, 0, lane)] * 2 for lane in (0, 384, 640, 896)]
+    weights_ref, adopted_out, kept_out, adopted_ref, kept_ref, rows_ref, sems, out_sems = refs[6:]
+    views = [(joined_ref, lane) for lane in (0, 384, 640, 896)]
     core = lax.axis_index("core")
     side = 1 - core
-
-    def at(start, size):
-        return pl.ds(pl.multiple_of(side * HALF + start, 128), size)
-
-    place_half(views, key_ref, weights_ref, adopted_ref, at, rows_ref, sems, core, side)
+    kept_copy = pltpu.make_async_copy(kept_ref, kept_out, out_sems.at[0])
+    adopted_copy = pltpu.make_async_copy(adopted_ref, adopted_out, out_sems.at[1])
     for i in range(3):
         adopted_ref[i, :, columns(core)] = half_ref[i]
         kept_ref[i, :, columns(core)] = own_ref[2 * i : 2 * i + 2, :]
         kept_ref[i, :, columns(side)] = other_ref[2 * i : 2 * i + 2, :]
+    kept_copy.start()
+
+    def at(start, size):
+        return pl.ds(pl.multiple_of(side * HALF + start, 128), size)
+
+    place_half(views, key_ref, weights_ref, adopted_ref, at, adopted_copy.start, rows_ref, sems, core, side)
+    kept_copy.wait()
+    adopted_copy.wait()
 
 
 def params(mib=40):
@@ -338,12 +343,9 @@
     return lax.ppermute(value, "core", [(0, 1), (1, 0)])
 
 
-def to_neighbours(up_and_down):
-    got = []
-    for i, axis in enumerate(("x", "y", "z")):
-        for value, shift in zip(up_and_down[2 * i : 2 * i + 2], (1, 3)):
-            got.append(lax.ppermute(value, axis, [(p, (p + shift) % 4) for p in range(4)]))
-    return got
+def to_neighbours(values):
+    pairs = [(2 * p + c, 2 * ((p + 1 + 2 * c) % 4) + c) for p in range(4) for c in range(2)]
+    return [lax.ppermute(value, (axis, "core"), pairs) for axis, value in zip("xyz", values)]
 
 
 def from_leaving(value, group):
@@ -356,24 +358,31 @@
     hbm = pl.BlockSpec(memory_space=pltpu.HBM)
     core = lax.axis_index("core")
     got = swapped(lax.dynamic_slice(grads, (0, (1 - core) * HALF), (256, HALF)))
-    own = lax.dynamic_slice(grads, (0, core * HALF), (256, HALF))
     low, middle = from_leaving(master, 0), from_leaving(first, 1)
-    piece = shape((32, 16, 256), BF)
-    *to_send, pair = pl.pallas_call(
+    piece = shape((64, 16, 256), BF)
+    keep, *to_send = pl.pallas_call(
         add_kernel,
-        in_specs=[vmem] * 7,
-        out_specs=[vmem] * 8,
-        out_shape=[shape((64, 16, 256), BF)] + [piece] * 6 + [shape((8, HALF), F32)],
-        scratch_shapes=[pltpu.VMEM((64, 16, 1024), BF), pltpu.VMEM((2, 8192), F32)],
+        in_specs=[vmem] * 4,
+        out_specs=[vmem] * 4,
+        out_shape=[piece] * 4,
+        scratch_shapes=[pltpu.VMEM((64, 16, 1024), BF)],
         compiler_params=params(),
         name="add_blocks",
-    )(own, got, master, first, second, low, middle)
-    keep, *to_send = to_send
+    )(grads, got, low, middle)
+    pair = pl.pallas_call(
+        pair_kernel,
+        in_specs=[vmem] * 5,
+        out_specs=vmem,
+        out_shape=shape((8, HALF), F32),
+        scratch_shapes=[pltpu.VMEM((2, 8192), F32)],
+        compiler_params=params(),
+        name="pair",
+    )(master, first, second, low, middle)
     arrived = to_neighbours(to_send)
     pair = swapped(pair)
     partial, old = pl.pallas_call(
         merge_kernel,
-        in_specs=[vmem] * 13,
+        in_specs=[vmem] * 10,
         out_specs=[vmem] * 2,
         out_shape=[shape((64, 16, 384), BF), shape((16, HALF), F32)],
         scratch_shapes=[pltpu.VMEM((2, 8192), F32), pltpu.VMEM((8, HALF), F32)],
@@ -397,18 +406,18 @@
     )(partial, old, new_owner.reshape(1, 64))
     other_new = swapped(other_new)
     blocks = lax.all_to_all(payload, CHIPS, 0, 0, tiled=True)
-    halves = pl.pallas_call(
-        halve_kernel,
+    mine = pl.pallas_call(
+        copy_kernel,
         in_specs=[vmem],
-        out_specs=[vmem] * 6,
-        out_shape=[piece] * 6,
-        compiler_params=params(),
-        name="halve",
+        out_specs=vmem,
+        out_shape=piece,
+        compiler_params=params(),
+        name="mine",
     )(blocks)
-    pieces = [blocks] + to_neighbours(halves)
+    pieces = [blocks] + to_neighbours([mine] * 3)
     joined = pl.pallas_call(
         join_kernel,
-        in_specs=[vmem] * 7,
+        in_specs=[vmem] * 4,
         out_specs=vmem,
         out_shape=shape((64, 16, 1152), BF),
         compiler_params=params(),
@@ -418,7 +427,7 @@
     scratch = [pltpu.VMEM((256, HALF), BF), pltpu.SemaphoreType.DMA((8,))]
     weights, adopted = pl.pallas_call(
         place_own_kernel,
-        in_specs=[vmem] * 8,
+        in_specs=[vmem] * 5,
         out_specs=[hbm, vmem],
         out_shape=[shape((256, 8192), BF), shape((3, 2, HALF), F32)],
         scratch_shapes=scratch,
@@ -429,9 +438,9 @@
     weights, adopted, kept = pl.pallas_call(
         place_other_kernel,
         in_specs=[vmem] * 2 + [hbm] + [vmem] * 3,
-        out_specs=[hbm, vmem, vmem],
+        out_specs=[hbm] * 3,
         out_shape=[shape((256, 8192), BF), shape((3, 2, 8192), F32), shape((3, 2, 8192), F32)],
-        scratch_shapes=scratch,
+        scratch_shapes=[pltpu.VMEM((3, 2, 8192), F32)] * 2 + scratch + [pltpu.SemaphoreType.DMA((2,))],
         input_output_aliases={2: 0},
         compiler_params=params(),
         name="place_other",

time: 95.4 us -> 89.6 us (0.939)
  starting transfers between devices: 29.4 us -> 17.8 us
  waiting for transfers between devices: 16.7 us -> 21 us
  blocking collectives: 39.1 us -> 41.8 us
    ppermute x12 -> x6, starting transfers between devices: 18 us -> 9.22 us  [to_neighbours(): lax.ppermute(value, (axis, 'core'), pairs)]
    ppermute x4, starting transfers between devices: 9.43 us -> 6.61 us  [swapped(): return lax.ppermute(value, 'core', [(0, 1), (1, 0)])]
    ppermute x12 -> x6, waiting for transfers between devices: 9.11 us -> 11.9 us  [to_neighbours(): lax.ppermute(value, (axis, 'core'), pairs)]
    all_to_all x1, blocking collectives: 16.8 us -> 18.7 us  [body(): blocks = lax.all_to_all(payload, CHIPS, 0, 0, tiled=True)]
    ppermute x4, waiting for transfers between devices: 2.81 us -> 4.03 us  [swapped(): return lax.ppermute(value, 'core', [(0, 1), (1, 0)])]
    pallas_call x5 -> x6, Pallas kernels: 3.4 us -> 3.47 us  [the longest x1 1.56 us: body(): pl.pallas_call(place_own_kernel, in_specs=[vmem] * 5, out_specs=[hbm, vme...]
  transfers between devices with their start and end apart: 18 -> 12, of which waited for: 9 -> 8; matrix products, arithmetic and copies ran while one was open for 0% -> 0% of each run, Pallas kernels for 2% -> 2%
where the time goes in v4:
time: 89.6 us; the launch traced here: 89.4 us
  blocking collectives  41.8 us (47%)
  waiting for transfers between devices  21 us (23%)
  starting transfers between devices  17.8 us (20%)
  Pallas kernels  6.06 us (7%)
  local copies, waits for them, and re-layouts  1.98 us (2%)
    all_to_all x1, blocking collectives, body(): partial = lax.all_to_all(partial, CHIPS, 0, 0, tiled=True)  23.1 us
    all_to_all x1, blocking collectives, body(): blocks = lax.all_to_all(payload, CHIPS, 0, 0, tiled=True)  18.7 us
    ppermute x6, waiting for transfers between devices, to_neighbours(): lax.ppermute(value, (axis, 'core'), pairs)  11.9 us
    ppermute x6, starting transfers between devices, to_neighbours(): lax.ppermute(value, (axis, 'core'), pairs)  9.22 us
    ppermute x4, starting transfers between devices, swapped(): return lax.ppermute(value, 'core', [(0, 1), (1, 0)])  6.61 us
    ppermute x2, waiting for transfers between devices, from_leaving(): lax.ppermute(value, ('y', 'z', 'x', 'core'), [(96 + rank, 32 * group + ra...  5.05 us
    ppermute x4, waiting for transfers between devices, swapped(): return lax.ppermute(value, 'core', [(0, 1), (1, 0)])  4.03 us
    dynamic_slice x1, local copies, waits for them, and re-layouts, body(): got = swapped(lax.dynamic_slice(grads, (0, (1 - core) * HALF), (256, HALF)))  1.95 us
  transfers between devices with their start and end apart: 12, of which 8 were waited for; matrix products, arithmetic and copies ran while one was open for 0% of the time, Pallas kernels for 2%

profile of v4, /device:TPU:1, one launch (start us, length us, event | category | flops | bytes accessed | tf_op | source)
XLA Modules:
  0.0 89.4 jit_solution(11093647145467120135)
XLA Ops:
  0.6 2.0 %dynamic-slice_bitcast_fusion = bf16[256,4096]{1,0:T(8,128)(2,1)S(1)} fusion(bf16[1,1,256,8192]{3,2,1,0:T(8,128)(2,1)} %param.5, s32[]{:T(128)S(6)} %select_n.3), kind=kLoop, calls=%fused_computation | loop fusion | bytes 4194308 | tf_op jit(solution)/shard_map/dynamic_slice | solution.py:360
  2.6 1.5 %collective-permute-start = (bf16[256,4096]{1,0:T(8,128)(2,1)S(1)}, bf16[256,4096]{1,0:T(8,128)(2,1)S(1)}, u32[]{:S(2)}, u32[]{:S(2)}) collective-permute-start(bf16[256,4096]{1,0:T(8,128)(2,1)S(1)} %dynamic-slice_bitcast_fusion), channel_id=1, source_target_pairs={{0,1},{1,0},{2,3},{3,2},{4,5},{5,4},{6,7},{7,6},{8,9},{9,8},{10,11... | collective-permute-start | bytes 6291464 | tf_op jit(solution)/shard_map/ppermute | solution.py:343
  4.1 1.3 %collective-permute-start.1 = (f32[2,8192]{1,0:T(2,128)}, f32[2,8192]{1,0:T(2,128)S(1)}, u32[]{:S(2)}, u32[]{:S(2)}) collective-permute-start(f32[2,8192]{1,0:T(2,128)} %master_ref.3), channel_id=1, source_target_pairs={{96,0},{97,1},{98,2},{99,3},{100,4},{101,5},{102,6},{103,7},{104,8... | collective-permute-start | bytes 196616 | tf_op jit(solution)/shard_map/ppermute | solution.py:352
  5.4 0.7 collective-permute-start.2
  6.1 5.0 %collective-permute-done.1.low_ref = f32[2,8192]{1,0:T(2,128)S(1)} collective-permute-done((f32[2,8192]{1,0:T(2,128)}, f32[2,8192]{1,0:T(2,128)S(1)}, u32[]{:S(2)}, u32[]{:S(2)}) %collective-permute-start.1) | collective-permute-done | bytes 65568 | tf_op jit(solution)/shard_map/ppermute | solution.py:352
  11.2 1.2 %add_blocks.1 = (bf16[64,16,256]{2,1,0:T(8,128)(2,1)S(1)}, bf16[64,16,256]{2,1,0:T(8,128)(2,1)S(1)}, bf16[64,16,256]{2,1,0:T(8,128)(2,1)S(1)}, bf16[64,16,256]{2,1,0:T(8,128)(2,1)S(1)}) custom-call(bf16[256,8192]{1,0:T(8,128)(2,1)S(1)} %bitcast.8, bf16[256,4096]{1,0:T(8,128)(2,1)S(1)} %collective-permute-done.got_ref, ...), custom_call_target="tpu_custom_call" | custom-call | tf_op jit(solution)/shard_map/add_blocks/pallas_call | solution.py:363
  12.3 2.6 %collective-permute-start.3 = (bf16[64,16,256]{2,1,0:T(8,128)(2,1)S(1)}, bf16[64,16,256]{2,1,0:T(8,128)(2,1)S(1)}, u32[]{:S(2)}, u32[]{:S(2)}) collective-permute-start(bf16[64,16,256]{2,1,0:T(8,128)(2,1)S(1)} %get-tuple-element.19), channel_id=1, source_target_pairs={{0,2},{1,7},{2,4},{3,1},{4,6},{5,3},{6,0},{7,5},{8,10},{9,15},{10,... | collective-permute-start | bytes 1572872 | tf_op jit(solution)/shard_map/ppermute | solution.py:348
  15.0 1.0 %collective-permute-start.4 = (bf16[64,16,256]{2,1,0:T(8,128)(2,1)S(1)}, bf16[64,16,256]{2,1,0:T(8,128)(2,1)S(1)}, u32[]{:S(2)}, u32[]{:S(2)}) collective-permute-start(bf16[64,16,256]{2,1,0:T(8,128)(2,1)S(1)} %get-tuple-element.20), channel_id=1, source_target_pairs={{0,32},{1,97},{32,64},{33,1},{64,96},{65,33},{96,0},{97,65},{2,34}... | collective-permute-start | bytes 1572872 | tf_op jit(solution)/shard_map/ppermute | solution.py:348
  16.0 3.8 %collective-permute-start.5 = (bf16[64,16,256]{2,1,0:T(8,128)(2,1)S(1)}, bf16[64,16,256]{2,1,0:T(8,128)(2,1)S(1)}, u32[]{:S(2)}, u32[]{:S(2)}) collective-permute-start(bf16[64,16,256]{2,1,0:T(8,128)(2,1)S(1)} %get-tuple-element.21), channel_id=1, source_target_pairs={{0,8},{1,25},{8,16},{9,1},{16,24},{17,9},{24,0},{25,17},{2,10},{3,... | collective-permute-start | bytes 1572872 | tf_op jit(solution)/shard_map/ppermute | solution.py:348
  19.9 1.3 %collective-permute-done.6.pair_ref = f32[8,4096]{1,0:T(8,128)S(1)} collective-permute-done((f32[8,4096]{1,0:T(8,128)S(1)}, f32[8,4096]{1,0:T(8,128)S(1)}, u32[]{:S(2)}, u32[]{:S(2)}) %collective-permute-start.6) | collective-permute-done | bytes 131104 | tf_op jit(solution)/shard_map/ppermute | solution.py:343
  21.3 2.8 %collective-permute-done.4.y_ref = bf16[64,16,256]{2,1,0:T(8,128)(2,1)S(1)} collective-permute-done((bf16[64,16,256]{2,1,0:T(8,128)(2,1)S(1)}, bf16[64,16,256]{2,1,0:T(8,128)(2,1)S(1)}, u32[]{:S(2)}, u32[]{:S(2)}) %collective-permute-start.4) | collective-permute-done | bytes 524320 | tf_op jit(solution)/shard_map/ppermute | solution.py:348
  24.1 1.8 %collective-permute-done.5.z_ref = bf16[64,16,256]{2,1,0:T(8,128)(2,1)S(1)} collective-permute-done((bf16[64,16,256]{2,1,0:T(8,128)(2,1)S(1)}, bf16[64,16,256]{2,1,0:T(8,128)(2,1)S(1)}, u32[]{:S(2)}, u32[]{:S(2)}) %collective-permute-start.5) | collective-permute-done | bytes 524320 | tf_op jit(solution)/shard_map/ppermute | solution.py:348
  25.9 0.5 merge.1
  26.4 23.1 %all_to_all.10.parts_ref = bf16[64,16,384]{2,1,0:T(8,128)(2,1)S(1)} all-to-all(bf16[64,16,384]{2,1,0:T(8,128)(2,1)S(1)} %get-tuple-element.22), channel_id=1, replica_groups=mesh['y'=4,'z'=4,'x'=4,'core'=2] {'y','z','x'}, dimensions={0} | all-to-all | bytes 1572864 | tf_op jit(solution)/shard_map/all_to_all | solution.py:392
  49.5 0.8 adam.1
  50.3 18.7 %all_to_all.11.blocks_ref = bf16[64,16,384]{2,1,0:T(8,128)(2,1)S(1)} all-to-all(bf16[64,16,384]{2,1,0:T(8,128)(2,1)S(1)} %get-tuple-element.24), channel_id=1, replica_groups=mesh['y'=4,'z'=4,'x'=4,'core'=2] {'y','z','x'}, dimensions={0} | all-to-all | bytes 1572864 | tf_op jit(solution)/shard_map/all_to_all | solution.py:408
  69.2 0.5 collective-permute-start.8
  69.8 1.0 %collective-permute-start.7 = (bf16[64,16,256]{2,1,0:T(8,128)(2,1)S(1)}, bf16[64,16,256]{2,1,0:T(8,128)(2,1)S(1)}, u32[]{:S(2)}, u32[]{:S(2)}) collective-permute-start(bf16[64,16,256]{2,1,0:T(8,128)(2,1)S(1)} %mine.1), channel_id=1, source_target_pairs={{0,2},{1,7},{2,4},{3,1},{4,6},{5,3},{6,0},{7,5},{8,10},{9,15},{10,... | collective-permute-start | bytes 1572872 | tf_op jit(solution)/shard_map/ppermute | solution.py:348
  70.8 6.6 %collective-permute-done.9.z_ref = bf16[64,16,256]{2,1,0:T(8,128)(2,1)S(1)} collective-permute-done((bf16[64,16,256]{2,1,0:T(8,128)(2,1)S(1)}, bf16[64,16,256]{2,1,0:T(8,128)(2,1)S(1)}, u32[]{:S(2)}, u32[]{:S(2)}) %collective-permute-start.9) | collective-permute-done | bytes 524320 | tf_op jit(solution)/shard_map/ppermute | solution.py:348
  77.6 0.5 collective-permute-done.7.x_ref
  78.3 4.9 %collective-permute-start.10 = (bf16[64,16,1152]{2,1,0:T(8,128)(2,1)S(1)}, bf16[64,16,1152]{2,1,0:T(8,128)(2,1)S(1)}, u32[]{:S(2)}, u32[]{:S(2)}) collective-permute-start(bf16[64,16,1152]{2,1,0:T(8,128)(2,1)S(1)} %join.1), channel_id=1, source_target_pairs={{0,1},{1,0},{2,3},{3,2},{4,5},{5,4},{6,7},{7,6},{8,9},{9,8},{10,11... | collective-permute-start | bytes 7077896 | tf_op jit(solution)/shard_map/ppermute | solution.py:343
  83.3 1.6 %place_own.1 = (bf16[256,8192]{1,0:T(8,128)(2,1)}, f32[3,2,4096]{2,1,0:T(2,128)S(1)}) custom-call(bf16[64,16,384]{2,1,0:T(8,128)(2,1)S(1)} %all_to_all.11.blocks_ref, bf16[64,16,256]{2,1,0:T(8,128)(2,1)S(1)} %collective-permute-done.7.x_ref, bf16[64,16,256]{2,1,0:T(8,128)(2,1)S(1)} %collective-permute-done.8.y_ref, ...), custom_call_target="tpu_custom_call" | custom-call | flops 8000000 | bytes 8000000 | tf_op jit(solution)/shard_map/place_own/pallas_call | solution.py:428
  84.9 2.7 %collective-permute-done.11.refs_5_ = f32[8,4096]{1,0:T(8,128)S(1)} collective-permute-done((f32[8,4096]{1,0:T(8,128)S(1)}, f32[8,4096]{1,0:T(8,128)S(1)}, u32[]{:S(2)}, u32[]{:S(2)}) %collective-permute-start.11) | collective-permute-done | bytes 131104 | tf_op jit(solution)/shard_map/ppermute | solution.py:343
  87.6 1.8 %place_other.1 = (bf16[256,8192]{1,0:T(8,128)(2,1)}, f32[3,2,8192]{2,1,0:T(2,128)}, f32[3,2,8192]{2,1,0:T(2,128)}) custom-call(bf16[64,16,1152]{2,1,0:T(8,128)(2,1)S(1)} %collective-permute-done.10.refs_0_, s32[1,256]{1,0:T(1,128)S(1)} %get-tuple-element.25.key_ref.refs_1_, ...), custom_call_target="tpu_custom_call", output_to_operand_aliasing={{0}: (2, {})} | custom-call | tf_op jit(solution)/shard_map/place_other/pallas_call | solution.py:438
  (21 shorter events, 0.8 us)
Async XLA Ops:
  0.6 10.5 %copy-start = (bf16[1,1,256,8192]{3,2,1,0:T(8,128)(2,1)S(1)}, bf16[1,1,256,8192]{3,2,1,0:T(8,128)(2,1)}, u32[]{:S(2)}) copy-start(bf16[1,1,256,8192]{3,2,1,0:T(8,128)(2,1)} %param.5) | copy-start | bytes 12582916
  2.6 8.5 %collective-permute-start = (bf16[256,4096]{1,0:T(8,128)(2,1)S(1)}, bf16[256,4096]{1,0:T(8,128)(2,1)S(1)}, u32[]{:S(2)}, u32[]{:S(2)}) collective-permute-start(bf16[256,4096]{1,0:T(8,128)(2,1)S(1)} %dynamic-slice_bitcast_fusion), channel_id=1, source_target_pairs={{0,1},{1,0},{2,3},{3,2},{4,5},{5,4},{6,7},{7,6},{8,9},{9,8},{10,11... | collective-permute-start | bytes 6291464 | tf_op jit(solution)/shard_map/ppermute | solution.py:343
  4.1 7.0 %collective-permute-start.1 = (f32[2,8192]{1,0:T(2,128)}, f32[2,8192]{1,0:T(2,128)S(1)}, u32[]{:S(2)}, u32[]{:S(2)}) collective-permute-start(f32[2,8192]{1,0:T(2,128)} %master_ref.3), channel_id=1, source_target_pairs={{96,0},{97,1},{98,2},{99,3},{100,4},{101,5},{102,6},{103,7},{104,8... | collective-permute-start | bytes 196616 | tf_op jit(solution)/shard_map/ppermute | solution.py:352
  5.4 5.7 %collective-permute-start.2 = (f32[2,8192]{1,0:T(2,128)}, f32[2,8192]{1,0:T(2,128)S(1)}, u32[]{:S(2)}, u32[]{:S(2)}) collective-permute-start(f32[2,8192]{1,0:T(2,128)} %first_ref.3), channel_id=1, source_target_pairs={{96,32},{97,33},{98,34},{99,35},{100,36},{101,37},{102,38},{103,39... | collective-permute-start | bytes 196616 | tf_op jit(solution)/shard_map/ppermute | solution.py:352
  11.1 8.6 %copy-start.1 = (f32[2,8192]{1,0:T(2,128)S(1)}, f32[2,8192]{1,0:T(2,128)}, u32[]{:S(2)}) copy-start(f32[2,8192]{1,0:T(2,128)} %master_ref.3) | copy-start | bytes 196612
  11.1 8.6 %copy-start.2 = (f32[2,8192]{1,0:T(2,128)S(1)}, f32[2,8192]{1,0:T(2,128)}, u32[]{:S(2)}) copy-start(f32[2,8192]{1,0:T(2,128)} %first_ref.3) | copy-start | bytes 196612
  11.2 8.6 %copy-start.3 = (f32[2,8192]{1,0:T(2,128)S(1)}, f32[2,8192]{1,0:T(2,128)}, u32[]{:S(2)}) copy-start(f32[2,8192]{1,0:T(2,128)} %second_ref.3) | copy-start | bytes 196612
  12.3 37.2 %copy-start.4 = (s32[64]{0:T(128)S(1)}, s32[64]{0:T(128)}, u32[]{:S(2)}) copy-start(s32[64]{0:T(128)} %param.9) | copy-start | bytes 772
  12.3 8.9 %collective-permute-start.3 = (bf16[64,16,256]{2,1,0:T(8,128)(2,1)S(1)}, bf16[64,16,256]{2,1,0:T(8,128)(2,1)S(1)}, u32[]{:S(2)}, u32[]{:S(2)}) collective-permute-start(bf16[64,16,256]{2,1,0:T(8,128)(2,1)S(1)} %get-tuple-element.19), channel_id=1, source_target_pairs={{0,2},{1,7},{2,4},{3,1},{4,6},{5,3},{6,0},{7,5},{8,10},{9,15},{10,... | collective-permute-start | bytes 1572872 | tf_op jit(solution)/shard_map/ppermute | solution.py:348
  15.0 9.1 %collective-permute-start.4 = (bf16[64,16,256]{2,1,0:T(8,128)(2,1)S(1)}, bf16[64,16,256]{2,1,0:T(8,128)(2,1)S(1)}, u32[]{:S(2)}, u32[]{:S(2)}) collective-permute-start(bf16[64,16,256]{2,1,0:T(8,128)(2,1)S(1)} %get-tuple-element.20), channel_id=1, source_target_pairs={{0,32},{1,97},{32,64},{33,1},{64,96},{65,33},{96,0},{97,65},{2,34}... | collective-permute-start | bytes 1572872 | tf_op jit(solution)/shard_map/ppermute | solution.py:348
  16.0 9.9 %collective-permute-start.5 = (bf16[64,16,256]{2,1,0:T(8,128)(2,1)S(1)}, bf16[64,16,256]{2,1,0:T(8,128)(2,1)S(1)}, u32[]{:S(2)}, u32[]{:S(2)}) collective-permute-start(bf16[64,16,256]{2,1,0:T(8,128)(2,1)S(1)} %get-tuple-element.21), channel_id=1, source_target_pairs={{0,8},{1,25},{8,16},{9,1},{16,24},{17,9},{24,0},{25,17},{2,10},{3,... | collective-permute-start | bytes 1572872 | tf_op jit(solution)/shard_map/ppermute | solution.py:348
  19.8 1.4 %collective-permute-start.6 = (f32[8,4096]{1,0:T(8,128)S(1)}, f32[8,4096]{1,0:T(8,128)S(1)}, u32[]{:S(2)}, u32[]{:S(2)}) collective-permute-start(f32[8,4096]{1,0:T(8,128)S(1)} %pair.1), channel_id=1, source_target_pairs={{0,1},{1,0},{2,3},{3,2},{4,5},{5,4},{6,7},{7,6},{8,9},{9,8},{10,11... | collective-permute-start | bytes 393224 | tf_op jit(solution)/shard_map/ppermute | solution.py:343
  69.0 8.4 %collective-permute-start.9 = (bf16[64,16,256]{2,1,0:T(8,128)(2,1)S(1)}, bf16[64,16,256]{2,1,0:T(8,128)(2,1)S(1)}, u32[]{:S(2)}, u32[]{:S(2)}) collective-permute-start(bf16[64,16,256]{2,1,0:T(8,128)(2,1)S(1)} %mine.1), channel_id=1, source_target_pairs={{0,8},{1,25},{8,16},{9,1},{16,24},{17,9},{24,0},{25,17},{2,10},{3,... | collective-permute-start | bytes 1572872 | tf_op jit(solution)/shard_map/ppermute | solution.py:348
  69.2 8.3 %collective-permute-start.8 = (bf16[64,16,256]{2,1,0:T(8,128)(2,1)S(1)}, bf16[64,16,256]{2,1,0:T(8,128)(2,1)S(1)}, u32[]{:S(2)}, u32[]{:S(2)}) collective-permute-start(bf16[64,16,256]{2,1,0:T(8,128)(2,1)S(1)} %mine.1), channel_id=1, source_target_pairs={{0,32},{1,97},{32,64},{33,1},{64,96},{65,33},{96,0},{97,65},{2,34}... | collective-permute-start | bytes 1572872 | tf_op jit(solution)/shard_map/ppermute | solution.py:348
  69.8 8.3 %collective-permute-start.7 = (bf16[64,16,256]{2,1,0:T(8,128)(2,1)S(1)}, bf16[64,16,256]{2,1,0:T(8,128)(2,1)S(1)}, u32[]{:S(2)}, u32[]{:S(2)}) collective-permute-start(bf16[64,16,256]{2,1,0:T(8,128)(2,1)S(1)} %mine.1), channel_id=1, source_target_pairs={{0,2},{1,7},{2,4},{3,1},{4,6},{5,3},{6,0},{7,5},{8,10},{9,15},{10,... | collective-permute-start | bytes 1572872 | tf_op jit(solution)/shard_map/ppermute | solution.py:348
  78.3 9.3 %collective-permute-start.10 = (bf16[64,16,1152]{2,1,0:T(8,128)(2,1)S(1)}, bf16[64,16,1152]{2,1,0:T(8,128)(2,1)S(1)}, u32[]{:S(2)}, u32[]{:S(2)}) collective-permute-start(bf16[64,16,1152]{2,1,0:T(8,128)(2,1)S(1)} %join.1), channel_id=1, source_target_pairs={{0,1},{1,0},{2,3},{3,2},{4,5},{5,4},{6,7},{7,6},{8,9},{9,8},{10,11... | collective-permute-start | bytes 7077896 | tf_op jit(solution)/shard_map/ppermute | solution.py:343
  83.2 4.3 %collective-permute-start.11 = (f32[8,4096]{1,0:T(8,128)S(1)}, f32[8,4096]{1,0:T(8,128)S(1)}, u32[]{:S(2)}, u32[]{:S(2)}) collective-permute-start(f32[8,4096]{1,0:T(8,128)S(1)} %get-tuple-element.29), channel_id=1, source_target_pairs={{0,1},{1,0},{2,3},{3,2},{4,5},{5,4},{6,7},{7,6},{8,9},{9,8},{10,11... | collective-permute-start | bytes 393224 | tf_op jit(solution)/shard_map/ppermute | solution.py:343

commit v5 on v4

--- a/solution.py
+++ b/solution.py
@@ -52,7 +52,7 @@
 
 def spread_rows(low_ref, middle_ref, second_ref):
     y = lax.axis_index("y")
-    return jnp.where(y == 0, low_ref[...], jnp.where(y == 1, middle_ref[...], second_ref[...]))
+    return jnp.where(y == 0, low_ref[...], jnp.where(y == 2, middle_ref[...], second_ref[...]))
 
 
 def pair_kernel(master_ref, first_ref, second_ref, low_ref, middle_ref, pair_ref, rows_ref):
@@ -171,7 +171,7 @@
 
     @pl.when(leaving)
     def _():
-        for i, y in enumerate((0, 1, 3)):
+        for i, y in enumerate((0, 2, 3)):
             for q in range(16):
                 parts = parts_ref[16 * y + q, :, 256:384].astype(F32)
                 for h in range(2):
@@ -231,12 +231,6 @@
 
 def copy_kernel(blocks_ref, out_ref):
     out_ref[...] = blocks_ref[:, :, 0:256]
-
-
-def join_kernel(blocks_ref, x_ref, y_ref, z_ref, out_ref):
-    out_ref[:, :, 0:384] = blocks_ref[...]
-    for at, ref in ((384, x_ref), (640, y_ref), (896, z_ref)):
-        out_ref[:, :, at : at + 256] = ref[...]
 
 
 def place_half(views, key_ref, weights_ref, adopted_ref, adopted_at, adopted_ready, rows_ref, sems, core, side):
@@ -310,9 +304,9 @@
 
 
 def place_other_kernel(*refs):
-    joined_ref, key_ref, _, half_ref, own_ref, other_ref = refs[:6]
-    weights_ref, adopted_out, kept_out, adopted_ref, kept_ref, rows_ref, sems, out_sems = refs[6:]
-    views = [(joined_ref, lane) for lane in (0, 384, 640, 896)]
+    key_ref, _, half_ref, own_ref, other_ref = refs[4:9]
+    weights_ref, adopted_out, kept_out, adopted_ref, kept_ref, rows_ref, sems, out_sems = refs[9:]
+    views = [(ref, 0) for ref in refs[:4]]
     core = lax.axis_index("core")
     side = 1 - core
     kept_copy = pltpu.make_async_copy(kept_ref, kept_out, out_sems.at[0])
@@ -358,7 +352,7 @@
     hbm = pl.BlockSpec(memory_space=pltpu.HBM)
     core = lax.axis_index("core")
     got = swapped(lax.dynamic_slice(grads, (0, (1 - core) * HALF), (256, HALF)))
-    low, middle = from_leaving(master, 0), from_leaving(first, 1)
+    low, middle = from_leaving(master, 0), from_leaving(first, 2)
     piece = shape((64, 16, 256), BF)
     keep, *to_send = pl.pallas_call(
         add_kernel,
@@ -415,15 +409,7 @@
         name="mine",
     )(blocks)
     pieces = [blocks] + to_neighbours([mine] * 3)
-    joined = pl.pallas_call(
-        join_kernel,
-        in_specs=[vmem] * 4,
-        out_specs=vmem,
-        out_shape=shape((64, 16, 1152), BF),
-        compiler_params=params(),
-        name="join",
-    )(*pieces)
-    other_joined = swapped(joined)
+    other_pieces = [swapped(value) for value in pieces]
     scratch = [pltpu.VMEM((256, HALF), BF), pltpu.SemaphoreType.DMA((8,))]
     weights, adopted = pl.pallas_call(
         place_own_kernel,
@@ -437,14 +423,14 @@
     )(*pieces, key)
     weights, adopted, kept = pl.pallas_call(
         place_other_kernel,
-        in_specs=[vmem] * 2 + [hbm] + [vmem] * 3,
+        in_specs=[vmem] * 5 + [hbm] + [vmem] * 3,
         out_specs=[hbm] * 3,
         out_shape=[shape((256, 8192), BF), shape((3, 2, 8192), F32), shape((3, 2, 8192), F32)],
         scratch_shapes=[pltpu.VMEM((3, 2, 8192), F32)] * 2 + scratch + [pltpu.SemaphoreType.DMA((2,))],
-        input_output_aliases={2: 0},
+        input_output_aliases={5: 0},
         compiler_params=params(),
         name="place_other",
-    )(other_joined, key, weights, adopted, own_new, other_new)
+    )(*other_pieces, key, weights, adopted, own_new, other_new)
     return (weights, kept.transpose(1, 0, 2), adopted.transpose(1, 0, 2)[None, None])
 
 

time: 89.6 us -> 85.3 us (0.952)
  waiting for transfers between devices: 21 us -> 14.9 us
  starting transfers between devices: 17.8 us -> 22.4 us
  blocking collectives: 41.8 us -> 39.1 us
    ppermute x4 -> x7, starting transfers between devices: 6.61 us -> 12.1 us  [swapped(): return lax.ppermute(value, 'core', [(0, 1), (1, 0)])]
    ppermute x6, waiting for transfers between devices: 11.9 us -> 8.04 us  [to_neighbours(): lax.ppermute(value, (axis, 'core'), pairs)]
    ppermute x4 -> x7, waiting for transfers between devices: 4.03 us -> 1.83 us  [swapped(): return lax.ppermute(value, 'core', [(0, 1), (1, 0)])]
    all_to_all x1, blocking collectives: 23.1 us -> 21.6 us  [body(): partial = lax.all_to_all(partial, CHIPS, 0, 0, tiled=True)]
    all_to_all x1, blocking collectives: 18.7 us -> 17.5 us  [body(): blocks = lax.all_to_all(payload, CHIPS, 0, 0, tiled=True)]
    pallas_call x2 -> x1, Pallas kernels: 1.97 us -> 1.81 us  [body(): pl.pallas_call(place_other_kernel, in_specs=[vmem] * 5 + [hbm] + [vmem] *...]
  transfers between devices with their start and end apart: 12 -> 15, of which waited for: 8 -> 7; matrix products, arithmetic and copies ran while one was open for 0% -> 0% of each run, Pallas kernels for 2% -> 2%
where the time goes in v5:
time: 85.3 us; the launch traced here: 85.1 us
  blocking collectives  39.1 us (46%)
  starting transfers between devices  22.4 us (26%)
  waiting for transfers between devices  14.9 us (17%)
  Pallas kernels  5.9 us (7%)
  local copies, waits for them, and re-layouts  1.98 us (2%)
    all_to_all x1, blocking collectives, body(): partial = lax.all_to_all(partial, CHIPS, 0, 0, tiled=True)  21.6 us
    all_to_all x1, blocking collectives, body(): blocks = lax.all_to_all(payload, CHIPS, 0, 0, tiled=True)  17.5 us
    ppermute x7, starting transfers between devices, swapped(): return lax.ppermute(value, 'core', [(0, 1), (1, 0)])  12.1 us
    ppermute x6, starting transfers between devices, to_neighbours(): lax.ppermute(value, (axis, 'core'), pairs)  8.38 us
    ppermute x6, waiting for transfers between devices, to_neighbours(): lax.ppermute(value, (axis, 'core'), pairs)  8.04 us
    ppermute x2, waiting for transfers between devices, from_leaving(): lax.ppermute(value, ('y', 'z', 'x', 'core'), [(96 + rank, 32 * group + ra...  5.05 us
    dynamic_slice x1, local copies, waits for them, and re-layouts, body(): got = swapped(lax.dynamic_slice(grads, (0, (1 - core) * HALF), (256, HALF)))  1.95 us
    ppermute x2, starting transfers between devices, from_leaving(): lax.ppermute(value, ('y', 'z', 'x', 'core'), [(96 + rank, 32 * group + ra...  1.94 us
  transfers between devices with their start and end apart: 15, of which 7 were waited for; matrix products, arithmetic and copies ran while one was open for 0% of the time, Pallas kernels for 2%

profile of v5, /device:TPU:1, one launch (start us, length us, event | category | flops | bytes accessed | tf_op | source)
XLA Modules:
  0.0 85.1 jit_solution(10101473986931710785)
XLA Ops:
  0.6 2.0 %dynamic-slice_bitcast_fusion = bf16[256,4096]{1,0:T(8,128)(2,1)S(1)} fusion(bf16[1,1,256,8192]{3,2,1,0:T(8,128)(2,1)} %param.5, s32[]{:T(128)S(6)} %select_n.3), kind=kLoop, calls=%fused_computation | loop fusion | bytes 4194308 | tf_op jit(solution)/shard_map/dynamic_slice | solution.py:354
  2.6 1.5 %collective-permute-start = (bf16[256,4096]{1,0:T(8,128)(2,1)S(1)}, bf16[256,4096]{1,0:T(8,128)(2,1)S(1)}, u32[]{:S(2)}, u32[]{:S(2)}) collective-permute-start(bf16[256,4096]{1,0:T(8,128)(2,1)S(1)} %dynamic-slice_bitcast_fusion), channel_id=1, source_target_pairs={{0,1},{1,0},{2,3},{3,2},{4,5},{5,4},{6,7},{7,6},{8,9},{9,8},{10,11... | collective-permute-start | bytes 6291464 | tf_op jit(solution)/shard_map/ppermute | solution.py:337
  4.1 1.3 %collective-permute-start.1 = (f32[2,8192]{1,0:T(2,128)}, f32[2,8192]{1,0:T(2,128)S(1)}, u32[]{:S(2)}, u32[]{:S(2)}) collective-permute-start(f32[2,8192]{1,0:T(2,128)} %master_ref.3), channel_id=1, source_target_pairs={{96,0},{97,1},{98,2},{99,3},{100,4},{101,5},{102,6},{103,7},{104,8... | collective-permute-start | bytes 196616 | tf_op jit(solution)/shard_map/ppermute | solution.py:346
  5.4 0.7 collective-permute-start.2
  6.1 5.0 %collective-permute-done.1.low_ref = f32[2,8192]{1,0:T(2,128)S(1)} collective-permute-done((f32[2,8192]{1,0:T(2,128)}, f32[2,8192]{1,0:T(2,128)S(1)}, u32[]{:S(2)}, u32[]{:S(2)}) %collective-permute-start.1) | collective-permute-done | bytes 65568 | tf_op jit(solution)/shard_map/ppermute | solution.py:346
  11.2 1.2 %add_blocks.1 = (bf16[64,16,256]{2,1,0:T(8,128)(2,1)S(1)}, bf16[64,16,256]{2,1,0:T(8,128)(2,1)S(1)}, bf16[64,16,256]{2,1,0:T(8,128)(2,1)S(1)}, bf16[64,16,256]{2,1,0:T(8,128)(2,1)S(1)}) custom-call(bf16[256,8192]{1,0:T(8,128)(2,1)S(1)} %bitcast.8, bf16[256,4096]{1,0:T(8,128)(2,1)S(1)} %collective-permute-done.got_ref, ...), custom_call_target="tpu_custom_call" | custom-call | tf_op jit(solution)/shard_map/add_blocks/pallas_call | solution.py:357
  12.3 2.6 %collective-permute-start.3 = (bf16[64,16,256]{2,1,0:T(8,128)(2,1)S(1)}, bf16[64,16,256]{2,1,0:T(8,128)(2,1)S(1)}, u32[]{:S(2)}, u32[]{:S(2)}) collective-permute-start(bf16[64,16,256]{2,1,0:T(8,128)(2,1)S(1)} %get-tuple-element.19), channel_id=1, source_target_pairs={{0,2},{1,7},{2,4},{3,1},{4,6},{5,3},{6,0},{7,5},{8,10},{9,15},{10,... | collective-permute-start | bytes 1572872 | tf_op jit(solution)/shard_map/ppermute | solution.py:342
  15.0 0.7 collective-permute-start.4
  15.6 3.8 %collective-permute-start.5 = (bf16[64,16,256]{2,1,0:T(8,128)(2,1)S(1)}, bf16[64,16,256]{2,1,0:T(8,128)(2,1)S(1)}, u32[]{:S(2)}, u32[]{:S(2)}) collective-permute-start(bf16[64,16,256]{2,1,0:T(8,128)(2,1)S(1)} %get-tuple-element.21), channel_id=1, source_target_pairs={{0,8},{1,25},{8,16},{9,1},{16,24},{17,9},{24,0},{25,17},{2,10},{3,... | collective-permute-start | bytes 1572872 | tf_op jit(solution)/shard_map/ppermute | solution.py:342
  19.5 1.3 %collective-permute-done.6.pair_ref = f32[8,4096]{1,0:T(8,128)S(1)} collective-permute-done((f32[8,4096]{1,0:T(8,128)S(1)}, f32[8,4096]{1,0:T(8,128)S(1)}, u32[]{:S(2)}, u32[]{:S(2)}) %collective-permute-start.6) | collective-permute-done | bytes 131104 | tf_op jit(solution)/shard_map/ppermute | solution.py:337
  21.1 2.2 %collective-permute-done.4.y_ref = bf16[64,16,256]{2,1,0:T(8,128)(2,1)S(1)} collective-permute-done((bf16[64,16,256]{2,1,0:T(8,128)(2,1)S(1)}, bf16[64,16,256]{2,1,0:T(8,128)(2,1)S(1)}, u32[]{:S(2)}, u32[]{:S(2)}) %collective-permute-start.4) | collective-permute-done | bytes 524320 | tf_op jit(solution)/shard_map/ppermute | solution.py:342
  23.3 2.2 %collective-permute-done.5.z_ref = bf16[64,16,256]{2,1,0:T(8,128)(2,1)S(1)} collective-permute-done((bf16[64,16,256]{2,1,0:T(8,128)(2,1)S(1)}, bf16[64,16,256]{2,1,0:T(8,128)(2,1)S(1)}, u32[]{:S(2)}, u32[]{:S(2)}) %collective-permute-start.5) | collective-permute-done | bytes 524320 | tf_op jit(solution)/shard_map/ppermute | solution.py:342
  26.0 21.6 %all_to_all.10.parts_ref = bf16[64,16,384]{2,1,0:T(8,128)(2,1)S(1)} all-to-all(bf16[64,16,384]{2,1,0:T(8,128)(2,1)S(1)} %get-tuple-element.22), channel_id=1, replica_groups=mesh['y'=4,'z'=4,'x'=4,'core'=2] {'y','z','x'}, dimensions={0} | all-to-all | bytes 1572864 | tf_op jit(solution)/shard_map/all_to_all | solution.py:386
  47.6 0.8 adam.1
  48.4 17.5 %all_to_all.11.blocks_ref = bf16[64,16,384]{2,1,0:T(8,128)(2,1)S(1)} all-to-all(bf16[64,16,384]{2,1,0:T(8,128)(2,1)S(1)} %get-tuple-element.24), channel_id=1, replica_groups=mesh['y'=4,'z'=4,'x'=4,'core'=2] {'y','z','x'}, dimensions={0} | all-to-all | bytes 1572864 | tf_op jit(solution)/shard_map/all_to_all | solution.py:402
  66.0 0.8 collective-permute-start.10
  66.7 0.5 collective-permute-start.8
  67.3 3.6 %collective-permute-start.7 = (bf16[64,16,384]{2,1,0:T(8,128)(2,1)S(1)}, bf16[64,16,384]{2,1,0:T(8,128)(2,1)S(1)}, u32[]{:S(2)}, u32[]{:S(2)}) collective-permute-start(bf16[64,16,384]{2,1,0:T(8,128)(2,1)S(1)} %all_to_all.11.blocks_ref), channel_id=1, source_target_pairs={{0,1},{1,0},{2,3},{3,2},{4,5},{5,4},{6,7},{7,6},{8,9},{9,8},{10,11... | collective-permute-start | bytes 2359304 | tf_op jit(solution)/shard_map/ppermute | solution.py:337
  70.9 3.4 %collective-permute-done.12.z_ref = bf16[64,16,256]{2,1,0:T(8,128)(2,1)S(1)} collective-permute-done((bf16[64,16,256]{2,1,0:T(8,128)(2,1)S(1)}, bf16[64,16,256]{2,1,0:T(8,128)(2,1)S(1)}, u32[]{:S(2)}, u32[]{:S(2)}) %collective-permute-start.12) | collective-permute-done | bytes 524320 | tf_op jit(solution)/shard_map/ppermute | solution.py:342
  74.3 5.7 %collective-permute-start.13 = (bf16[64,16,256]{2,1,0:T(8,128)(2,1)S(1)}, bf16[64,16,256]{2,1,0:T(8,128)(2,1)S(1)}, u32[]{:S(2)}, u32[]{:S(2)}) collective-permute-start(bf16[64,16,256]{2,1,0:T(8,128)(2,1)S(1)} %collective-permute-done.12.z_ref), channel_id=1, source_target_pairs={{0,1},{1,0},{2,3},{3,2},{4,5},{5,4},{6,7},{7,6},{8,9},{9,8},{10,11... | collective-permute-start | bytes 1572872 | tf_op jit(solution)/shard_map/ppermute | solution.py:337
  80.0 0.6 collective-permute-start.11
  80.7 0.5 collective-permute-start.14
  81.2 1.6 %place_own.1 = (bf16[256,8192]{1,0:T(8,128)(2,1)}, f32[3,2,4096]{2,1,0:T(2,128)S(1)}) custom-call(bf16[64,16,384]{2,1,0:T(8,128)(2,1)S(1)} %all_to_all.11.blocks_ref, bf16[64,16,256]{2,1,0:T(8,128)(2,1)S(1)} %collective-permute-done.8.x_ref, bf16[64,16,256]{2,1,0:T(8,128)(2,1)S(1)} %collective-permute-done.10.y_ref, ...), custom_call_target="tpu_custom_call" | custom-call | flops 8000000 | bytes 8000000 | tf_op jit(solution)/shard_map/place_own/pallas_call | solution.py:414
  83.3 1.8 %place_other.1 = (bf16[256,8192]{1,0:T(8,128)(2,1)}, f32[3,2,8192]{2,1,0:T(2,128)}, f32[3,2,8192]{2,1,0:T(2,128)}) custom-call(bf16[64,16,384]{2,1,0:T(8,128)(2,1)S(1)} %collective-permute-done.7.refs_0_, bf16[64,16,256]{2,1,0:T(8,128)(2,1)S(1)} %collective-permute-done.9.refs_1_, ...), custom_call_target="tpu_custom_call", output_to_operand_aliasing={{0}: (5, {})} | custom-call | tf_op jit(solution)/shard_map/place_other/pallas_call | solution.py:424
  (26 shorter events, 1.5 us)
Async XLA Ops:
  0.6 10.5 %copy-start = (bf16[1,1,256,8192]{3,2,1,0:T(8,128)(2,1)S(1)}, bf16[1,1,256,8192]{3,2,1,0:T(8,128)(2,1)}, u32[]{:S(2)}) copy-start(bf16[1,1,256,8192]{3,2,1,0:T(8,128)(2,1)} %param.5) | copy-start | bytes 12582916
  2.6 16.8 %copy-start.1 = (f32[2,8192]{1,0:T(2,128)S(1)}, f32[2,8192]{1,0:T(2,128)}, u32[]{:S(2)}) copy-start(f32[2,8192]{1,0:T(2,128)} %master_ref.3) | copy-start | bytes 196612
  2.6 16.8 %copy-start.2 = (f32[2,8192]{1,0:T(2,128)S(1)}, f32[2,8192]{1,0:T(2,128)}, u32[]{:S(2)}) copy-start(f32[2,8192]{1,0:T(2,128)} %first_ref.3) | copy-start | bytes 196612
  2.6 16.8 %copy-start.3 = (f32[2,8192]{1,0:T(2,128)S(1)}, f32[2,8192]{1,0:T(2,128)}, u32[]{:S(2)}) copy-start(f32[2,8192]{1,0:T(2,128)} %second_ref.3) | copy-start | bytes 196612
  2.6 8.5 %collective-permute-start = (bf16[256,4096]{1,0:T(8,128)(2,1)S(1)}, bf16[256,4096]{1,0:T(8,128)(2,1)S(1)}, u32[]{:S(2)}, u32[]{:S(2)}) collective-permute-start(bf16[256,4096]{1,0:T(8,128)(2,1)S(1)} %dynamic-slice_bitcast_fusion), channel_id=1, source_target_pairs={{0,1},{1,0},{2,3},{3,2},{4,5},{5,4},{6,7},{7,6},{8,9},{9,8},{10,11... | collective-permute-start | bytes 6291464 | tf_op jit(solution)/shard_map/ppermute | solution.py:337
  4.1 7.0 %collective-permute-start.1 = (f32[2,8192]{1,0:T(2,128)}, f32[2,8192]{1,0:T(2,128)S(1)}, u32[]{:S(2)}, u32[]{:S(2)}) collective-permute-start(f32[2,8192]{1,0:T(2,128)} %master_ref.3), channel_id=1, source_target_pairs={{96,0},{97,1},{98,2},{99,3},{100,4},{101,5},{102,6},{103,7},{104,8... | collective-permute-start | bytes 196616 | tf_op jit(solution)/shard_map/ppermute | solution.py:346
  5.4 5.7 %collective-permute-start.2 = (f32[2,8192]{1,0:T(2,128)}, f32[2,8192]{1,0:T(2,128)S(1)}, u32[]{:S(2)}, u32[]{:S(2)}) collective-permute-start(f32[2,8192]{1,0:T(2,128)} %first_ref.3), channel_id=1, source_target_pairs={{96,64},{97,65},{98,66},{99,67},{100,68},{101,69},{102,70},{103,71... | collective-permute-start | bytes 196616 | tf_op jit(solution)/shard_map/ppermute | solution.py:346
  11.2 36.4 %copy-start.4 = (s32[64]{0:T(128)S(1)}, s32[64]{0:T(128)}, u32[]{:S(2)}) copy-start(s32[64]{0:T(128)} %param.9) | copy-start | bytes 772
  12.3 8.8 %collective-permute-start.3 = (bf16[64,16,256]{2,1,0:T(8,128)(2,1)S(1)}, bf16[64,16,256]{2,1,0:T(8,128)(2,1)S(1)}, u32[]{:S(2)}, u32[]{:S(2)}) collective-permute-start(bf16[64,16,256]{2,1,0:T(8,128)(2,1)S(1)} %get-tuple-element.19), channel_id=1, source_target_pairs={{0,2},{1,7},{2,4},{3,1},{4,6},{5,3},{6,0},{7,5},{8,10},{9,15},{10,... | collective-permute-start | bytes 1572872 | tf_op jit(solution)/shard_map/ppermute | solution.py:342
  15.0 8.3 %collective-permute-start.4 = (bf16[64,16,256]{2,1,0:T(8,128)(2,1)S(1)}, bf16[64,16,256]{2,1,0:T(8,128)(2,1)S(1)}, u32[]{:S(2)}, u32[]{:S(2)}) collective-permute-start(bf16[64,16,256]{2,1,0:T(8,128)(2,1)S(1)} %get-tuple-element.20), channel_id=1, source_target_pairs={{0,32},{1,97},{32,64},{33,1},{64,96},{65,33},{96,0},{97,65},{2,34}... | collective-permute-start | bytes 1572872 | tf_op jit(solution)/shard_map/ppermute | solution.py:342
  15.6 9.9 %collective-permute-start.5 = (bf16[64,16,256]{2,1,0:T(8,128)(2,1)S(1)}, bf16[64,16,256]{2,1,0:T(8,128)(2,1)S(1)}, u32[]{:S(2)}, u32[]{:S(2)}) collective-permute-start(bf16[64,16,256]{2,1,0:T(8,128)(2,1)S(1)} %get-tuple-element.21), channel_id=1, source_target_pairs={{0,8},{1,25},{8,16},{9,1},{16,24},{17,9},{24,0},{25,17},{2,10},{3,... | collective-permute-start | bytes 1572872 | tf_op jit(solution)/shard_map/ppermute | solution.py:342
  19.4 1.4 %collective-permute-start.6 = (f32[8,4096]{1,0:T(8,128)S(1)}, f32[8,4096]{1,0:T(8,128)S(1)}, u32[]{:S(2)}, u32[]{:S(2)}) collective-permute-start(f32[8,4096]{1,0:T(8,128)S(1)} %pair.1), channel_id=1, source_target_pairs={{0,1},{1,0},{2,3},{3,2},{4,5},{5,4},{6,7},{7,6},{8,9},{9,8},{10,11... | collective-permute-start | bytes 393224 | tf_op jit(solution)/shard_map/ppermute | solution.py:337
  65.9 8.4 %collective-permute-start.12 = (bf16[64,16,256]{2,1,0:T(8,128)(2,1)S(1)}, bf16[64,16,256]{2,1,0:T(8,128)(2,1)S(1)}, u32[]{:S(2)}, u32[]{:S(2)}) collective-permute-start(bf16[64,16,256]{2,1,0:T(8,128)(2,1)S(1)} %mine.1), channel_id=1, source_target_pairs={{0,8},{1,25},{8,16},{9,1},{16,24},{17,9},{24,0},{25,17},{2,10},{3,... | collective-permute-start | bytes 1572872 | tf_op jit(solution)/shard_map/ppermute | solution.py:342
  66.0 14.0 %collective-permute-start.10 = (bf16[64,16,256]{2,1,0:T(8,128)(2,1)S(1)}, bf16[64,16,256]{2,1,0:T(8,128)(2,1)S(1)}, u32[]{:S(2)}, u32[]{:S(2)}) collective-permute-start(bf16[64,16,256]{2,1,0:T(8,128)(2,1)S(1)} %mine.1), channel_id=1, source_target_pairs={{0,32},{1,97},{32,64},{33,1},{64,96},{65,33},{96,0},{97,65},{2,34}... | collective-permute-start | bytes 1572872 | tf_op jit(solution)/shard_map/ppermute | solution.py:342
  66.7 13.9 %collective-permute-start.8 = (bf16[64,16,256]{2,1,0:T(8,128)(2,1)S(1)}, bf16[64,16,256]{2,1,0:T(8,128)(2,1)S(1)}, u32[]{:S(2)}, u32[]{:S(2)}) collective-permute-start(bf16[64,16,256]{2,1,0:T(8,128)(2,1)S(1)} %mine.1), channel_id=1, source_target_pairs={{0,2},{1,7},{2,4},{3,1},{4,6},{5,3},{6,0},{7,5},{8,10},{9,15},{10,... | collective-permute-start | bytes 1572872 | tf_op jit(solution)/shard_map/ppermute | solution.py:342
  67.3 16.0 %collective-permute-start.7 = (bf16[64,16,384]{2,1,0:T(8,128)(2,1)S(1)}, bf16[64,16,384]{2,1,0:T(8,128)(2,1)S(1)}, u32[]{:S(2)}, u32[]{:S(2)}) collective-permute-start(bf16[64,16,384]{2,1,0:T(8,128)(2,1)S(1)} %all_to_all.11.blocks_ref), channel_id=1, source_target_pairs={{0,1},{1,0},{2,3},{3,2},{4,5},{5,4},{6,7},{7,6},{8,9},{9,8},{10,11... | collective-permute-start | bytes 2359304 | tf_op jit(solution)/shard_map/ppermute | solution.py:337
  74.3 8.9 %collective-permute-start.13 = (bf16[64,16,256]{2,1,0:T(8,128)(2,1)S(1)}, bf16[64,16,256]{2,1,0:T(8,128)(2,1)S(1)}, u32[]{:S(2)}, u32[]{:S(2)}) collective-permute-start(bf16[64,16,256]{2,1,0:T(8,128)(2,1)S(1)} %collective-permute-done.12.z_ref), channel_id=1, source_target_pairs={{0,1},{1,0},{2,3},{3,2},{4,5},{5,4},{6,7},{7,6},{8,9},{9,8},{10,11... | collective-permute-start | bytes 1572872 | tf_op jit(solution)/shard_map/ppermute | solution.py:337
  80.0 3.2 %collective-permute-start.11 = (bf16[64,16,256]{2,1,0:T(8,128)(2,1)S(1)}, bf16[64,16,256]{2,1,0:T(8,128)(2,1)S(1)}, u32[]{:S(2)}, u32[]{:S(2)}) collective-permute-start(bf16[64,16,256]{2,1,0:T(8,128)(2,1)S(1)} %collective-permute-done.10.y_ref), channel_id=1, source_target_pairs={{0,1},{1,0},{2,3},{3,2},{4,5},{5,4},{6,7},{7,6},{8,9},{9,8},{10,11... | collective-permute-start | bytes 1572872 | tf_op jit(solution)/shard_map/ppermute | solution.py:337
  80.7 2.6 %collective-permute-start.9 = (bf16[64,16,256]{2,1,0:T(8,128)(2,1)S(1)}, bf16[64,16,256]{2,1,0:T(8,128)(2,1)S(1)}, u32[]{:S(2)}, u32[]{:S(2)}) collective-permute-start(bf16[64,16,256]{2,1,0:T(8,128)(2,1)S(1)} %collective-permute-done.8.x_ref), channel_id=1, source_target_pairs={{0,1},{1,0},{2,3},{3,2},{4,5},{5,4},{6,7},{7,6},{8,9},{9,8},{10,11... | collective-permute-start | bytes 1572872 | tf_op jit(solution)/shard_map/ppermute | solution.py:337
  80.7 2.6 %collective-permute-start.14 = (f32[8,4096]{1,0:T(8,128)S(1)}, f32[8,4096]{1,0:T(8,128)S(1)}, u32[]{:S(2)}, u32[]{:S(2)}) collective-permute-start(f32[8,4096]{1,0:T(8,128)S(1)} %get-tuple-element.29), channel_id=1, source_target_pairs={{0,1},{1,0},{2,3},{3,2},{4,5},{5,4},{6,7},{7,6},{8,9},{9,8},{10,11... | collective-permute-start | bytes 393224 | tf_op jit(solution)/shard_map/ppermute | solution.py:337

commit v6 on v5

--- a/solution.py
+++ b/solution.py
@@ -50,17 +50,17 @@
     return pltpu.roll(rows, 4, axis=0)
 
 
-def spread_rows(low_ref, middle_ref, second_ref):
-    y = lax.axis_index("y")
-    return jnp.where(y == 0, low_ref[...], jnp.where(y == 2, middle_ref[...], second_ref[...]))
-
-
-def pair_kernel(master_ref, first_ref, second_ref, low_ref, middle_ref, pair_ref, rows_ref):
+def stack_kernel(master_ref, first_ref, out_ref):
+    out_ref[0:2, :] = master_ref[...]
+    out_ref[2:4, :] = first_ref[...]
+
+
+def pair_kernel(master_ref, first_ref, second_ref, passed_ref, pair_ref):
     other = columns(1 - lax.axis_index("core"))
+    pair_ref[...] = jnp.zeros_like(pair_ref)
     for i, ref in enumerate((master_ref, first_ref, second_ref)):
         pair_ref[2 * i : 2 * i + 2, :] = ref[:, other]
-    rows_ref[...] = spread_rows(low_ref, middle_ref, second_ref)
-    pair_ref[6:8, :] = rows_ref[:, other]
+    pair_ref[8:12, :] = passed_ref[:, other]
 
 
 def chip_class(chip):
@@ -76,48 +76,43 @@
 
 
 def add_kernel(
-    grads_ref, got_ref, low_ref, middle_ref, keep_ref, x_ref, y_ref, z_ref, blocks_ref
+    grads_ref, got_ref, passed_ref, keep_ref, x_ref, y_ref, z_ref
 ):
     core = lax.axis_index("core")
-    low = iota((8, 1024), 0) < 4
+    kind = chip_class(own_chip())
+    low = iota((8, 256), 0) < 4
+    pieces = (keep_ref, x_ref, y_ref, z_ref)
 
     def kept(i, carry):
         rows = pl.ds(pl.multiple_of(16 * i, 16), 16)
-        parts = []
-        for k in range(4):
-            cut = pl.ds(pl.multiple_of(core * HALF + k * 1024, 1024), 1024)
-            got = got_ref[rows, k * 1024 : (k + 1) * 1024]
-            parts.append(grads_ref[rows, cut].astype(F32) + got.astype(F32))
-        for tile in range(2):
-            c = [part[8 * tile : 8 * tile + 8] for part in parts]
-            even = [jnp.where(low, c[k], turned(c[k + 1])) for k in (0, 2)]
-            odd = [jnp.where(low, turned(c[k]), c[k + 1]) for k in (0, 2)]
-            for chip, block in ((4 * i + 2 * tile, even), (4 * i + 2 * tile + 1, odd)):
-                blocks_ref[chip] = jnp.concatenate(block, axis=0).astype(BF)
+        for axis, ref in enumerate(pieces):
+            parts = []
+            for k in range(4):
+                at = (kind ^ axis) * 4 + k
+                parts.append(grads_ref[rows, quarter(core * 16 + at)].astype(F32) + got_ref[rows, quarter(at)].astype(F32))
+            for tile in range(2):
+                c = [part[8 * tile : 8 * tile + 8] for part in parts]
+                even = [jnp.where(low, c[k], turned(c[k + 1])) for k in (0, 2)]
+                odd = [jnp.where(low, turned(c[k]), c[k + 1]) for k in (0, 2)]
+                for chip, block in ((4 * i + 2 * tile, even), (4 * i + 2 * tile + 1, odd)):
+                    ref[chip] = jnp.concatenate(block, axis=0).astype(BF)
         return carry
 
     lax.fori_loop(0, 12, kept, 0)
 
     def leave(q, carry):
-        cut = pl.ds(pl.multiple_of(q * 256, 256), 256)
-        own_cut = pl.ds(pl.multiple_of(core * HALF + q * 256, 256), 256)
-        for a in range(4):
-            rows = slice(192 + 16 * a, 208 + 16 * a)
-            total = grads_ref[rows, own_cut].astype(F32) + got_ref[rows, cut].astype(F32)
-            blocks_ref[48 + q, :, a * 256 : (a + 1) * 256] = total.astype(BF)
-        return carry
-
-    lax.fori_loop(0, 16, leave, 0)
-    kind = chip_class(own_chip())
-    keep_ref[...] = blocks_ref[:, :, quarter(kind)]
-    for axis, ref in enumerate((x_ref, y_ref, z_ref)):
-        ref[...] = blocks_ref[:, :, quarter(kind ^ (axis + 1))]
+        for axis, ref in enumerate(pieces):
+            rows = pl.ds(pl.multiple_of(192 + 16 * (kind ^ axis), 16), 16)
+            total = grads_ref[rows, quarter(core * 16 + q)].astype(F32) + got_ref[rows, quarter(q)].astype(F32)
+            ref[48 + q] = total.astype(BF)
+        return carry
+
+    lax.fori_loop(0, 16, leave, 0, unroll=4)
 
 
 def merge_kernel(
     keep_ref, x_ref, y_ref, z_ref,
-    master_ref, first_ref, second_ref, low_ref, middle_ref, pair_ref,
-    out_ref, old_ref, rows_ref, split_ref,
+    master_ref, first_ref, second_ref, passed_ref, pair_ref, out_ref, old_ref, split_ref,
 ):
     core = lax.axis_index("core")
 
@@ -130,18 +125,19 @@
 
     lax.fori_loop(0, 64, add, 0, unroll=8)
 
-    rows_ref[...] = spread_rows(low_ref, middle_ref, second_ref)
+    old_ref[12:16, :] = jnp.zeros((4, HALF), F32)
     for mine in range(2):
 
         @pl.when(core == mine)
         def _():
-            for i, ref in enumerate((master_ref, first_ref, second_ref, rows_ref)):
+            for i, ref in enumerate((master_ref, first_ref, second_ref)):
                 at = 4 * i + 2 * mine
                 old_ref[at : at + 2, :] = ref[:, mine * HALF : (mine + 1) * HALF]
                 at = 4 * i + 2 * (1 - mine)
                 old_ref[at : at + 2, :] = pair_ref[2 * i : 2 * i + 2, :]
 
-    passed = old_ref[12:16, :]
+    passed = passed_ref[:, columns(core)] + pair_ref[8:12, :]
+    passed = jnp.where(lax.axis_index("y") == 3, old_ref[8:12, :], passed)
     high = passed.astype(BF).astype(F32)
     split_ref[0:4, :] = high
     split_ref[4:8, :] = passed - high
@@ -171,19 +167,27 @@
 
     @pl.when(leaving)
     def _():
-        for i, y in enumerate((0, 2, 3)):
+        for y in (0, 2, 3):
             for q in range(16):
                 parts = parts_ref[16 * y + q, :, 256:384].astype(F32)
+                row = 4 * (q % 4)
                 for h in range(2):
                     value = parts[8 * h : 8 * h + 4] + parts[8 * h + 4 : 8 * h + 8]
-                    at = (q // 4) * 256 + h * 128
-                    old_ref[i, 4 * (q % 4) : 4 * (q % 4) + 4, at : at + 128] = value
+                    cut = slice((q // 4) * 256 + h * 128, (q // 4) * 256 + h * 128 + 128)
+                    if y == 3:
+                        old_ref[2, row : row + 4, cut] = value
+                    else:
+                        old_ref[0, row + y : row + y + 2, cut] = value[0:2]
+                        old_ref[1, row + y : row + y + 2, cut] = value[2:4]
 
     @pl.when(jnp.logical_not(leaving))
     def _():
         for i in range(3):
-            for k in range(4):
-                old_ref[i, 4 * k : 4 * k + 4, :] = chip_ref[4 * i : 4 * i + 4, k * 1024 : (k + 1) * 1024]
+            for n in range(16):
+                k, u = n % 4, n // 4
+                old_ref[i, 4 * k : 4 * k + 4, u * 256 : (u + 1) * 256] = chip_ref[
+                    4 * i : 4 * i + 4, n * 256 : (n + 1) * 256
+                ]
 
     new = adam_update(old_ref[0], old_ref[1], old_ref[2], gradient)
     own_ref[6:8, :] = jnp.zeros((2, HALF), F32)
@@ -194,12 +198,13 @@
         @pl.when(core == mine)
         def _():
             for i in range(3):
-                for k in range(4):
-                    cut = slice(k * 1024, (k + 1) * 1024)
+                for n in range(16):
+                    k, u = n % 4, n // 4
+                    cut, lanes = slice(n * 256, (n + 1) * 256), slice(u * 256, (u + 1) * 256)
                     at = 4 * k + 2 * mine
-                    own_ref[2 * i : 2 * i + 2, cut] = values[i][at : at + 2, :]
+                    own_ref[2 * i : 2 * i + 2, cut] = values[i][at : at + 2, lanes]
                     at = 4 * k + 2 * (1 - mine)
-                    other_ref[2 * i : 2 * i + 2, cut] = values[i][at : at + 2, :]
+                    other_ref[2 * i : 2 * i + 2, cut] = values[i][at : at + 2, lanes]
 
     weights = new[0].astype(BF)
 
@@ -259,7 +264,7 @@
                     tiles.append(cut)
                 rows = pl.ds(pl.multiple_of(32 * i + 16 * g, 16), 16)
                 for k in range(4):
-                    rows_ref[rows, quarter((kind ^ axis) + 4 * k)] = jnp.concatenate(
+                    rows_ref[rows, quarter((kind ^ axis) * 4 + k)] = jnp.concatenate(
                         [tiles[0][k], tiles[1][k]], axis=0
                     ).astype(BF)
         store(i).start()
@@ -342,8 +347,9 @@
     return [lax.ppermute(value, (axis, "core"), pairs) for axis, value in zip("xyz", values)]
 
 
-def from_leaving(value, group):
-    return lax.ppermute(value, ("y", "z", "x", "core"), [(96 + rank, 32 * group + rank) for rank in range(32)])
+def from_leaving(value):
+    pairs = [(96 + rank, 64 * (rank % 2) + rank) for rank in range(32)]
+    return lax.ppermute(value, ("y", "z", "x", "core"), pairs)
 
 
 def body(local_grads, master, first, second, new_owner):
@@ -352,37 +358,43 @@
     hbm = pl.BlockSpec(memory_space=pltpu.HBM)
     core = lax.axis_index("core")
     got = swapped(lax.dynamic_slice(grads, (0, (1 - core) * HALF), (256, HALF)))
-    low, middle = from_leaving(master, 0), from_leaving(first, 2)
+    stacked = pl.pallas_call(
+        stack_kernel,
+        in_specs=[vmem] * 2,
+        out_specs=vmem,
+        out_shape=shape((4, 8192), F32),
+        compiler_params=params(),
+        name="stack",
+    )(master, first)
+    passed = from_leaving(stacked)
     piece = shape((64, 16, 256), BF)
     keep, *to_send = pl.pallas_call(
         add_kernel,
-        in_specs=[vmem] * 4,
+        in_specs=[vmem] * 3,
         out_specs=[vmem] * 4,
         out_shape=[piece] * 4,
-        scratch_shapes=[pltpu.VMEM((64, 16, 1024), BF)],
         compiler_params=params(),
         name="add_blocks",
-    )(grads, got, low, middle)
+    )(grads, got, passed)
     pair = pl.pallas_call(
         pair_kernel,
-        in_specs=[vmem] * 5,
+        in_specs=[vmem] * 4,
         out_specs=vmem,
-        out_shape=shape((8, HALF), F32),
-        scratch_shapes=[pltpu.VMEM((2, 8192), F32)],
+        out_shape=shape((16, HALF), F32),
         compiler_params=params(),
         name="pair",
-    )(master, first, second, low, middle)
+    )(master, first, second, passed)
     arrived = to_neighbours(to_send)
     pair = swapped(pair)
     partial, old = pl.pallas_call(
         merge_kernel,
-        in_specs=[vmem] * 10,
+        in_specs=[vmem] * 9,
         out_specs=[vmem] * 2,
         out_shape=[shape((64, 16, 384), BF), shape((16, HALF), F32)],
-        scratch_shapes=[pltpu.VMEM((2, 8192), F32), pltpu.VMEM((8, HALF), F32)],
+        scratch_shapes=[pltpu.VMEM((8, HALF), F32)],
         compiler_params=params(),
         name="merge",
-    )(keep, *arrived, master, first, second, low, middle, pair)
+    )(keep, *arrived, master, first, second, passed, pair)
     partial = lax.all_to_all(partial, CHIPS, 0, 0, tiled=True)
     payload, own_new, other_new, key = pl.pallas_call(
         adam_kernel,

time: 85.3 us -> 83.7 us (0.981)
  starting transfers between devices: 22.4 us -> 25.8 us
  waiting for transfers between devices: 14.9 us -> 11.8 us
  blocking collectives: 39.1 us -> 37.4 us
    ppermute x2 -> x1, waiting for transfers between devices: 5.05 us -> 0.01 us  [from_leaving(): return lax.ppermute(value, ('y', 'z', 'x', 'core'), pairs)]
    ppermute x7, waiting for transfers between devices: 1.83 us -> 5.08 us  [swapped(): return lax.ppermute(value, 'core', [(0, 1), (1, 0)])]
    ppermute x6, starting transfers between devices: 8.38 us -> 11.2 us  [to_neighbours(): lax.ppermute(value, (axis, 'core'), pairs)]
    ppermute x7, starting transfers between devices: 12.1 us -> 13.9 us  [swapped(): return lax.ppermute(value, 'core', [(0, 1), (1, 0)])]
    ppermute x6, waiting for transfers between devices: 8.04 us -> 6.72 us  [to_neighbours(): lax.ppermute(value, (axis, 'core'), pairs)]
    ppermute x2 -> x1, starting transfers between devices: 1.94 us -> 0.67 us  [from_leaving(): return lax.ppermute(value, ('y', 'z', 'x', 'core'), pairs)]
    all_to_all x1, blocking collectives: 21.6 us -> 20.3 us  [body(): partial = lax.all_to_all(partial, CHIPS, 0, 0, tiled=True)]
  transfers between devices with their start and end apart: 15 -> 14, of which waited for: 7 -> 6; matrix products, arithmetic and copies ran while one was open for 0% -> 0% of each run, Pallas kernels for 2% -> 2%
where the time goes in v6:
time: 83.7 us; the launch traced here: 83.5 us
  blocking collectives  37.4 us (45%)
  starting transfers between devices  25.8 us (31%)
  waiting for transfers between devices  11.8 us (14%)
  Pallas kernels  5.7 us (7%)
  local copies, waits for them, and re-layouts  1.98 us (2%)
    all_to_all x1, blocking collectives, body(): partial = lax.all_to_all(partial, CHIPS, 0, 0, tiled=True)  20.3 us
    all_to_all x1, blocking collectives, body(): blocks = lax.all_to_all(payload, CHIPS, 0, 0, tiled=True)  17.1 us
    ppermute x7, starting transfers between devices, swapped(): return lax.ppermute(value, 'core', [(0, 1), (1, 0)])  13.9 us
    ppermute x6, starting transfers between devices, to_neighbours(): lax.ppermute(value, (axis, 'core'), pairs)  11.2 us
    ppermute x6, waiting for transfers between devices, to_neighbours(): lax.ppermute(value, (axis, 'core'), pairs)  6.72 us
    ppermute x7, waiting for transfers between devices, swapped(): return lax.ppermute(value, 'core', [(0, 1), (1, 0)])  5.08 us
    dynamic_slice x1, local copies, waits for them, and re-layouts, body(): got = swapped(lax.dynamic_slice(grads, (0, (1 - core) * HALF), (256, HALF)))  1.95 us
    pallas_call x1, Pallas kernels, body(): pl.pallas_call(place_other_kernel, in_specs=[vmem] * 5 + [hbm] + [vmem] *...  1.81 us
  transfers between devices with their start and end apart: 14, of which 6 were waited for; matrix products, arithmetic and copies ran while one was open for 0% of the time, Pallas kernels for 2%

profile of v6, /device:TPU:1, one launch (start us, length us, event | category | flops | bytes accessed | tf_op | source)
XLA Modules:
  0.0 83.5 jit_solution(4948452642147758987)
XLA Ops:
  0.7 2.0 %dynamic-slice_bitcast_fusion = bf16[256,4096]{1,0:T(8,128)(2,1)S(1)} fusion(bf16[1,1,256,8192]{3,2,1,0:T(8,128)(2,1)} %param.5, s32[]{:T(128)S(6)} %select_n.3), kind=kLoop, calls=%fused_computation | loop fusion | bytes 4194308 | tf_op jit(solution)/shard_map/dynamic_slice | solution.py:360
  2.6 1.5 %collective-permute-start = (bf16[256,4096]{1,0:T(8,128)(2,1)S(1)}, bf16[256,4096]{1,0:T(8,128)(2,1)S(1)}, u32[]{:S(2)}, u32[]{:S(2)}) collective-permute-start(bf16[256,4096]{1,0:T(8,128)(2,1)S(1)} %dynamic-slice_bitcast_fusion), channel_id=1, source_target_pairs={{0,1},{1,0},{2,3},{3,2},{4,5},{5,4},{6,7},{7,6},{8,9},{9,8},{10,11... | collective-permute-start | bytes 6291464 | tf_op jit(solution)/shard_map/ppermute | solution.py:342
  4.2 0.7 collective-permute-start.1
  4.9 3.1 %collective-permute-done.got_ref = bf16[256,4096]{1,0:T(8,128)(2,1)S(1)} collective-permute-done((bf16[256,4096]{1,0:T(8,128)(2,1)S(1)}, bf16[256,4096]{1,0:T(8,128)(2,1)S(1)}, u32[]{:S(2)}, u32[]{:S(2)}) %collective-permute-start) | collective-permute-done | bytes 2097184 | tf_op jit(solution)/shard_map/ppermute | solution.py:342
  7.9 0.9 %add_blocks.1 = (bf16[64,16,256]{2,1,0:T(8,128)(2,1)S(1)}, bf16[64,16,256]{2,1,0:T(8,128)(2,1)S(1)}, bf16[64,16,256]{2,1,0:T(8,128)(2,1)S(1)}, bf16[64,16,256]{2,1,0:T(8,128)(2,1)S(1)}) custom-call(bf16[256,8192]{1,0:T(8,128)(2,1)S(1)} %bitcast.8, bf16[256,4096]{1,0:T(8,128)(2,1)S(1)} %collective-permute-done.got_ref, ...), custom_call_target="tpu_custom_call" | custom-call | tf_op jit(solution)/shard_map/add_blocks/pallas_call | solution.py:371
  8.9 2.6 %collective-permute-start.2 = (bf16[64,16,256]{2,1,0:T(8,128)(2,1)S(1)}, bf16[64,16,256]{2,1,0:T(8,128)(2,1)S(1)}, u32[]{:S(2)}, u32[]{:S(2)}) collective-permute-start(bf16[64,16,256]{2,1,0:T(8,128)(2,1)S(1)} %get-tuple-element.19), channel_id=1, source_target_pairs={{0,2},{1,7},{2,4},{3,1},{4,6},{5,3},{6,0},{7,5},{8,10},{9,15},{10,... | collective-permute-start | bytes 1572872 | tf_op jit(solution)/shard_map/ppermute | solution.py:347
  11.5 3.3 %collective-permute-start.3 = (bf16[64,16,256]{2,1,0:T(8,128)(2,1)S(1)}, bf16[64,16,256]{2,1,0:T(8,128)(2,1)S(1)}, u32[]{:S(2)}, u32[]{:S(2)}) collective-permute-start(bf16[64,16,256]{2,1,0:T(8,128)(2,1)S(1)} %get-tuple-element.20), channel_id=1, source_target_pairs={{0,32},{1,97},{32,64},{33,1},{64,96},{65,33},{96,0},{97,65},{2,34}... | collective-permute-start | bytes 1572872 | tf_op jit(solution)/shard_map/ppermute | solution.py:347
  14.8 3.8 %collective-permute-start.4 = (bf16[64,16,256]{2,1,0:T(8,128)(2,1)S(1)}, bf16[64,16,256]{2,1,0:T(8,128)(2,1)S(1)}, u32[]{:S(2)}, u32[]{:S(2)}) collective-permute-start(bf16[64,16,256]{2,1,0:T(8,128)(2,1)S(1)} %get-tuple-element.21), channel_id=1, source_target_pairs={{0,8},{1,25},{8,16},{9,1},{16,24},{17,9},{24,0},{25,17},{2,10},{3,... | collective-permute-start | bytes 1572872 | tf_op jit(solution)/shard_map/ppermute | solution.py:347
  18.7 1.5 %collective-permute-done.5.pair_ref = f32[16,4096]{1,0:T(8,128)S(1)} collective-permute-done((f32[16,4096]{1,0:T(8,128)S(1)}, f32[16,4096]{1,0:T(8,128)S(1)}, u32[]{:S(2)}, u32[]{:S(2)}) %collective-permute-start.5) | collective-permute-done | bytes 262176 | tf_op jit(solution)/shard_map/ppermute | solution.py:342
  20.3 0.7 collective-permute-done.3.y_ref
  21.0 3.8 %collective-permute-done.4.z_ref = bf16[64,16,256]{2,1,0:T(8,128)(2,1)S(1)} collective-permute-done((bf16[64,16,256]{2,1,0:T(8,128)(2,1)S(1)}, bf16[64,16,256]{2,1,0:T(8,128)(2,1)S(1)}, u32[]{:S(2)}, u32[]{:S(2)}) %collective-permute-start.4) | collective-permute-done | bytes 524320 | tf_op jit(solution)/shard_map/ppermute | solution.py:347
  25.2 20.3 %all_to_all.10.parts_ref = bf16[64,16,384]{2,1,0:T(8,128)(2,1)S(1)} all-to-all(bf16[64,16,384]{2,1,0:T(8,128)(2,1)S(1)} %get-tuple-element.22), channel_id=1, replica_groups=mesh['y'=4,'z'=4,'x'=4,'core'=2] {'y','z','x'}, dimensions={0} | all-to-all | bytes 1572864 | tf_op jit(solution)/shard_map/all_to_all | solution.py:398
  45.5 0.8 adam.1
  46.3 17.1 %all_to_all.11.blocks_ref = bf16[64,16,384]{2,1,0:T(8,128)(2,1)S(1)} all-to-all(bf16[64,16,384]{2,1,0:T(8,128)(2,1)S(1)} %get-tuple-element.24), channel_id=1, replica_groups=mesh['y'=4,'z'=4,'x'=4,'core'=2] {'y','z','x'}, dimensions={0} | all-to-all | bytes 1572864 | tf_op jit(solution)/shard_map/all_to_all | solution.py:414
  63.5 0.6 collective-permute-start.9
  64.1 0.8 %collective-permute-start.7 = (bf16[64,16,256]{2,1,0:T(8,128)(2,1)S(1)}, bf16[64,16,256]{2,1,0:T(8,128)(2,1)S(1)}, u32[]{:S(2)}, u32[]{:S(2)}) collective-permute-start(bf16[64,16,256]{2,1,0:T(8,128)(2,1)S(1)} %mine.1), channel_id=1, source_target_pairs={{0,2},{1,7},{2,4},{3,1},{4,6},{5,3},{6,0},{7,5},{8,10},{9,15},{10,... | collective-permute-start | bytes 1572872 | tf_op jit(solution)/shard_map/ppermute | solution.py:347
  65.0 4.3 %collective-permute-start.6 = (bf16[64,16,384]{2,1,0:T(8,128)(2,1)S(1)}, bf16[64,16,384]{2,1,0:T(8,128)(2,1)S(1)}, u32[]{:S(2)}, u32[]{:S(2)}) collective-permute-start(bf16[64,16,384]{2,1,0:T(8,128)(2,1)S(1)} %all_to_all.11.blocks_ref), channel_id=1, source_target_pairs={{0,1},{1,0},{2,3},{3,2},{4,5},{5,4},{6,7},{7,6},{8,9},{9,8},{10,11... | collective-permute-start | bytes 2359304 | tf_op jit(solution)/shard_map/ppermute | solution.py:342
  69.3 2.3 %collective-permute-done.11.z_ref = bf16[64,16,256]{2,1,0:T(8,128)(2,1)S(1)} collective-permute-done((bf16[64,16,256]{2,1,0:T(8,128)(2,1)S(1)}, bf16[64,16,256]{2,1,0:T(8,128)(2,1)S(1)}, u32[]{:S(2)}, u32[]{:S(2)}) %collective-permute-start.11) | collective-permute-done | bytes 524320 | tf_op jit(solution)/shard_map/ppermute | solution.py:347
  71.6 6.9 %collective-permute-start.12 = (bf16[64,16,256]{2,1,0:T(8,128)(2,1)S(1)}, bf16[64,16,256]{2,1,0:T(8,128)(2,1)S(1)}, u32[]{:S(2)}, u32[]{:S(2)}) collective-permute-start(bf16[64,16,256]{2,1,0:T(8,128)(2,1)S(1)} %collective-permute-done.11.z_ref), channel_id=1, source_target_pairs={{0,1},{1,0},{2,3},{3,2},{4,5},{5,4},{6,7},{7,6},{8,9},{9,8},{10,11... | collective-permute-start | bytes 1572872 | tf_op jit(solution)/shard_map/ppermute | solution.py:342
  78.4 0.6 collective-permute-start.10
  79.1 0.5 collective-permute-start.13
  79.6 1.6 %place_own.1 = (bf16[256,8192]{1,0:T(8,128)(2,1)}, f32[3,2,4096]{2,1,0:T(2,128)S(1)}) custom-call(bf16[64,16,384]{2,1,0:T(8,128)(2,1)S(1)} %all_to_all.11.blocks_ref, bf16[64,16,256]{2,1,0:T(8,128)(2,1)S(1)} %collective-permute-done.7.x_ref, bf16[64,16,256]{2,1,0:T(8,128)(2,1)S(1)} %collective-permute-done.9.y_ref, ...), custom_call_target="tpu_custom_call" | custom-call | flops 8000000 | bytes 8000000 | tf_op jit(solution)/shard_map/place_own/pallas_call | solution.py:426
  81.1 0.5 collective-permute-done.13.refs_8_
  81.7 1.8 %place_other.1 = (bf16[256,8192]{1,0:T(8,128)(2,1)}, f32[3,2,8192]{2,1,0:T(2,128)}, f32[3,2,8192]{2,1,0:T(2,128)}) custom-call(bf16[64,16,384]{2,1,0:T(8,128)(2,1)S(1)} %collective-permute-done.6.refs_0_, bf16[64,16,256]{2,1,0:T(8,128)(2,1)S(1)} %collective-permute-done.8.refs_1_, ...), custom_call_target="tpu_custom_call", output_to_operand_aliasing={{0}: (5, {})} | custom-call | tf_op jit(solution)/shard_map/place_other/pallas_call | solution.py:436
  (25 shorter events, 0.8 us)
Async XLA Ops:
  0.6 3.5 %copy-start.2 = (f32[2,8192]{1,0:T(2,128)S(1)}, f32[2,8192]{1,0:T(2,128)}, u32[]{:S(2)}) copy-start(f32[2,8192]{1,0:T(2,128)} %first_ref.5) | copy-start | bytes 196612
  0.6 3.5 %copy-start.1 = (f32[2,8192]{1,0:T(2,128)S(1)}, f32[2,8192]{1,0:T(2,128)}, u32[]{:S(2)}) copy-start(f32[2,8192]{1,0:T(2,128)} %master_ref.5) | copy-start | bytes 196612
  0.7 7.3 %copy-start = (bf16[1,1,256,8192]{3,2,1,0:T(8,128)(2,1)S(1)}, bf16[1,1,256,8192]{3,2,1,0:T(8,128)(2,1)}, u32[]{:S(2)}) copy-start(bf16[1,1,256,8192]{3,2,1,0:T(8,128)(2,1)} %param.5) | copy-start | bytes 12582916
  2.6 16.0 %copy-start.3 = (f32[2,8192]{1,0:T(2,128)S(1)}, f32[2,8192]{1,0:T(2,128)}, u32[]{:S(2)}) copy-start(f32[2,8192]{1,0:T(2,128)} %second_ref.3) | copy-start | bytes 196612
  2.6 5.3 %collective-permute-start = (bf16[256,4096]{1,0:T(8,128)(2,1)S(1)}, bf16[256,4096]{1,0:T(8,128)(2,1)S(1)}, u32[]{:S(2)}, u32[]{:S(2)}) collective-permute-start(bf16[256,4096]{1,0:T(8,128)(2,1)S(1)} %dynamic-slice_bitcast_fusion), channel_id=1, source_target_pairs={{0,1},{1,0},{2,3},{3,2},{4,5},{5,4},{6,7},{7,6},{8,9},{9,8},{10,11... | collective-permute-start | bytes 6291464 | tf_op jit(solution)/shard_map/ppermute | solution.py:342
  4.2 0.7 collective-permute-start.1
  7.9 37.6 %copy-start.4 = (s32[64]{0:T(128)S(1)}, s32[64]{0:T(128)}, u32[]{:S(2)}) copy-start(s32[64]{0:T(128)} %param.9) | copy-start | bytes 772
  8.9 11.4 %collective-permute-start.2 = (bf16[64,16,256]{2,1,0:T(8,128)(2,1)S(1)}, bf16[64,16,256]{2,1,0:T(8,128)(2,1)S(1)}, u32[]{:S(2)}, u32[]{:S(2)}) collective-permute-start(bf16[64,16,256]{2,1,0:T(8,128)(2,1)S(1)} %get-tuple-element.19), channel_id=1, source_target_pairs={{0,2},{1,7},{2,4},{3,1},{4,6},{5,3},{6,0},{7,5},{8,10},{9,15},{10,... | collective-permute-start | bytes 1572872 | tf_op jit(solution)/shard_map/ppermute | solution.py:347
  11.5 9.4 %collective-permute-start.3 = (bf16[64,16,256]{2,1,0:T(8,128)(2,1)S(1)}, bf16[64,16,256]{2,1,0:T(8,128)(2,1)S(1)}, u32[]{:S(2)}, u32[]{:S(2)}) collective-permute-start(bf16[64,16,256]{2,1,0:T(8,128)(2,1)S(1)} %get-tuple-element.20), channel_id=1, source_target_pairs={{0,32},{1,97},{32,64},{33,1},{64,96},{65,33},{96,0},{97,65},{2,34}... | collective-permute-start | bytes 1572872 | tf_op jit(solution)/shard_map/ppermute | solution.py:347
  14.8 9.9 %collective-permute-start.4 = (bf16[64,16,256]{2,1,0:T(8,128)(2,1)S(1)}, bf16[64,16,256]{2,1,0:T(8,128)(2,1)S(1)}, u32[]{:S(2)}, u32[]{:S(2)}) collective-permute-start(bf16[64,16,256]{2,1,0:T(8,128)(2,1)S(1)} %get-tuple-element.21), channel_id=1, source_target_pairs={{0,8},{1,25},{8,16},{9,1},{16,24},{17,9},{24,0},{25,17},{2,10},{3,... | collective-permute-start | bytes 1572872 | tf_op jit(solution)/shard_map/ppermute | solution.py:347
  18.6 1.6 %collective-permute-start.5 = (f32[16,4096]{1,0:T(8,128)S(1)}, f32[16,4096]{1,0:T(8,128)S(1)}, u32[]{:S(2)}, u32[]{:S(2)}) collective-permute-start(f32[16,4096]{1,0:T(8,128)S(1)} %pair.1), channel_id=1, source_target_pairs={{0,1},{1,0},{2,3},{3,2},{4,5},{5,4},{6,7},{7,6},{8,9},{9,8},{10,11... | collective-permute-start | bytes 786440 | tf_op jit(solution)/shard_map/ppermute | solution.py:342
  63.5 8.1 %collective-permute-start.11 = (bf16[64,16,256]{2,1,0:T(8,128)(2,1)S(1)}, bf16[64,16,256]{2,1,0:T(8,128)(2,1)S(1)}, u32[]{:S(2)}, u32[]{:S(2)}) collective-permute-start(bf16[64,16,256]{2,1,0:T(8,128)(2,1)S(1)} %mine.1), channel_id=1, source_target_pairs={{0,8},{1,25},{8,16},{9,1},{16,24},{17,9},{24,0},{25,17},{2,10},{3,... | collective-permute-start | bytes 1572872 | tf_op jit(solution)/shard_map/ppermute | solution.py:347
  63.5 14.9 %collective-permute-start.9 = (bf16[64,16,256]{2,1,0:T(8,128)(2,1)S(1)}, bf16[64,16,256]{2,1,0:T(8,128)(2,1)S(1)}, u32[]{:S(2)}, u32[]{:S(2)}) collective-permute-start(bf16[64,16,256]{2,1,0:T(8,128)(2,1)S(1)} %mine.1), channel_id=1, source_target_pairs={{0,32},{1,97},{32,64},{33,1},{64,96},{65,33},{96,0},{97,65},{2,34}... | collective-permute-start | bytes 1572872 | tf_op jit(solution)/shard_map/ppermute | solution.py:347
  64.1 15.0 %collective-permute-start.7 = (bf16[64,16,256]{2,1,0:T(8,128)(2,1)S(1)}, bf16[64,16,256]{2,1,0:T(8,128)(2,1)S(1)}, u32[]{:S(2)}, u32[]{:S(2)}) collective-permute-start(bf16[64,16,256]{2,1,0:T(8,128)(2,1)S(1)} %mine.1), channel_id=1, source_target_pairs={{0,2},{1,7},{2,4},{3,1},{4,6},{5,3},{6,0},{7,5},{8,10},{9,15},{10,... | collective-permute-start | bytes 1572872 | tf_op jit(solution)/shard_map/ppermute | solution.py:347
  65.0 16.7 %collective-permute-start.6 = (bf16[64,16,384]{2,1,0:T(8,128)(2,1)S(1)}, bf16[64,16,384]{2,1,0:T(8,128)(2,1)S(1)}, u32[]{:S(2)}, u32[]{:S(2)}) collective-permute-start(bf16[64,16,384]{2,1,0:T(8,128)(2,1)S(1)} %all_to_all.11.blocks_ref), channel_id=1, source_target_pairs={{0,1},{1,0},{2,3},{3,2},{4,5},{5,4},{6,7},{7,6},{8,9},{9,8},{10,11... | collective-permute-start | bytes 2359304 | tf_op jit(solution)/shard_map/ppermute | solution.py:342
  71.6 10.1 %collective-permute-start.12 = (bf16[64,16,256]{2,1,0:T(8,128)(2,1)S(1)}, bf16[64,16,256]{2,1,0:T(8,128)(2,1)S(1)}, u32[]{:S(2)}, u32[]{:S(2)}) collective-permute-start(bf16[64,16,256]{2,1,0:T(8,128)(2,1)S(1)} %collective-permute-done.11.z_ref), channel_id=1, source_target_pairs={{0,1},{1,0},{2,3},{3,2},{4,5},{5,4},{6,7},{7,6},{8,9},{9,8},{10,11... | collective-permute-start | bytes 1572872 | tf_op jit(solution)/shard_map/ppermute | solution.py:342
  78.4 3.2 %collective-permute-start.10 = (bf16[64,16,256]{2,1,0:T(8,128)(2,1)S(1)}, bf16[64,16,256]{2,1,0:T(8,128)(2,1)S(1)}, u32[]{:S(2)}, u32[]{:S(2)}) collective-permute-start(bf16[64,16,256]{2,1,0:T(8,128)(2,1)S(1)} %collective-permute-done.9.y_ref), channel_id=1, source_target_pairs={{0,1},{1,0},{2,3},{3,2},{4,5},{5,4},{6,7},{7,6},{8,9},{9,8},{10,11... | collective-permute-start | bytes 1572872 | tf_op jit(solution)/shard_map/ppermute | solution.py:342
  79.1 2.6 %collective-permute-start.8 = (bf16[64,16,256]{2,1,0:T(8,128)(2,1)S(1)}, bf16[64,16,256]{2,1,0:T(8,128)(2,1)S(1)}, u32[]{:S(2)}, u32[]{:S(2)}) collective-permute-start(bf16[64,16,256]{2,1,0:T(8,128)(2,1)S(1)} %collective-permute-done.7.x_ref), channel_id=1, source_target_pairs={{0,1},{1,0},{2,3},{3,2},{4,5},{5,4},{6,7},{7,6},{8,9},{9,8},{10,11... | collective-permute-start | bytes 1572872 | tf_op jit(solution)/shard_map/ppermute | solution.py:342
  79.1 2.6 %collective-permute-start.13 = (f32[8,4096]{1,0:T(8,128)S(1)}, f32[8,4096]{1,0:T(8,128)S(1)}, u32[]{:S(2)}, u32[]{:S(2)}) collective-permute-start(f32[8,4096]{1,0:T(8,128)S(1)} %get-tuple-element.29), channel_id=1, source_target_pairs={{0,1},{1,0},{2,3},{3,2},{4,5},{5,4},{6,7},{7,6},{8,9},{9,8},{10,11... | collective-permute-start | bytes 393224 | tf_op jit(solution)/shard_map/ppermute | solution.py:342

commit v7 on v6

--- a/solution.py
+++ b/solution.py
@@ -343,7 +343,7 @@
 
 
 def to_neighbours(values):
-    pairs = [(2 * p + c, 2 * ((p + 1 + 2 * c) % 4) + c) for p in range(4) for c in range(2)]
+    pairs = [(2 * p + c, 2 * ((p + 3 - 2 * c) % 4) + c) for p in range(4) for c in range(2)]
     return [lax.ppermute(value, (axis, "core"), pairs) for axis, value in zip("xyz", values)]
 
 

time: 83.7 us -> 82.1 us (0.981)
  waiting for transfers between devices: 11.8 us -> 6.78 us
  blocking collectives: 37.4 us -> 39.6 us
  starting transfers between devices: 25.8 us -> 27 us
    ppermute x7, starting transfers between devices: 13.9 us -> 21.7 us  [swapped(): return lax.ppermute(value, 'core', [(0, 1), (1, 0)])]
    ppermute x6, starting transfers between devices: 11.2 us -> 4.69 us  [to_neighbours(): lax.ppermute(value, (axis, 'core'), pairs)]
    ppermute x6, waiting for transfers between devices: 6.72 us -> 2.4 us  [to_neighbours(): lax.ppermute(value, (axis, 'core'), pairs)]
    all_to_all x1, blocking collectives: 20.3 us -> 22.8 us  [body(): partial = lax.all_to_all(partial, CHIPS, 0, 0, tiled=True)]
  transfers between devices with their start and end apart: 14 -> 14, of which waited for: 6 -> 5; matrix products, arithmetic and copies ran while one was open for 0% -> 0% of each run, Pallas kernels for 2% -> 2%
where the time goes in v7:
time: 82.1 us; the launch traced here: 81.9 us
  blocking collectives  39.6 us (48%)
  starting transfers between devices  27 us (33%)
  waiting for transfers between devices  6.78 us (8%)
  Pallas kernels  5.7 us (7%)
  local copies, waits for them, and re-layouts  1.98 us (2%)
    all_to_all x1, blocking collectives, body(): partial = lax.all_to_all(partial, CHIPS, 0, 0, tiled=True)  22.8 us
    ppermute x7, starting transfers between devices, swapped(): return lax.ppermute(value, 'core', [(0, 1), (1, 0)])  21.7 us
    all_to_all x1, blocking collectives, body(): blocks = lax.all_to_all(payload, CHIPS, 0, 0, tiled=True)  16.8 us
    ppermute x6, starting transfers between devices, to_neighbours(): lax.ppermute(value, (axis, 'core'), pairs)  4.69 us
    ppermute x7, waiting for transfers between devices, swapped(): return lax.ppermute(value, 'core', [(0, 1), (1, 0)])  4.38 us
    ppermute x6, waiting for transfers between devices, to_neighbours(): lax.ppermute(value, (axis, 'core'), pairs)  2.4 us
    dynamic_slice x1, local copies, waits for them, and re-layouts, body(): got = swapped(lax.dynamic_slice(grads, (0, (1 - core) * HALF), (256, HALF)))  1.95 us
    pallas_call x1, Pallas kernels, body(): pl.pallas_call(place_other_kernel, in_specs=[vmem] * 5 + [hbm] + [vmem] *...  1.81 us
  transfers between devices with their start and end apart: 14, of which 5 were waited for; matrix products, arithmetic and copies ran while one was open for 0% of the time, Pallas kernels for 2%

profile of v7, /device:TPU:1, one launch (start us, length us, event | category | flops | bytes accessed | tf_op | source)
XLA Modules:
  0.0 81.9 jit_solution(11242261799065931538)
XLA Ops:
  0.7 2.0 %dynamic-slice_bitcast_fusion = bf16[256,4096]{1,0:T(8,128)(2,1)S(1)} fusion(bf16[1,1,256,8192]{3,2,1,0:T(8,128)(2,1)} %param.5, s32[]{:T(128)S(6)} %select_n.3), kind=kLoop, calls=%fused_computation | loop fusion | bytes 4194308 | tf_op jit(solution)/shard_map/dynamic_slice | solution.py:360
  2.6 1.5 %collective-permute-start = (bf16[256,4096]{1,0:T(8,128)(2,1)S(1)}, bf16[256,4096]{1,0:T(8,128)(2,1)S(1)}, u32[]{:S(2)}, u32[]{:S(2)}) collective-permute-start(bf16[256,4096]{1,0:T(8,128)(2,1)S(1)} %dynamic-slice_bitcast_fusion), channel_id=1, source_target_pairs={{0,1},{1,0},{2,3},{3,2},{4,5},{5,4},{6,7},{7,6},{8,9},{9,8},{10,11... | collective-permute-start | bytes 6291464 | tf_op jit(solution)/shard_map/ppermute | solution.py:342
  4.2 0.7 collective-permute-start.1
  4.9 3.1 %collective-permute-done.got_ref = bf16[256,4096]{1,0:T(8,128)(2,1)S(1)} collective-permute-done((bf16[256,4096]{1,0:T(8,128)(2,1)S(1)}, bf16[256,4096]{1,0:T(8,128)(2,1)S(1)}, u32[]{:S(2)}, u32[]{:S(2)}) %collective-permute-start) | collective-permute-done | bytes 2097184 | tf_op jit(solution)/shard_map/ppermute | solution.py:342
  7.9 0.9 %add_blocks.1 = (bf16[64,16,256]{2,1,0:T(8,128)(2,1)S(1)}, bf16[64,16,256]{2,1,0:T(8,128)(2,1)S(1)}, bf16[64,16,256]{2,1,0:T(8,128)(2,1)S(1)}, bf16[64,16,256]{2,1,0:T(8,128)(2,1)S(1)}) custom-call(bf16[256,8192]{1,0:T(8,128)(2,1)S(1)} %bitcast.8, bf16[256,4096]{1,0:T(8,128)(2,1)S(1)} %collective-permute-done.got_ref, ...), custom_call_target="tpu_custom_call" | custom-call | tf_op jit(solution)/shard_map/add_blocks/pallas_call | solution.py:371
  8.9 1.4 %collective-permute-start.2 = (bf16[64,16,256]{2,1,0:T(8,128)(2,1)S(1)}, bf16[64,16,256]{2,1,0:T(8,128)(2,1)S(1)}, u32[]{:S(2)}, u32[]{:S(2)}) collective-permute-start(bf16[64,16,256]{2,1,0:T(8,128)(2,1)S(1)} %get-tuple-element.19), channel_id=1, source_target_pairs={{0,6},{1,3},{2,0},{3,5},{4,2},{5,7},{6,4},{7,1},{8,14},{9,11},{10,... | collective-permute-start | bytes 1572872 | tf_op jit(solution)/shard_map/ppermute | solution.py:347
  10.2 1.3 %collective-permute-start.3 = (bf16[64,16,256]{2,1,0:T(8,128)(2,1)S(1)}, bf16[64,16,256]{2,1,0:T(8,128)(2,1)S(1)}, u32[]{:S(2)}, u32[]{:S(2)}) collective-permute-start(bf16[64,16,256]{2,1,0:T(8,128)(2,1)S(1)} %get-tuple-element.20), channel_id=1, source_target_pairs={{0,96},{1,33},{32,0},{33,65},{64,32},{65,97},{96,64},{97,1},{2,98}... | collective-permute-start | bytes 1572872 | tf_op jit(solution)/shard_map/ppermute | solution.py:347
  11.5 1.6 %collective-permute-start.4 = (bf16[64,16,256]{2,1,0:T(8,128)(2,1)S(1)}, bf16[64,16,256]{2,1,0:T(8,128)(2,1)S(1)}, u32[]{:S(2)}, u32[]{:S(2)}) collective-permute-start(bf16[64,16,256]{2,1,0:T(8,128)(2,1)S(1)} %get-tuple-element.21), channel_id=1, source_target_pairs={{0,24},{1,9},{8,0},{9,17},{16,8},{17,25},{24,16},{25,1},{2,26},{3,... | collective-permute-start | bytes 1572872 | tf_op jit(solution)/shard_map/ppermute | solution.py:347
  13.2 7.1 %collective-permute-start.5 = (f32[16,4096]{1,0:T(8,128)S(1)}, f32[16,4096]{1,0:T(8,128)S(1)}, u32[]{:S(2)}, u32[]{:S(2)}) collective-permute-start(f32[16,4096]{1,0:T(8,128)S(1)} %pair.1), channel_id=1, source_target_pairs={{0,1},{1,0},{2,3},{3,2},{4,5},{5,4},{6,7},{7,6},{8,9},{9,8},{10,11... | collective-permute-start | bytes 786440 | tf_op jit(solution)/shard_map/ppermute | solution.py:342
  20.4 1.2 %collective-permute-done.5.pair_ref = f32[16,4096]{1,0:T(8,128)S(1)} collective-permute-done((f32[16,4096]{1,0:T(8,128)S(1)}, f32[16,4096]{1,0:T(8,128)S(1)}, u32[]{:S(2)}, u32[]{:S(2)}) %collective-permute-start.5) | collective-permute-done | bytes 262176 | tf_op jit(solution)/shard_map/ppermute | solution.py:342
  21.5 0.3 collective-permute-done.4.z_ref
  21.9 0.5 merge.1
  22.3 22.8 %all_to_all.10.parts_ref = bf16[64,16,384]{2,1,0:T(8,128)(2,1)S(1)} all-to-all(bf16[64,16,384]{2,1,0:T(8,128)(2,1)S(1)} %get-tuple-element.22), channel_id=1, replica_groups=mesh['y'=4,'z'=4,'x'=4,'core'=2] {'y','z','x'}, dimensions={0} | all-to-all | bytes 1572864 | tf_op jit(solution)/shard_map/all_to_all | solution.py:398
  45.1 0.8 adam.1
  45.9 16.8 %all_to_all.11.blocks_ref = bf16[64,16,384]{2,1,0:T(8,128)(2,1)S(1)} all-to-all(bf16[64,16,384]{2,1,0:T(8,128)(2,1)S(1)} %get-tuple-element.24), channel_id=1, replica_groups=mesh['y'=4,'z'=4,'x'=4,'core'=2] {'y','z','x'}, dimensions={0} | all-to-all | bytes 1572864 | tf_op jit(solution)/shard_map/all_to_all | solution.py:414
  62.9 0.3 collective-permute-start.9
  63.2 7.0 %collective-permute-start.6 = (bf16[64,16,384]{2,1,0:T(8,128)(2,1)S(1)}, bf16[64,16,384]{2,1,0:T(8,128)(2,1)S(1)}, u32[]{:S(2)}, u32[]{:S(2)}) collective-permute-start(bf16[64,16,384]{2,1,0:T(8,128)(2,1)S(1)} %all_to_all.11.blocks_ref), channel_id=1, source_target_pairs={{0,1},{1,0},{2,3},{3,2},{4,5},{5,4},{6,7},{7,6},{8,9},{9,8},{10,11... | collective-permute-start | bytes 2359304 | tf_op jit(solution)/shard_map/ppermute | solution.py:342
  70.2 2.1 %collective-permute-done.11.z_ref = bf16[64,16,256]{2,1,0:T(8,128)(2,1)S(1)} collective-permute-done((bf16[64,16,256]{2,1,0:T(8,128)(2,1)S(1)}, bf16[64,16,256]{2,1,0:T(8,128)(2,1)S(1)}, u32[]{:S(2)}, u32[]{:S(2)}) %collective-permute-start.11) | collective-permute-done | bytes 524320 | tf_op jit(solution)/shard_map/ppermute | solution.py:347
  72.2 4.5 %collective-permute-start.12 = (bf16[64,16,256]{2,1,0:T(8,128)(2,1)S(1)}, bf16[64,16,256]{2,1,0:T(8,128)(2,1)S(1)}, u32[]{:S(2)}, u32[]{:S(2)}) collective-permute-start(bf16[64,16,256]{2,1,0:T(8,128)(2,1)S(1)} %collective-permute-done.11.z_ref), channel_id=1, source_target_pairs={{0,1},{1,0},{2,3},{3,2},{4,5},{5,4},{6,7},{7,6},{8,9},{9,8},{10,11... | collective-permute-start | bytes 1572872 | tf_op jit(solution)/shard_map/ppermute | solution.py:342
  76.8 0.4 collective-permute-start.10
  77.2 1.1 %collective-permute-start.8 = (bf16[64,16,256]{2,1,0:T(8,128)(2,1)S(1)}, bf16[64,16,256]{2,1,0:T(8,128)(2,1)S(1)}, u32[]{:S(2)}, u32[]{:S(2)}) collective-permute-start(bf16[64,16,256]{2,1,0:T(8,128)(2,1)S(1)} %collective-permute-done.7.x_ref), channel_id=1, source_target_pairs={{0,1},{1,0},{2,3},{3,2},{4,5},{5,4},{6,7},{7,6},{8,9},{9,8},{10,11... | collective-permute-start | bytes 1572872 | tf_op jit(solution)/shard_map/ppermute | solution.py:342
  78.3 1.6 %place_own.1 = (bf16[256,8192]{1,0:T(8,128)(2,1)}, f32[3,2,4096]{2,1,0:T(2,128)S(1)}) custom-call(bf16[64,16,384]{2,1,0:T(8,128)(2,1)S(1)} %all_to_all.11.blocks_ref, bf16[64,16,256]{2,1,0:T(8,128)(2,1)S(1)} %collective-permute-done.7.x_ref, bf16[64,16,256]{2,1,0:T(8,128)(2,1)S(1)} %collective-permute-done.9.y_ref, ...), custom_call_target="tpu_custom_call" | custom-call | flops 8000000 | bytes 8000000 | tf_op jit(solution)/shard_map/place_own/pallas_call | solution.py:426
  79.9 0.2 collective-permute-done.13.refs_8_
  80.0 1.8 %place_other.1 = (bf16[256,8192]{1,0:T(8,128)(2,1)}, f32[3,2,8192]{2,1,0:T(2,128)}, f32[3,2,8192]{2,1,0:T(2,128)}) custom-call(bf16[64,16,384]{2,1,0:T(8,128)(2,1)S(1)} %collective-permute-done.6.refs_0_, bf16[64,16,256]{2,1,0:T(8,128)(2,1)S(1)} %collective-permute-done.8.refs_1_, ...), custom_call_target="tpu_custom_call", output_to_operand_aliasing={{0}: (5, {})} | custom-call | tf_op jit(solution)/shard_map/place_other/pallas_call | solution.py:436
  (25 shorter events, 0.3 us)
Async XLA Ops:
  0.6 3.5 %copy-start.2 = (f32[2,8192]{1,0:T(2,128)S(1)}, f32[2,8192]{1,0:T(2,128)}, u32[]{:S(2)}) copy-start(f32[2,8192]{1,0:T(2,128)} %first_ref.5) | copy-start | bytes 196612
  0.6 3.5 %copy-start.1 = (f32[2,8192]{1,0:T(2,128)S(1)}, f32[2,8192]{1,0:T(2,128)}, u32[]{:S(2)}) copy-start(f32[2,8192]{1,0:T(2,128)} %master_ref.5) | copy-start | bytes 196612
  0.7 7.3 %copy-start = (bf16[1,1,256,8192]{3,2,1,0:T(8,128)(2,1)S(1)}, bf16[1,1,256,8192]{3,2,1,0:T(8,128)(2,1)}, u32[]{:S(2)}) copy-start(bf16[1,1,256,8192]{3,2,1,0:T(8,128)(2,1)} %param.5) | copy-start | bytes 12582916
  2.6 10.6 %copy-start.3 = (f32[2,8192]{1,0:T(2,128)S(1)}, f32[2,8192]{1,0:T(2,128)}, u32[]{:S(2)}) copy-start(f32[2,8192]{1,0:T(2,128)} %second_ref.3) | copy-start | bytes 196612
  2.6 5.3 %collective-permute-start = (bf16[256,4096]{1,0:T(8,128)(2,1)S(1)}, bf16[256,4096]{1,0:T(8,128)(2,1)S(1)}, u32[]{:S(2)}, u32[]{:S(2)}) collective-permute-start(bf16[256,4096]{1,0:T(8,128)(2,1)S(1)} %dynamic-slice_bitcast_fusion), channel_id=1, source_target_pairs={{0,1},{1,0},{2,3},{3,2},{4,5},{5,4},{6,7},{7,6},{8,9},{9,8},{10,11... | collective-permute-start | bytes 6291464 | tf_op jit(solution)/shard_map/ppermute | solution.py:342
  4.2 0.7 collective-permute-start.1
  7.9 37.2 %copy-start.4 = (s32[64]{0:T(128)S(1)}, s32[64]{0:T(128)}, u32[]{:S(2)}) copy-start(s32[64]{0:T(128)} %param.9) | copy-start | bytes 772
  8.9 12.7 %collective-permute-start.2 = (bf16[64,16,256]{2,1,0:T(8,128)(2,1)S(1)}, bf16[64,16,256]{2,1,0:T(8,128)(2,1)S(1)}, u32[]{:S(2)}, u32[]{:S(2)}) collective-permute-start(bf16[64,16,256]{2,1,0:T(8,128)(2,1)S(1)} %get-tuple-element.19), channel_id=1, source_target_pairs={{0,6},{1,3},{2,0},{3,5},{4,2},{5,7},{6,4},{7,1},{8,14},{9,11},{10,... | collective-permute-start | bytes 1572872 | tf_op jit(solution)/shard_map/ppermute | solution.py:347
  10.2 11.3 %collective-permute-start.3 = (bf16[64,16,256]{2,1,0:T(8,128)(2,1)S(1)}, bf16[64,16,256]{2,1,0:T(8,128)(2,1)S(1)}, u32[]{:S(2)}, u32[]{:S(2)}) collective-permute-start(bf16[64,16,256]{2,1,0:T(8,128)(2,1)S(1)} %get-tuple-element.20), channel_id=1, source_target_pairs={{0,96},{1,33},{32,0},{33,65},{64,32},{65,97},{96,64},{97,1},{2,98}... | collective-permute-start | bytes 1572872 | tf_op jit(solution)/shard_map/ppermute | solution.py:347
  11.5 10.3 %collective-permute-start.4 = (bf16[64,16,256]{2,1,0:T(8,128)(2,1)S(1)}, bf16[64,16,256]{2,1,0:T(8,128)(2,1)S(1)}, u32[]{:S(2)}, u32[]{:S(2)}) collective-permute-start(bf16[64,16,256]{2,1,0:T(8,128)(2,1)S(1)} %get-tuple-element.21), channel_id=1, source_target_pairs={{0,24},{1,9},{8,0},{9,17},{16,8},{17,25},{24,16},{25,1},{2,26},{3,... | collective-permute-start | bytes 1572872 | tf_op jit(solution)/shard_map/ppermute | solution.py:347
  13.2 8.3 %collective-permute-start.5 = (f32[16,4096]{1,0:T(8,128)S(1)}, f32[16,4096]{1,0:T(8,128)S(1)}, u32[]{:S(2)}, u32[]{:S(2)}) collective-permute-start(f32[16,4096]{1,0:T(8,128)S(1)} %pair.1), channel_id=1, source_target_pairs={{0,1},{1,0},{2,3},{3,2},{4,5},{5,4},{6,7},{7,6},{8,9},{9,8},{10,11... | collective-permute-start | bytes 786440 | tf_op jit(solution)/shard_map/ppermute | solution.py:342
  62.8 9.5 %collective-permute-start.11 = (bf16[64,16,256]{2,1,0:T(8,128)(2,1)S(1)}, bf16[64,16,256]{2,1,0:T(8,128)(2,1)S(1)}, u32[]{:S(2)}, u32[]{:S(2)}) collective-permute-start(bf16[64,16,256]{2,1,0:T(8,128)(2,1)S(1)} %mine.1), channel_id=1, source_target_pairs={{0,24},{1,9},{8,0},{9,17},{16,8},{17,25},{24,16},{25,1},{2,26},{3,... | collective-permute-start | bytes 1572872 | tf_op jit(solution)/shard_map/ppermute | solution.py:347
  62.9 13.9 %collective-permute-start.9 = (bf16[64,16,256]{2,1,0:T(8,128)(2,1)S(1)}, bf16[64,16,256]{2,1,0:T(8,128)(2,1)S(1)}, u32[]{:S(2)}, u32[]{:S(2)}) collective-permute-start(bf16[64,16,256]{2,1,0:T(8,128)(2,1)S(1)} %mine.1), channel_id=1, source_target_pairs={{0,96},{1,33},{32,0},{33,65},{64,32},{65,97},{96,64},{97,1},{2,98}... | collective-permute-start | bytes 1572872 | tf_op jit(solution)/shard_map/ppermute | solution.py:347
  63.1 14.0 %collective-permute-start.7 = (bf16[64,16,256]{2,1,0:T(8,128)(2,1)S(1)}, bf16[64,16,256]{2,1,0:T(8,128)(2,1)S(1)}, u32[]{:S(2)}, u32[]{:S(2)}) collective-permute-start(bf16[64,16,256]{2,1,0:T(8,128)(2,1)S(1)} %mine.1), channel_id=1, source_target_pairs={{0,6},{1,3},{2,0},{3,5},{4,2},{5,7},{6,4},{7,1},{8,14},{9,11},{10,... | collective-permute-start | bytes 1572872 | tf_op jit(solution)/shard_map/ppermute | solution.py:347
  63.2 16.9 %collective-permute-start.6 = (bf16[64,16,384]{2,1,0:T(8,128)(2,1)S(1)}, bf16[64,16,384]{2,1,0:T(8,128)(2,1)S(1)}, u32[]{:S(2)}, u32[]{:S(2)}) collective-permute-start(bf16[64,16,384]{2,1,0:T(8,128)(2,1)S(1)} %all_to_all.11.blocks_ref), channel_id=1, source_target_pairs={{0,1},{1,0},{2,3},{3,2},{4,5},{5,4},{6,7},{7,6},{8,9},{9,8},{10,11... | collective-permute-start | bytes 2359304 | tf_op jit(solution)/shard_map/ppermute | solution.py:342
  72.2 7.8 %collective-permute-start.12 = (bf16[64,16,256]{2,1,0:T(8,128)(2,1)S(1)}, bf16[64,16,256]{2,1,0:T(8,128)(2,1)S(1)}, u32[]{:S(2)}, u32[]{:S(2)}) collective-permute-start(bf16[64,16,256]{2,1,0:T(8,128)(2,1)S(1)} %collective-permute-done.11.z_ref), channel_id=1, source_target_pairs={{0,1},{1,0},{2,3},{3,2},{4,5},{5,4},{6,7},{7,6},{8,9},{9,8},{10,11... | collective-permute-start | bytes 1572872 | tf_op jit(solution)/shard_map/ppermute | solution.py:342
  76.8 3.3 %collective-permute-start.10 = (bf16[64,16,256]{2,1,0:T(8,128)(2,1)S(1)}, bf16[64,16,256]{2,1,0:T(8,128)(2,1)S(1)}, u32[]{:S(2)}, u32[]{:S(2)}) collective-permute-start(bf16[64,16,256]{2,1,0:T(8,128)(2,1)S(1)} %collective-permute-done.9.y_ref), channel_id=1, source_target_pairs={{0,1},{1,0},{2,3},{3,2},{4,5},{5,4},{6,7},{7,6},{8,9},{9,8},{10,11... | collective-permute-start | bytes 1572872 | tf_op jit(solution)/shard_map/ppermute | solution.py:342
  77.2 2.9 %collective-permute-start.8 = (bf16[64,16,256]{2,1,0:T(8,128)(2,1)S(1)}, bf16[64,16,256]{2,1,0:T(8,128)(2,1)S(1)}, u32[]{:S(2)}, u32[]{:S(2)}) collective-permute-start(bf16[64,16,256]{2,1,0:T(8,128)(2,1)S(1)} %collective-permute-done.7.x_ref), channel_id=1, source_target_pairs={{0,1},{1,0},{2,3},{3,2},{4,5},{5,4},{6,7},{7,6},{8,9},{9,8},{10,11... | collective-permute-start | bytes 1572872 | tf_op jit(solution)/shard_map/ppermute | solution.py:342
  78.3 1.7 %collective-permute-start.13 = (f32[8,4096]{1,0:T(8,128)S(1)}, f32[8,4096]{1,0:T(8,128)S(1)}, u32[]{:S(2)}, u32[]{:S(2)}) collective-permute-start(f32[8,4096]{1,0:T(8,128)S(1)} %get-tuple-element.29), channel_id=1, source_target_pairs={{0,1},{1,0},{2,3},{3,2},{4,5},{5,4},{6,7},{7,6},{8,9},{9,8},{10,11... | collective-permute-start | bytes 393224 | tf_op jit(solution)/shard_map/ppermute | solution.py:342

commit v8 on v7

--- a/solution.py
+++ b/solution.py
@@ -98,7 +98,7 @@
                     ref[chip] = jnp.concatenate(block, axis=0).astype(BF)
         return carry
 
-    lax.fori_loop(0, 12, kept, 0)
+    lax.fori_loop(0, 12, kept, 0, unroll=6)
 
     def leave(q, carry):
         for axis, ref in enumerate(pieces):
@@ -107,7 +107,7 @@
             ref[48 + q] = total.astype(BF)
         return carry
 
-    lax.fori_loop(0, 16, leave, 0, unroll=4)
+    lax.fori_loop(0, 16, leave, 0, unroll=16)
 
 
 def merge_kernel(
@@ -123,7 +123,7 @@
         out_ref[d, :, 0:256] = total.astype(BF)
         return carry
 
-    lax.fori_loop(0, 64, add, 0, unroll=8)
+    lax.fori_loop(0, 64, add, 0, unroll=16)
 
     old_ref[12:16, :] = jnp.zeros((4, HALF), F32)
     for mine in range(2):
@@ -153,7 +153,7 @@
         out_ref[48 + q, :, 256:384] = jnp.concatenate([parts[:, 0:128], parts[:, 128:256]], axis=0).astype(BF)
         return carry
 
-    lax.fori_loop(0, 16, leave, 0, unroll=4)
+    lax.fori_loop(0, 16, leave, 0, unroll=16)
 
 
 def adam_kernel(parts_ref, chip_ref, owner_ref, out_ref, own_ref, other_ref, key_ref, old_ref):
@@ -292,7 +292,7 @@
                     2 * i : 2 * i + 2, q * 128 : (q + 1) * 128
                 ]
     adopted_ready()
-    lax.fori_loop(0, 6, kept, 0)
+    lax.fori_loop(0, 6, kept, 0, unroll=6)
     for i in range(8):
         store(i).wait()
 

time: 82.1 us -> 81.6 us (level)
  no operation moved by 1% of the time
where the time goes in v8:
time: 81.6 us; the launch traced here: 81.4 us
  blocking collectives  39.6 us (49%)
  starting transfers between devices  27.1 us (33%)
  waiting for transfers between devices  6.91 us (8%)
  Pallas kernels  5.11 us (6%)
  local copies, waits for them, and re-layouts  1.98 us (2%)
    all_to_all x1, blocking collectives, body(): partial = lax.all_to_all(partial, CHIPS, 0, 0, tiled=True)  22.8 us
    ppermute x7, starting transfers between devices, swapped(): return lax.ppermute(value, 'core', [(0, 1), (1, 0)])  21.7 us
    all_to_all x1, blocking collectives, body(): blocks = lax.all_to_all(payload, CHIPS, 0, 0, tiled=True)  16.8 us
    ppermute x6, starting transfers between devices, to_neighbours(): lax.ppermute(value, (axis, 'core'), pairs)  4.69 us
    ppermute x7, waiting for transfers between devices, swapped(): return lax.ppermute(value, 'core', [(0, 1), (1, 0)])  4.51 us
    ppermute x6, waiting for transfers between devices, to_neighbours(): lax.ppermute(value, (axis, 'core'), pairs)  2.4 us
    dynamic_slice x1, local copies, waits for them, and re-layouts, body(): got = swapped(lax.dynamic_slice(grads, (0, (1 - core) * HALF), (256, HALF)))  1.95 us
  transfers between devices with their start and end apart: 14, of which 5 were waited for; matrix products, arithmetic and copies ran while one was open for 0% of the time, Pallas kernels for 2%

profile of v8, /device:TPU:1, one launch (start us, length us, event | category | flops | bytes accessed | tf_op | source)
XLA Modules:
  0.0 81.4 jit_solution(4732594145013773568)
XLA Ops:
  0.7 2.0 %dynamic-slice_bitcast_fusion = bf16[256,4096]{1,0:T(8,128)(2,1)S(1)} fusion(bf16[1,1,256,8192]{3,2,1,0:T(8,128)(2,1)} %param.5, s32[]{:T(128)S(6)} %select_n.3), kind=kLoop, calls=%fused_computation | loop fusion | bytes 4194308 | tf_op jit(solution)/shard_map/dynamic_slice | solution.py:360
  2.6 1.5 %collective-permute-start = (bf16[256,4096]{1,0:T(8,128)(2,1)S(1)}, bf16[256,4096]{1,0:T(8,128)(2,1)S(1)}, u32[]{:S(2)}, u32[]{:S(2)}) collective-permute-start(bf16[256,4096]{1,0:T(8,128)(2,1)S(1)} %dynamic-slice_bitcast_fusion), channel_id=1, source_target_pairs={{0,1},{1,0},{2,3},{3,2},{4,5},{5,4},{6,7},{7,6},{8,9},{9,8},{10,11... | collective-permute-start | bytes 6291464 | tf_op jit(solution)/shard_map/ppermute | solution.py:342
  4.2 0.7 collective-permute-start.1
  4.9 3.1 %collective-permute-done.got_ref = bf16[256,4096]{1,0:T(8,128)(2,1)S(1)} collective-permute-done((bf16[256,4096]{1,0:T(8,128)(2,1)S(1)}, bf16[256,4096]{1,0:T(8,128)(2,1)S(1)}, u32[]{:S(2)}, u32[]{:S(2)}) %collective-permute-start) | collective-permute-done | bytes 2097184 | tf_op jit(solution)/shard_map/ppermute | solution.py:342
  7.9 0.8 add_blocks.1
  8.7 1.4 %collective-permute-start.2 = (bf16[64,16,256]{2,1,0:T(8,128)(2,1)S(1)}, bf16[64,16,256]{2,1,0:T(8,128)(2,1)S(1)}, u32[]{:S(2)}, u32[]{:S(2)}) collective-permute-start(bf16[64,16,256]{2,1,0:T(8,128)(2,1)S(1)} %get-tuple-element.19), channel_id=1, source_target_pairs={{0,6},{1,3},{2,0},{3,5},{4,2},{5,7},{6,4},{7,1},{8,14},{9,11},{10,... | collective-permute-start | bytes 1572872 | tf_op jit(solution)/shard_map/ppermute | solution.py:347
  10.1 1.3 %collective-permute-start.3 = (bf16[64,16,256]{2,1,0:T(8,128)(2,1)S(1)}, bf16[64,16,256]{2,1,0:T(8,128)(2,1)S(1)}, u32[]{:S(2)}, u32[]{:S(2)}) collective-permute-start(bf16[64,16,256]{2,1,0:T(8,128)(2,1)S(1)} %get-tuple-element.20), channel_id=1, source_target_pairs={{0,96},{1,33},{32,0},{33,65},{64,32},{65,97},{96,64},{97,1},{2,98}... | collective-permute-start | bytes 1572872 | tf_op jit(solution)/shard_map/ppermute | solution.py:347
  11.4 1.6 %collective-permute-start.4 = (bf16[64,16,256]{2,1,0:T(8,128)(2,1)S(1)}, bf16[64,16,256]{2,1,0:T(8,128)(2,1)S(1)}, u32[]{:S(2)}, u32[]{:S(2)}) collective-permute-start(bf16[64,16,256]{2,1,0:T(8,128)(2,1)S(1)} %get-tuple-element.21), channel_id=1, source_target_pairs={{0,24},{1,9},{8,0},{9,17},{16,8},{17,25},{24,16},{25,1},{2,26},{3,... | collective-permute-start | bytes 1572872 | tf_op jit(solution)/shard_map/ppermute | solution.py:347
  13.0 7.1 %collective-permute-start.5 = (f32[16,4096]{1,0:T(8,128)S(1)}, f32[16,4096]{1,0:T(8,128)S(1)}, u32[]{:S(2)}, u32[]{:S(2)}) collective-permute-start(f32[16,4096]{1,0:T(8,128)S(1)} %pair.1), channel_id=1, source_target_pairs={{0,1},{1,0},{2,3},{3,2},{4,5},{5,4},{6,7},{7,6},{8,9},{9,8},{10,11... | collective-permute-start | bytes 786440 | tf_op jit(solution)/shard_map/ppermute | solution.py:342
  20.2 1.2 %collective-permute-done.5.pair_ref = f32[16,4096]{1,0:T(8,128)S(1)} collective-permute-done((f32[16,4096]{1,0:T(8,128)S(1)}, f32[16,4096]{1,0:T(8,128)S(1)}, u32[]{:S(2)}, u32[]{:S(2)}) %collective-permute-start.5) | collective-permute-done | bytes 262176 | tf_op jit(solution)/shard_map/ppermute | solution.py:342
  21.4 0.3 collective-permute-done.4.z_ref
  21.7 0.4 merge.1
  22.1 22.8 %all_to_all.10.parts_ref = bf16[64,16,384]{2,1,0:T(8,128)(2,1)S(1)} all-to-all(bf16[64,16,384]{2,1,0:T(8,128)(2,1)S(1)} %get-tuple-element.22), channel_id=1, replica_groups=mesh['y'=4,'z'=4,'x'=4,'core'=2] {'y','z','x'}, dimensions={0} | all-to-all | bytes 1572864 | tf_op jit(solution)/shard_map/all_to_all | solution.py:398
  44.9 0.8 adam.1
  45.7 16.8 %all_to_all.11.blocks_ref = bf16[64,16,384]{2,1,0:T(8,128)(2,1)S(1)} all-to-all(bf16[64,16,384]{2,1,0:T(8,128)(2,1)S(1)} %get-tuple-element.24), channel_id=1, replica_groups=mesh['y'=4,'z'=4,'x'=4,'core'=2] {'y','z','x'}, dimensions={0} | all-to-all | bytes 1572864 | tf_op jit(solution)/shard_map/all_to_all | solution.py:414
  62.6 0.3 collective-permute-start.9
  62.9 7.0 %collective-permute-start.6 = (bf16[64,16,384]{2,1,0:T(8,128)(2,1)S(1)}, bf16[64,16,384]{2,1,0:T(8,128)(2,1)S(1)}, u32[]{:S(2)}, u32[]{:S(2)}) collective-permute-start(bf16[64,16,384]{2,1,0:T(8,128)(2,1)S(1)} %all_to_all.11.blocks_ref), channel_id=1, source_target_pairs={{0,1},{1,0},{2,3},{3,2},{4,5},{5,4},{6,7},{7,6},{8,9},{9,8},{10,11... | collective-permute-start | bytes 2359304 | tf_op jit(solution)/shard_map/ppermute | solution.py:342
  69.9 2.1 %collective-permute-done.11.z_ref = bf16[64,16,256]{2,1,0:T(8,128)(2,1)S(1)} collective-permute-done((bf16[64,16,256]{2,1,0:T(8,128)(2,1)S(1)}, bf16[64,16,256]{2,1,0:T(8,128)(2,1)S(1)}, u32[]{:S(2)}, u32[]{:S(2)}) %collective-permute-start.11) | collective-permute-done | bytes 524320 | tf_op jit(solution)/shard_map/ppermute | solution.py:347
  72.0 4.5 %collective-permute-start.12 = (bf16[64,16,256]{2,1,0:T(8,128)(2,1)S(1)}, bf16[64,16,256]{2,1,0:T(8,128)(2,1)S(1)}, u32[]{:S(2)}, u32[]{:S(2)}) collective-permute-start(bf16[64,16,256]{2,1,0:T(8,128)(2,1)S(1)} %collective-permute-done.11.z_ref), channel_id=1, source_target_pairs={{0,1},{1,0},{2,3},{3,2},{4,5},{5,4},{6,7},{7,6},{8,9},{9,8},{10,11... | collective-permute-start | bytes 1572872 | tf_op jit(solution)/shard_map/ppermute | solution.py:342
  76.5 0.4 collective-permute-start.10
  76.9 1.1 %collective-permute-start.8 = (bf16[64,16,256]{2,1,0:T(8,128)(2,1)S(1)}, bf16[64,16,256]{2,1,0:T(8,128)(2,1)S(1)}, u32[]{:S(2)}, u32[]{:S(2)}) collective-permute-start(bf16[64,16,256]{2,1,0:T(8,128)(2,1)S(1)} %collective-permute-done.7.x_ref), channel_id=1, source_target_pairs={{0,1},{1,0},{2,3},{3,2},{4,5},{5,4},{6,7},{7,6},{8,9},{9,8},{10,11... | collective-permute-start | bytes 1572872 | tf_op jit(solution)/shard_map/ppermute | solution.py:342
  78.1 1.4 %place_own.1 = (bf16[256,8192]{1,0:T(8,128)(2,1)}, f32[3,2,4096]{2,1,0:T(2,128)S(1)}) custom-call(bf16[64,16,384]{2,1,0:T(8,128)(2,1)S(1)} %all_to_all.11.blocks_ref, bf16[64,16,256]{2,1,0:T(8,128)(2,1)S(1)} %collective-permute-done.7.x_ref, bf16[64,16,256]{2,1,0:T(8,128)(2,1)S(1)} %collective-permute-done.9.y_ref, ...), custom_call_target="tpu_custom_call" | custom-call | flops 8000000 | bytes 8000000 | tf_op jit(solution)/shard_map/place_own/pallas_call | solution.py:426
  79.5 0.3 collective-permute-done.13.refs_8_
  79.8 1.6 %place_other.1 = (bf16[256,8192]{1,0:T(8,128)(2,1)}, f32[3,2,8192]{2,1,0:T(2,128)}, f32[3,2,8192]{2,1,0:T(2,128)}) custom-call(bf16[64,16,384]{2,1,0:T(8,128)(2,1)S(1)} %collective-permute-done.6.refs_0_, bf16[64,16,256]{2,1,0:T(8,128)(2,1)S(1)} %collective-permute-done.8.refs_1_, ...), custom_call_target="tpu_custom_call", output_to_operand_aliasing={{0}: (5, {})} | custom-call | tf_op jit(solution)/shard_map/place_other/pallas_call | solution.py:436
  (25 shorter events, 0.3 us)
Async XLA Ops:
  0.6 3.5 %copy-start.2 = (f32[2,8192]{1,0:T(2,128)S(1)}, f32[2,8192]{1,0:T(2,128)}, u32[]{:S(2)}) copy-start(f32[2,8192]{1,0:T(2,128)} %first_ref.5) | copy-start | bytes 196612
  0.6 3.5 %copy-start.1 = (f32[2,8192]{1,0:T(2,128)S(1)}, f32[2,8192]{1,0:T(2,128)}, u32[]{:S(2)}) copy-start(f32[2,8192]{1,0:T(2,128)} %master_ref.5) | copy-start | bytes 196612
  0.7 7.3 %copy-start = (bf16[1,1,256,8192]{3,2,1,0:T(8,128)(2,1)S(1)}, bf16[1,1,256,8192]{3,2,1,0:T(8,128)(2,1)}, u32[]{:S(2)}) copy-start(bf16[1,1,256,8192]{3,2,1,0:T(8,128)(2,1)} %param.5) | copy-start | bytes 12582916
  2.6 10.4 %copy-start.3 = (f32[2,8192]{1,0:T(2,128)S(1)}, f32[2,8192]{1,0:T(2,128)}, u32[]{:S(2)}) copy-start(f32[2,8192]{1,0:T(2,128)} %second_ref.3) | copy-start | bytes 196612
  2.6 5.3 %collective-permute-start = (bf16[256,4096]{1,0:T(8,128)(2,1)S(1)}, bf16[256,4096]{1,0:T(8,128)(2,1)S(1)}, u32[]{:S(2)}, u32[]{:S(2)}) collective-permute-start(bf16[256,4096]{1,0:T(8,128)(2,1)S(1)} %dynamic-slice_bitcast_fusion), channel_id=1, source_target_pairs={{0,1},{1,0},{2,3},{3,2},{4,5},{5,4},{6,7},{7,6},{8,9},{9,8},{10,11... | collective-permute-start | bytes 6291464 | tf_op jit(solution)/shard_map/ppermute | solution.py:342
  4.2 0.7 collective-permute-start.1
  7.9 36.9 %copy-start.4 = (s32[64]{0:T(128)S(1)}, s32[64]{0:T(128)}, u32[]{:S(2)}) copy-start(s32[64]{0:T(128)} %param.9) | copy-start | bytes 772
  8.7 12.7 %collective-permute-start.2 = (bf16[64,16,256]{2,1,0:T(8,128)(2,1)S(1)}, bf16[64,16,256]{2,1,0:T(8,128)(2,1)S(1)}, u32[]{:S(2)}, u32[]{:S(2)}) collective-permute-start(bf16[64,16,256]{2,1,0:T(8,128)(2,1)S(1)} %get-tuple-element.19), channel_id=1, source_target_pairs={{0,6},{1,3},{2,0},{3,5},{4,2},{5,7},{6,4},{7,1},{8,14},{9,11},{10,... | collective-permute-start | bytes 1572872 | tf_op jit(solution)/shard_map/ppermute | solution.py:347
  10.1 11.3 %collective-permute-start.3 = (bf16[64,16,256]{2,1,0:T(8,128)(2,1)S(1)}, bf16[64,16,256]{2,1,0:T(8,128)(2,1)S(1)}, u32[]{:S(2)}, u32[]{:S(2)}) collective-permute-start(bf16[64,16,256]{2,1,0:T(8,128)(2,1)S(1)} %get-tuple-element.20), channel_id=1, source_target_pairs={{0,96},{1,33},{32,0},{33,65},{64,32},{65,97},{96,64},{97,1},{2,98}... | collective-permute-start | bytes 1572872 | tf_op jit(solution)/shard_map/ppermute | solution.py:347
  11.4 10.3 %collective-permute-start.4 = (bf16[64,16,256]{2,1,0:T(8,128)(2,1)S(1)}, bf16[64,16,256]{2,1,0:T(8,128)(2,1)S(1)}, u32[]{:S(2)}, u32[]{:S(2)}) collective-permute-start(bf16[64,16,256]{2,1,0:T(8,128)(2,1)S(1)} %get-tuple-element.21), channel_id=1, source_target_pairs={{0,24},{1,9},{8,0},{9,17},{16,8},{17,25},{24,16},{25,1},{2,26},{3,... | collective-permute-start | bytes 1572872 | tf_op jit(solution)/shard_map/ppermute | solution.py:347
  13.0 8.3 %collective-permute-start.5 = (f32[16,4096]{1,0:T(8,128)S(1)}, f32[16,4096]{1,0:T(8,128)S(1)}, u32[]{:S(2)}, u32[]{:S(2)}) collective-permute-start(f32[16,4096]{1,0:T(8,128)S(1)} %pair.1), channel_id=1, source_target_pairs={{0,1},{1,0},{2,3},{3,2},{4,5},{5,4},{6,7},{7,6},{8,9},{9,8},{10,11... | collective-permute-start | bytes 786440 | tf_op jit(solution)/shard_map/ppermute | solution.py:342
  62.5 9.5 %collective-permute-start.11 = (bf16[64,16,256]{2,1,0:T(8,128)(2,1)S(1)}, bf16[64,16,256]{2,1,0:T(8,128)(2,1)S(1)}, u32[]{:S(2)}, u32[]{:S(2)}) collective-permute-start(bf16[64,16,256]{2,1,0:T(8,128)(2,1)S(1)} %mine.1), channel_id=1, source_target_pairs={{0,24},{1,9},{8,0},{9,17},{16,8},{17,25},{24,16},{25,1},{2,26},{3,... | collective-permute-start | bytes 1572872 | tf_op jit(solution)/shard_map/ppermute | solution.py:347
  62.6 13.9 %collective-permute-start.9 = (bf16[64,16,256]{2,1,0:T(8,128)(2,1)S(1)}, bf16[64,16,256]{2,1,0:T(8,128)(2,1)S(1)}, u32[]{:S(2)}, u32[]{:S(2)}) collective-permute-start(bf16[64,16,256]{2,1,0:T(8,128)(2,1)S(1)} %mine.1), channel_id=1, source_target_pairs={{0,96},{1,33},{32,0},{33,65},{64,32},{65,97},{96,64},{97,1},{2,98}... | collective-permute-start | bytes 1572872 | tf_op jit(solution)/shard_map/ppermute | solution.py:347
  62.9 14.0 %collective-permute-start.7 = (bf16[64,16,256]{2,1,0:T(8,128)(2,1)S(1)}, bf16[64,16,256]{2,1,0:T(8,128)(2,1)S(1)}, u32[]{:S(2)}, u32[]{:S(2)}) collective-permute-start(bf16[64,16,256]{2,1,0:T(8,128)(2,1)S(1)} %mine.1), channel_id=1, source_target_pairs={{0,6},{1,3},{2,0},{3,5},{4,2},{5,7},{6,4},{7,1},{8,14},{9,11},{10,... | collective-permute-start | bytes 1572872 | tf_op jit(solution)/shard_map/ppermute | solution.py:347
  62.9 16.9 %collective-permute-start.6 = (bf16[64,16,384]{2,1,0:T(8,128)(2,1)S(1)}, bf16[64,16,384]{2,1,0:T(8,128)(2,1)S(1)}, u32[]{:S(2)}, u32[]{:S(2)}) collective-permute-start(bf16[64,16,384]{2,1,0:T(8,128)(2,1)S(1)} %all_to_all.11.blocks_ref), channel_id=1, source_target_pairs={{0,1},{1,0},{2,3},{3,2},{4,5},{5,4},{6,7},{7,6},{8,9},{9,8},{10,11... | collective-permute-start | bytes 2359304 | tf_op jit(solution)/shard_map/ppermute | solution.py:342
  72.0 7.8 %collective-permute-start.12 = (bf16[64,16,256]{2,1,0:T(8,128)(2,1)S(1)}, bf16[64,16,256]{2,1,0:T(8,128)(2,1)S(1)}, u32[]{:S(2)}, u32[]{:S(2)}) collective-permute-start(bf16[64,16,256]{2,1,0:T(8,128)(2,1)S(1)} %collective-permute-done.11.z_ref), channel_id=1, source_target_pairs={{0,1},{1,0},{2,3},{3,2},{4,5},{5,4},{6,7},{7,6},{8,9},{9,8},{10,11... | collective-permute-start | bytes 1572872 | tf_op jit(solution)/shard_map/ppermute | solution.py:342
  76.5 3.3 %collective-permute-start.10 = (bf16[64,16,256]{2,1,0:T(8,128)(2,1)S(1)}, bf16[64,16,256]{2,1,0:T(8,128)(2,1)S(1)}, u32[]{:S(2)}, u32[]{:S(2)}) collective-permute-start(bf16[64,16,256]{2,1,0:T(8,128)(2,1)S(1)} %collective-permute-done.9.y_ref), channel_id=1, source_target_pairs={{0,1},{1,0},{2,3},{3,2},{4,5},{5,4},{6,7},{7,6},{8,9},{9,8},{10,11... | collective-permute-start | bytes 1572872 | tf_op jit(solution)/shard_map/ppermute | solution.py:342
  76.9 2.9 %collective-permute-start.8 = (bf16[64,16,256]{2,1,0:T(8,128)(2,1)S(1)}, bf16[64,16,256]{2,1,0:T(8,128)(2,1)S(1)}, u32[]{:S(2)}, u32[]{:S(2)}) collective-permute-start(bf16[64,16,256]{2,1,0:T(8,128)(2,1)S(1)} %collective-permute-done.7.x_ref), channel_id=1, source_target_pairs={{0,1},{1,0},{2,3},{3,2},{4,5},{5,4},{6,7},{7,6},{8,9},{9,8},{10,11... | collective-permute-start | bytes 1572872 | tf_op jit(solution)/shard_map/ppermute | solution.py:342
  78.1 1.7 %collective-permute-start.13 = (f32[8,4096]{1,0:T(8,128)S(1)}, f32[8,4096]{1,0:T(8,128)S(1)}, u32[]{:S(2)}, u32[]{:S(2)}) collective-permute-start(f32[8,4096]{1,0:T(8,128)S(1)} %get-tuple-element.29), channel_id=1, source_target_pairs={{0,1},{1,0},{2,3},{3,2},{4,5},{5,4},{6,7},{7,6},{8,9},{9,8},{10,11... | collective-permute-start | bytes 393224 | tf_op jit(solution)/shard_map/ppermute | solution.py:342

commit v9 on v8

--- a/solution.py
+++ b/solution.py
@@ -57,7 +57,7 @@
 
 def pair_kernel(master_ref, first_ref, second_ref, passed_ref, pair_ref):
     other = columns(1 - lax.axis_index("core"))
-    pair_ref[...] = jnp.zeros_like(pair_ref)
+    pair_ref[6:8, :] = jnp.zeros((2, HALF), F32)
     for i, ref in enumerate((master_ref, first_ref, second_ref)):
         pair_ref[2 * i : 2 * i + 2, :] = ref[:, other]
     pair_ref[8:12, :] = passed_ref[:, other]
@@ -98,7 +98,7 @@
                     ref[chip] = jnp.concatenate(block, axis=0).astype(BF)
         return carry
 
-    lax.fori_loop(0, 12, kept, 0, unroll=6)
+    lax.fori_loop(0, 12, kept, 0, unroll=12)
 
     def leave(q, carry):
         for axis, ref in enumerate(pieces):
@@ -123,7 +123,7 @@
         out_ref[d, :, 0:256] = total.astype(BF)
         return carry
 
-    lax.fori_loop(0, 64, add, 0, unroll=16)
+    lax.fori_loop(0, 64, add, 0, unroll=64)
 
     old_ref[12:16, :] = jnp.zeros((4, HALF), F32)
     for mine in range(2):
@@ -380,7 +380,7 @@
         pair_kernel,
         in_specs=[vmem] * 4,
         out_specs=vmem,
-        out_shape=shape((16, HALF), F32),
+        out_shape=shape((12, HALF), F32),
         compiler_params=params(),
         name="pair",
     )(master, first, second, passed)

time: 81.6 us -> 81.5 us (level)
  no operation moved by 1% of the time
where the time goes in v9:
time: 81.5 us; the launch traced here: 81.3 us
  blocking collectives  39.6 us (49%)
  starting transfers between devices  26.9 us (33%)
  waiting for transfers between devices  6.97 us (9%)
  Pallas kernels  5.05 us (6%)
  local copies, waits for them, and re-layouts  1.98 us (2%)
    all_to_all x1, blocking collectives, body(): partial = lax.all_to_all(partial, CHIPS, 0, 0, tiled=True)  22.8 us
    ppermute x7, starting transfers between devices, swapped(): return lax.ppermute(value, 'core', [(0, 1), (1, 0)])  21.6 us
    all_to_all x1, blocking collectives, body(): blocks = lax.all_to_all(payload, CHIPS, 0, 0, tiled=True)  16.9 us
    ppermute x6, starting transfers between devices, to_neighbours(): lax.ppermute(value, (axis, 'core'), pairs)  4.64 us
    ppermute x7, waiting for transfers between devices, swapped(): return lax.ppermute(value, 'core', [(0, 1), (1, 0)])  4.51 us
    ppermute x6, waiting for transfers between devices, to_neighbours(): lax.ppermute(value, (axis, 'core'), pairs)  2.45 us
    dynamic_slice x1, local copies, waits for them, and re-layouts, body(): got = swapped(lax.dynamic_slice(grads, (0, (1 - core) * HALF), (256, HALF)))  1.95 us
  transfers between devices with their start and end apart: 14, of which 5 were waited for; matrix products, arithmetic and copies ran while one was open for 0% of the time, Pallas kernels for 2%

profile of v9, /device:TPU:1, one launch (start us, length us, event | category | flops | bytes accessed | tf_op | source)
XLA Modules:
  0.0 81.3 jit_solution(15705940557872783213)
XLA Ops:
  0.7 2.0 %dynamic-slice_bitcast_fusion = bf16[256,4096]{1,0:T(8,128)(2,1)S(1)} fusion(bf16[1,1,256,8192]{3,2,1,0:T(8,128)(2,1)} %param.5, s32[]{:T(128)S(6)} %select_n.3), kind=kLoop, calls=%fused_computation | loop fusion | bytes 4194308 | tf_op jit(solution)/shard_map/dynamic_slice | solution.py:360
  2.6 1.5 %collective-permute-start = (bf16[256,4096]{1,0:T(8,128)(2,1)S(1)}, bf16[256,4096]{1,0:T(8,128)(2,1)S(1)}, u32[]{:S(2)}, u32[]{:S(2)}) collective-permute-start(bf16[256,4096]{1,0:T(8,128)(2,1)S(1)} %dynamic-slice_bitcast_fusion), channel_id=1, source_target_pairs={{0,1},{1,0},{2,3},{3,2},{4,5},{5,4},{6,7},{7,6},{8,9},{9,8},{10,11... | collective-permute-start | bytes 6291464 | tf_op jit(solution)/shard_map/ppermute | solution.py:342
  4.2 0.7 collective-permute-start.1
  4.9 3.1 %collective-permute-done.got_ref = bf16[256,4096]{1,0:T(8,128)(2,1)S(1)} collective-permute-done((bf16[256,4096]{1,0:T(8,128)(2,1)S(1)}, bf16[256,4096]{1,0:T(8,128)(2,1)S(1)}, u32[]{:S(2)}, u32[]{:S(2)}) %collective-permute-start) | collective-permute-done | bytes 2097184 | tf_op jit(solution)/shard_map/ppermute | solution.py:342
  7.9 0.7 add_blocks.1
  8.7 1.4 %collective-permute-start.2 = (bf16[64,16,256]{2,1,0:T(8,128)(2,1)S(1)}, bf16[64,16,256]{2,1,0:T(8,128)(2,1)S(1)}, u32[]{:S(2)}, u32[]{:S(2)}) collective-permute-start(bf16[64,16,256]{2,1,0:T(8,128)(2,1)S(1)} %get-tuple-element.19), channel_id=1, source_target_pairs={{0,6},{1,3},{2,0},{3,5},{4,2},{5,7},{6,4},{7,1},{8,14},{9,11},{10,... | collective-permute-start | bytes 1572872 | tf_op jit(solution)/shard_map/ppermute | solution.py:347
  10.0 1.3 %collective-permute-start.3 = (bf16[64,16,256]{2,1,0:T(8,128)(2,1)S(1)}, bf16[64,16,256]{2,1,0:T(8,128)(2,1)S(1)}, u32[]{:S(2)}, u32[]{:S(2)}) collective-permute-start(bf16[64,16,256]{2,1,0:T(8,128)(2,1)S(1)} %get-tuple-element.20), channel_id=1, source_target_pairs={{0,96},{1,33},{32,0},{33,65},{64,32},{65,97},{96,64},{97,1},{2,98}... | collective-permute-start | bytes 1572872 | tf_op jit(solution)/shard_map/ppermute | solution.py:347
  11.3 1.6 %collective-permute-start.4 = (bf16[64,16,256]{2,1,0:T(8,128)(2,1)S(1)}, bf16[64,16,256]{2,1,0:T(8,128)(2,1)S(1)}, u32[]{:S(2)}, u32[]{:S(2)}) collective-permute-start(bf16[64,16,256]{2,1,0:T(8,128)(2,1)S(1)} %get-tuple-element.21), channel_id=1, source_target_pairs={{0,24},{1,9},{8,0},{9,17},{16,8},{17,25},{24,16},{25,1},{2,26},{3,... | collective-permute-start | bytes 1572872 | tf_op jit(solution)/shard_map/ppermute | solution.py:347
  13.0 7.1 %collective-permute-start.5 = (f32[12,4096]{1,0:T(8,128)S(1)}, f32[12,4096]{1,0:T(8,128)S(1)}, u32[]{:S(2)}, u32[]{:S(2)}) collective-permute-start(f32[12,4096]{1,0:T(8,128)S(1)} %pair.1), channel_id=1, source_target_pairs={{0,1},{1,0},{2,3},{3,2},{4,5},{5,4},{6,7},{7,6},{8,9},{9,8},{10,11... | collective-permute-start | bytes 589832 | tf_op jit(solution)/shard_map/ppermute | solution.py:342
  20.1 1.2 %collective-permute-done.5.pair_ref = f32[12,4096]{1,0:T(8,128)S(1)} collective-permute-done((f32[12,4096]{1,0:T(8,128)S(1)}, f32[12,4096]{1,0:T(8,128)S(1)}, u32[]{:S(2)}, u32[]{:S(2)}) %collective-permute-start.5) | collective-permute-done | bytes 196640 | tf_op jit(solution)/shard_map/ppermute | solution.py:342
  21.3 0.3 collective-permute-done.4.z_ref
  21.6 0.4 merge.1
  22.1 22.8 %all_to_all.10.parts_ref = bf16[64,16,384]{2,1,0:T(8,128)(2,1)S(1)} all-to-all(bf16[64,16,384]{2,1,0:T(8,128)(2,1)S(1)} %get-tuple-element.22), channel_id=1, replica_groups=mesh['y'=4,'z'=4,'x'=4,'core'=2] {'y','z','x'}, dimensions={0} | all-to-all | bytes 1572864 | tf_op jit(solution)/shard_map/all_to_all | solution.py:398
  44.8 0.8 adam.1
  45.6 16.9 %all_to_all.11.blocks_ref = bf16[64,16,384]{2,1,0:T(8,128)(2,1)S(1)} all-to-all(bf16[64,16,384]{2,1,0:T(8,128)(2,1)S(1)} %get-tuple-element.24), channel_id=1, replica_groups=mesh['y'=4,'z'=4,'x'=4,'core'=2] {'y','z','x'}, dimensions={0} | all-to-all | bytes 1572864 | tf_op jit(solution)/shard_map/all_to_all | solution.py:414
  62.6 0.3 collective-permute-start.9
  62.9 7.0 %collective-permute-start.6 = (bf16[64,16,384]{2,1,0:T(8,128)(2,1)S(1)}, bf16[64,16,384]{2,1,0:T(8,128)(2,1)S(1)}, u32[]{:S(2)}, u32[]{:S(2)}) collective-permute-start(bf16[64,16,384]{2,1,0:T(8,128)(2,1)S(1)} %all_to_all.11.blocks_ref), channel_id=1, source_target_pairs={{0,1},{1,0},{2,3},{3,2},{4,5},{5,4},{6,7},{7,6},{8,9},{9,8},{10,11... | collective-permute-start | bytes 2359304 | tf_op jit(solution)/shard_map/ppermute | solution.py:342
  69.9 2.1 %collective-permute-done.11.z_ref = bf16[64,16,256]{2,1,0:T(8,128)(2,1)S(1)} collective-permute-done((bf16[64,16,256]{2,1,0:T(8,128)(2,1)S(1)}, bf16[64,16,256]{2,1,0:T(8,128)(2,1)S(1)}, u32[]{:S(2)}, u32[]{:S(2)}) %collective-permute-start.11) | collective-permute-done | bytes 524320 | tf_op jit(solution)/shard_map/ppermute | solution.py:347
  72.0 4.5 %collective-permute-start.12 = (bf16[64,16,256]{2,1,0:T(8,128)(2,1)S(1)}, bf16[64,16,256]{2,1,0:T(8,128)(2,1)S(1)}, u32[]{:S(2)}, u32[]{:S(2)}) collective-permute-start(bf16[64,16,256]{2,1,0:T(8,128)(2,1)S(1)} %collective-permute-done.11.z_ref), channel_id=1, source_target_pairs={{0,1},{1,0},{2,3},{3,2},{4,5},{5,4},{6,7},{7,6},{8,9},{9,8},{10,11... | collective-permute-start | bytes 1572872 | tf_op jit(solution)/shard_map/ppermute | solution.py:342
  76.5 0.4 collective-permute-start.10
  76.9 1.1 %collective-permute-start.8 = (bf16[64,16,256]{2,1,0:T(8,128)(2,1)S(1)}, bf16[64,16,256]{2,1,0:T(8,128)(2,1)S(1)}, u32[]{:S(2)}, u32[]{:S(2)}) collective-permute-start(bf16[64,16,256]{2,1,0:T(8,128)(2,1)S(1)} %collective-permute-done.7.x_ref), channel_id=1, source_target_pairs={{0,1},{1,0},{2,3},{3,2},{4,5},{5,4},{6,7},{7,6},{8,9},{9,8},{10,11... | collective-permute-start | bytes 1572872 | tf_op jit(solution)/shard_map/ppermute | solution.py:342
  78.0 1.4 %place_own.1 = (bf16[256,8192]{1,0:T(8,128)(2,1)}, f32[3,2,4096]{2,1,0:T(2,128)S(1)}) custom-call(bf16[64,16,384]{2,1,0:T(8,128)(2,1)S(1)} %all_to_all.11.blocks_ref, bf16[64,16,256]{2,1,0:T(8,128)(2,1)S(1)} %collective-permute-done.7.x_ref, bf16[64,16,256]{2,1,0:T(8,128)(2,1)S(1)} %collective-permute-done.9.y_ref, ...), custom_call_target="tpu_custom_call" | custom-call | flops 8000000 | bytes 8000000 | tf_op jit(solution)/shard_map/place_own/pallas_call | solution.py:426
  79.4 0.3 collective-permute-done.13.refs_8_
  79.7 1.6 %place_other.1 = (bf16[256,8192]{1,0:T(8,128)(2,1)}, f32[3,2,8192]{2,1,0:T(2,128)}, f32[3,2,8192]{2,1,0:T(2,128)}) custom-call(bf16[64,16,384]{2,1,0:T(8,128)(2,1)S(1)} %collective-permute-done.6.refs_0_, bf16[64,16,256]{2,1,0:T(8,128)(2,1)S(1)} %collective-permute-done.8.refs_1_, ...), custom_call_target="tpu_custom_call", output_to_operand_aliasing={{0}: (5, {})} | custom-call | tf_op jit(solution)/shard_map/place_other/pallas_call | solution.py:436
  (25 shorter events, 0.2 us)
Async XLA Ops:
  0.6 3.5 %copy-start.2 = (f32[2,8192]{1,0:T(2,128)S(1)}, f32[2,8192]{1,0:T(2,128)}, u32[]{:S(2)}) copy-start(f32[2,8192]{1,0:T(2,128)} %first_ref.5) | copy-start | bytes 196612
  0.6 3.5 %copy-start.1 = (f32[2,8192]{1,0:T(2,128)S(1)}, f32[2,8192]{1,0:T(2,128)}, u32[]{:S(2)}) copy-start(f32[2,8192]{1,0:T(2,128)} %master_ref.5) | copy-start | bytes 196612
  0.7 7.3 %copy-start = (bf16[1,1,256,8192]{3,2,1,0:T(8,128)(2,1)S(1)}, bf16[1,1,256,8192]{3,2,1,0:T(8,128)(2,1)}, u32[]{:S(2)}) copy-start(bf16[1,1,256,8192]{3,2,1,0:T(8,128)(2,1)} %param.5) | copy-start | bytes 12582916
  2.6 10.3 %copy-start.3 = (f32[2,8192]{1,0:T(2,128)S(1)}, f32[2,8192]{1,0:T(2,128)}, u32[]{:S(2)}) copy-start(f32[2,8192]{1,0:T(2,128)} %second_ref.3) | copy-start | bytes 196612
  2.6 5.3 %collective-permute-start = (bf16[256,4096]{1,0:T(8,128)(2,1)S(1)}, bf16[256,4096]{1,0:T(8,128)(2,1)S(1)}, u32[]{:S(2)}, u32[]{:S(2)}) collective-permute-start(bf16[256,4096]{1,0:T(8,128)(2,1)S(1)} %dynamic-slice_bitcast_fusion), channel_id=1, source_target_pairs={{0,1},{1,0},{2,3},{3,2},{4,5},{5,4},{6,7},{7,6},{8,9},{9,8},{10,11... | collective-permute-start | bytes 6291464 | tf_op jit(solution)/shard_map/ppermute | solution.py:342
  4.2 0.7 collective-permute-start.1
  7.9 36.9 %copy-start.4 = (s32[64]{0:T(128)S(1)}, s32[64]{0:T(128)}, u32[]{:S(2)}) copy-start(s32[64]{0:T(128)} %param.9) | copy-start | bytes 772
  8.7 12.6 %collective-permute-start.2 = (bf16[64,16,256]{2,1,0:T(8,128)(2,1)S(1)}, bf16[64,16,256]{2,1,0:T(8,128)(2,1)S(1)}, u32[]{:S(2)}, u32[]{:S(2)}) collective-permute-start(bf16[64,16,256]{2,1,0:T(8,128)(2,1)S(1)} %get-tuple-element.19), channel_id=1, source_target_pairs={{0,6},{1,3},{2,0},{3,5},{4,2},{5,7},{6,4},{7,1},{8,14},{9,11},{10,... | collective-permute-start | bytes 1572872 | tf_op jit(solution)/shard_map/ppermute | solution.py:347
  10.0 11.3 %collective-permute-start.3 = (bf16[64,16,256]{2,1,0:T(8,128)(2,1)S(1)}, bf16[64,16,256]{2,1,0:T(8,128)(2,1)S(1)}, u32[]{:S(2)}, u32[]{:S(2)}) collective-permute-start(bf16[64,16,256]{2,1,0:T(8,128)(2,1)S(1)} %get-tuple-element.20), channel_id=1, source_target_pairs={{0,96},{1,33},{32,0},{33,65},{64,32},{65,97},{96,64},{97,1},{2,98}... | collective-permute-start | bytes 1572872 | tf_op jit(solution)/shard_map/ppermute | solution.py:347
  11.3 10.3 %collective-permute-start.4 = (bf16[64,16,256]{2,1,0:T(8,128)(2,1)S(1)}, bf16[64,16,256]{2,1,0:T(8,128)(2,1)S(1)}, u32[]{:S(2)}, u32[]{:S(2)}) collective-permute-start(bf16[64,16,256]{2,1,0:T(8,128)(2,1)S(1)} %get-tuple-element.21), channel_id=1, source_target_pairs={{0,24},{1,9},{8,0},{9,17},{16,8},{17,25},{24,16},{25,1},{2,26},{3,... | collective-permute-start | bytes 1572872 | tf_op jit(solution)/shard_map/ppermute | solution.py:347
  13.0 8.3 %collective-permute-start.5 = (f32[12,4096]{1,0:T(8,128)S(1)}, f32[12,4096]{1,0:T(8,128)S(1)}, u32[]{:S(2)}, u32[]{:S(2)}) collective-permute-start(f32[12,4096]{1,0:T(8,128)S(1)} %pair.1), channel_id=1, source_target_pairs={{0,1},{1,0},{2,3},{3,2},{4,5},{5,4},{6,7},{7,6},{8,9},{9,8},{10,11... | collective-permute-start | bytes 589832 | tf_op jit(solution)/shard_map/ppermute | solution.py:342
  62.5 9.4 %collective-permute-start.11 = (bf16[64,16,256]{2,1,0:T(8,128)(2,1)S(1)}, bf16[64,16,256]{2,1,0:T(8,128)(2,1)S(1)}, u32[]{:S(2)}, u32[]{:S(2)}) collective-permute-start(bf16[64,16,256]{2,1,0:T(8,128)(2,1)S(1)} %mine.1), channel_id=1, source_target_pairs={{0,24},{1,9},{8,0},{9,17},{16,8},{17,25},{24,16},{25,1},{2,26},{3,... | collective-permute-start | bytes 1572872 | tf_op jit(solution)/shard_map/ppermute | solution.py:347
  62.6 13.9 %collective-permute-start.9 = (bf16[64,16,256]{2,1,0:T(8,128)(2,1)S(1)}, bf16[64,16,256]{2,1,0:T(8,128)(2,1)S(1)}, u32[]{:S(2)}, u32[]{:S(2)}) collective-permute-start(bf16[64,16,256]{2,1,0:T(8,128)(2,1)S(1)} %mine.1), channel_id=1, source_target_pairs={{0,96},{1,33},{32,0},{33,65},{64,32},{65,97},{96,64},{97,1},{2,98}... | collective-permute-start | bytes 1572872 | tf_op jit(solution)/shard_map/ppermute | solution.py:347
  62.9 14.0 %collective-permute-start.7 = (bf16[64,16,256]{2,1,0:T(8,128)(2,1)S(1)}, bf16[64,16,256]{2,1,0:T(8,128)(2,1)S(1)}, u32[]{:S(2)}, u32[]{:S(2)}) collective-permute-start(bf16[64,16,256]{2,1,0:T(8,128)(2,1)S(1)} %mine.1), channel_id=1, source_target_pairs={{0,6},{1,3},{2,0},{3,5},{4,2},{5,7},{6,4},{7,1},{8,14},{9,11},{10,... | collective-permute-start | bytes 1572872 | tf_op jit(solution)/shard_map/ppermute | solution.py:347
  62.9 16.8 %collective-permute-start.6 = (bf16[64,16,384]{2,1,0:T(8,128)(2,1)S(1)}, bf16[64,16,384]{2,1,0:T(8,128)(2,1)S(1)}, u32[]{:S(2)}, u32[]{:S(2)}) collective-permute-start(bf16[64,16,384]{2,1,0:T(8,128)(2,1)S(1)} %all_to_all.11.blocks_ref), channel_id=1, source_target_pairs={{0,1},{1,0},{2,3},{3,2},{4,5},{5,4},{6,7},{7,6},{8,9},{9,8},{10,11... | collective-permute-start | bytes 2359304 | tf_op jit(solution)/shard_map/ppermute | solution.py:342
  72.0 7.8 %collective-permute-start.12 = (bf16[64,16,256]{2,1,0:T(8,128)(2,1)S(1)}, bf16[64,16,256]{2,1,0:T(8,128)(2,1)S(1)}, u32[]{:S(2)}, u32[]{:S(2)}) collective-permute-start(bf16[64,16,256]{2,1,0:T(8,128)(2,1)S(1)} %collective-permute-done.11.z_ref), channel_id=1, source_target_pairs={{0,1},{1,0},{2,3},{3,2},{4,5},{5,4},{6,7},{7,6},{8,9},{9,8},{10,11... | collective-permute-start | bytes 1572872 | tf_op jit(solution)/shard_map/ppermute | solution.py:342
  76.5 3.3 %collective-permute-start.10 = (bf16[64,16,256]{2,1,0:T(8,128)(2,1)S(1)}, bf16[64,16,256]{2,1,0:T(8,128)(2,1)S(1)}, u32[]{:S(2)}, u32[]{:S(2)}) collective-permute-start(bf16[64,16,256]{2,1,0:T(8,128)(2,1)S(1)} %collective-permute-done.9.y_ref), channel_id=1, source_target_pairs={{0,1},{1,0},{2,3},{3,2},{4,5},{5,4},{6,7},{7,6},{8,9},{9,8},{10,11... | collective-permute-start | bytes 1572872 | tf_op jit(solution)/shard_map/ppermute | solution.py:342
  76.9 2.9 %collective-permute-start.8 = (bf16[64,16,256]{2,1,0:T(8,128)(2,1)S(1)}, bf16[64,16,256]{2,1,0:T(8,128)(2,1)S(1)}, u32[]{:S(2)}, u32[]{:S(2)}) collective-permute-start(bf16[64,16,256]{2,1,0:T(8,128)(2,1)S(1)} %collective-permute-done.7.x_ref), channel_id=1, source_target_pairs={{0,1},{1,0},{2,3},{3,2},{4,5},{5,4},{6,7},{7,6},{8,9},{9,8},{10,11... | collective-permute-start | bytes 1572872 | tf_op jit(solution)/shard_map/ppermute | solution.py:342
  78.0 1.7 %collective-permute-start.13 = (f32[8,4096]{1,0:T(8,128)S(1)}, f32[8,4096]{1,0:T(8,128)S(1)}, u32[]{:S(2)}, u32[]{:S(2)}) collective-permute-start(f32[8,4096]{1,0:T(8,128)S(1)} %get-tuple-element.29), channel_id=1, source_target_pairs={{0,1},{1,0},{2,3},{3,2},{4,5},{5,4},{6,7},{7,6},{8,9},{9,8},{10,11... | collective-permute-start | bytes 393224 | tf_op jit(solution)/shard_map/ppermute | solution.py:342
